TPU v7x, 32 devices: a whole 2x2x4 slice. The times are simulated.
32 devices in a mesh: dp: 8 (over y, x, core), tensor: 4 (over z).
Axes of the slice: x: 2, y: 2, z: 4, core: 2. Of those that a mesh axis runs over, the one named last changes fastest.
Arguments:
- resid_in: float32 [8192, 1536], P(('dp', 'tensor')), may hold values from -6 to 6
- in_weight: bfloat16 [2, 1536, 2, 3072], P(None, 'dp', None, 'tensor'), may hold values from -0.15625 to 0.15625
- out_weight: bfloat16 [2, 1536, 3072], P(None, 'dp', 'tensor'), may hold values from -0.109375 to 0.109375
- shared_weight: bfloat16 [2, 1536, 304], replicated, may hold values from -0.15625 to 0.15625
- small_params: float32 [2, 21392], replicated, may hold values from -12 to 3.5
- in_momentum: float32 [2, 1536, 2, 3072], P(None, 'dp', None, 'tensor'), may hold values from -256 to 256
- out_momentum: float32 [2, 1536, 3072], P(None, 'dp', 'tensor'), may hold values from -256 to 256
- shared_momentum: float32 [2, 1536, 304], replicated, may hold values from -256 to 256
- small_first: float32 [2, 21392], replicated, may hold values from -119.48181 to 119.48181
- small_second: float32 [2, 21392], replicated, may hold values from 38.78093 to 15512.371
- resid_grad: float32 [8192, 1536], P(('dp', 'tensor')), may hold values from -6 to 6
Outputs:
- resid_out: float32 [8192, 1536], P(('dp', 'tensor'))
- input_grad: float32 [8192, 1536], P(('dp', 'tensor'))
- small_grad: float32 [2, 21392], replicated
- small_second_new: float32 [2, 21392], replicated
- small_new: float32 [2, 21392], replicated
- in_momentum_new: float32 [2, 1536, 2, 3072], P(None, 'dp', None, 'tensor')
- in_weight_new: float32 [2, 1536, 2, 3072], P(None, 'dp', None, 'tensor')
- out_momentum_new: float32 [2, 1536, 3072], P(None, 'dp', 'tensor')
- out_weight_new: float32 [2, 1536, 3072], P(None, 'dp', 'tensor')
- shared_momentum_new: float32 [2, 1536, 304], replicated
- shared_weight_new: float32 [2, 1536, 304], replicated
All inputs are finite; a program needn't handle non-finite values.
Results may differ from a plain program's by a relative error of at most 0.013.
Values may be sent and summed in bfloat16 or wider, within the bound.
A program may use at most 256 MiB of HBM per device.

v0:
```python
import jax
import jax.numpy as jnp
from jax import lax
from jax.sharding import PartitionSpec as P

D = 1536
INNER = 3072
HEADS = 48
STATE = 128
KERNEL = 4
SPAN = 256
LAYERS = 2
STEP = 10
SSM_COLS = 304


epsilon = 1e-05
highest = lax.Precision.HIGHEST
coef_first = 3.4445
coef_second = -4.775
coef_third = 2.0315
muon_decay = 0.95
muon_rate = 0.2
beta_first = 0.9
beta_second = 0.95
adam_rate = 0.2


def unpack(vector):
    amounts = (KERNEL * INNER, INNER, INNER, KERNEL * 2 * STATE, 2 * STATE, HEADS, HEADS, HEADS, D)
    pieces = []
    offset = 0
    for amount in amounts:
        pieces.append(vector[offset : offset + amount])
        offset = offset + amount
    return (
        pieces[0].reshape(KERNEL, INNER),
        pieces[1],
        pieces[2],
        pieces[3].reshape(KERNEL, 2 * STATE),
        pieces[4],
        pieces[5],
        pieces[6],
        pieces[7],
        pieces[8],
    )


def causal_conv(values, weights, biases):
    length = values.shape[0]
    padded = jnp.concatenate([jnp.zeros((KERNEL - 1, values.shape[1]), jnp.float32), values], 0)
    result = jnp.zeros_like(values) + biases[None, :]
    for offset in range(KERNEL):
        result = result + weights[offset][None, :] * padded[offset : offset + length]
    return result


def span_step(carry_state, pieces):
    values, inputs, readout, log_decay, timestep = pieces
    length = values.shape[0]
    cumulative = jnp.cumsum(log_decay, axis=0).T
    step_heads = timestep.T
    head_values = jnp.transpose(values, (1, 0, 2))
    row_index = lax.broadcasted_iota(jnp.int32, (length, length), 0)
    col_index = lax.broadcasted_iota(jnp.int32, (length, length), 1)
    causal = (row_index >= col_index)[None, :, :]
    spread = jnp.where(causal, cumulative[:, :, None] - cumulative[:, None, :], 0.0)
    decay_mask = jnp.where(causal, jnp.exp(spread), 0.0)
    scores = jnp.dot(readout, inputs.T, precision=highest)
    mixing = scores[None, :, :] * decay_mask * step_heads[:, None, :]
    inside = jnp.einsum("hts,hsp->htp", mixing, head_values, precision=highest)
    carried = (
        jnp.einsum("tn,hnp->htp", readout, carry_state, precision=highest)
        * jnp.exp(cumulative)[:, :, None]
    )
    tail_weight = jnp.exp(cumulative[:, -1:] - cumulative) * step_heads
    fresh_state = jnp.einsum(
        "sn,hsp->hnp", inputs, tail_weight[:, :, None] * head_values, precision=highest
    )
    new_state = jnp.exp(cumulative[:, -1])[:, None, None] * carry_state + fresh_state
    return (new_state, jnp.transpose(inside + carried, (1, 0, 2)))


def mixer_core(
    gate_in, x_in, bc_in, dt_raw, conv_x_w, conv_x_b, conv_s_w, conv_s_b, a_log, dt_bias, skip
):
    length = x_in.shape[0]
    head_count = a_log.shape[0]
    head_width = x_in.shape[1] // head_count
    x_conv = jax.nn.silu(causal_conv(x_in, conv_x_w, conv_x_b))
    bc_conv = jax.nn.silu(causal_conv(bc_in, conv_s_w, conv_s_b))
    timestep = jax.nn.softplus(dt_raw + dt_bias[None, :])
    log_decay = -timestep * jnp.exp(a_log)[None, :]
    values = x_conv.reshape(length, head_count, head_width)
    blocks = length // SPAN
    pieces = (
        values.reshape(blocks, SPAN, head_count, head_width),
        bc_conv[:, :STATE].reshape(blocks, SPAN, STATE),
        bc_conv[:, STATE:].reshape(blocks, SPAN, STATE),
        log_decay.reshape(blocks, SPAN, head_count),
        timestep.reshape(blocks, SPAN, head_count),
    )
    initial = jnp.zeros((head_count, STATE, head_width), jnp.float32)
    last_state, outputs = lax.scan(jax.checkpoint(span_step), initial, pieces)
    result = outputs.reshape(length, head_count, head_width) + skip[None, :, None] * values
    return result.reshape(length, head_count * head_width) * jax.nn.silu(gate_in)


def orthogonal(matrix):
    current = matrix / (jnp.sqrt(jnp.sum(matrix * matrix)) + 1e-07)
    for iteration in range(5):
        gram = jnp.dot(current, current.T, precision=highest)
        poly = coef_second * gram + coef_third * jnp.dot(gram, gram, precision=highest)
        current = coef_first * current + jnp.dot(poly, current, precision=highest)
    return current


def place(part, start, total, axis_number):
    shape = list(part.shape)
    shape[axis_number] = total
    return lax.dynamic_update_slice_in_dim(jnp.zeros(shape, jnp.float32), part, start, axis_number)


def body(
    resid_in,
    in_weight,
    out_weight,
    shared_weight,
    small_params,
    in_momentum,
    out_momentum,
    shared_momentum,
    small_first,
    small_second,
    resid_grad,
):
    tensor_index = lax.axis_index("tensor")
    tensor_count = lax.axis_size("tensor")
    local_cols = in_weight.shape[3]
    local_heads = HEADS // tensor_count
    col_start = tensor_index * local_cols
    head_start = tensor_index * local_heads
    shard_rows = in_weight.shape[1]

    def fetch(layer_number):
        return (
            lax.all_gather(in_weight[layer_number], "dp", axis=0, tiled=True),
            lax.all_gather(out_weight[layer_number], "dp", axis=0, tiled=True),
        )

    def local_params(small):
        conv_x_w, conv_x_b, norm_gain, conv_s_w, conv_s_b, a_log, dt_bias, skip, in_gain = unpack(
            small
        )
        return (
            lax.dynamic_slice_in_dim(conv_x_w, col_start, local_cols, 1),
            lax.dynamic_slice_in_dim(conv_x_b, col_start, local_cols, 0),
            lax.dynamic_slice_in_dim(norm_gain, col_start, local_cols, 0),
            conv_s_w,
            conv_s_b,
            lax.dynamic_slice_in_dim(a_log, head_start, local_heads, 0),
            lax.dynamic_slice_in_dim(dt_bias, head_start, local_heads, 0),
            lax.dynamic_slice_in_dim(skip, head_start, local_heads, 0),
            in_gain,
        )

    residual = resid_in
    saved = []
    for layer_number in range(LAYERS):
        w_in, w_out = fetch(layer_number)
        w_shared = shared_weight[layer_number]
        conv_x_w, conv_x_b, gain_local, conv_s_w, conv_s_b, a_log, dt_bias, skip, in_gain = (
            local_params(small_params[layer_number])
        )
        inverse_in = lax.rsqrt(jnp.mean(residual * residual, -1, keepdims=True) + epsilon)
        normed_low = (residual * inverse_in * in_gain).astype(jnp.bfloat16)
        gathered = lax.all_gather(normed_low, "tensor", axis=0, tiled=True)
        gate_x = lax.dot_general(
            gathered, w_in, (((1,), (0,)), ((), ())), preferred_element_type=jnp.float32
        )
        shared = jnp.dot(gathered, w_shared, preferred_element_type=jnp.float32)
        dt_local = lax.dynamic_slice_in_dim(shared, 2 * STATE + head_start, local_heads, 1)
        mixer_out, pullback = jax.vjp(
            mixer_core,
            gate_x[:, 0],
            gate_x[:, 1],
            shared[:, : 2 * STATE],
            dt_local,
            conv_x_w,
            conv_x_b,
            conv_s_w,
            conv_s_b,
            a_log,
            dt_bias,
            skip,
        )
        squares = lax.psum(jnp.sum(mixer_out * mixer_out, -1), "tensor")
        inverse_gate = lax.rsqrt(squares / INNER + epsilon)
        normalized = mixer_out * inverse_gate[:, None]
        scaled_low = (normalized * gain_local).astype(jnp.bfloat16)
        branch = lax.psum_scatter(
            lax.dot_general(
                scaled_low, w_out, (((1,), (1,)), ((), ())), preferred_element_type=jnp.float32
            ),
            "tensor",
            scatter_dimension=0,
            tiled=True,
        )
        kept = None
        saved.append(
            (residual, inverse_in, gathered, normalized, inverse_gate, scaled_low, pullback, kept)
        )
        residual = residual + branch
    grad_resid = resid_grad
    in_grads = [None] * LAYERS
    out_grads = [None] * LAYERS
    shared_grads = [None] * LAYERS
    small_grads = [None] * LAYERS
    for layer_number in reversed(range(LAYERS)):
        layer_in, inverse_in, gathered, normalized, inverse_gate, scaled_low, pullback, kept = (
            saved[layer_number]
        )
        w_in, w_out = fetch(layer_number)
        w_shared = shared_weight[layer_number]
        conv_x_w, conv_x_b, gain_local, conv_s_w, conv_s_b, a_log, dt_bias, skip, in_gain = (
            local_params(small_params[layer_number])
        )
        d_branch = grad_resid.astype(jnp.bfloat16)
        d_rows = lax.all_gather(d_branch, "tensor", axis=0, tiled=True)
        out_grads[layer_number] = lax.dot_general(
            d_rows, scaled_low, (((0,), (0,)), ((), ())), preferred_element_type=jnp.float32
        )
        d_scaled = jnp.dot(d_rows, w_out, preferred_element_type=jnp.float32)
        d_norm_gain = jnp.sum(d_scaled * normalized, 0)
        d_normalized = d_scaled * gain_local
        dots = lax.psum(jnp.sum(d_normalized * normalized, -1), "tensor")
        d_mixer = inverse_gate[:, None] * (d_normalized - normalized * (dots / INNER)[:, None])
        (
            d_gate,
            d_xin,
            d_bc,
            d_dt,
            d_conv_x_w,
            d_conv_x_b,
            d_conv_s_w,
            d_conv_s_b,
            d_a_log,
            d_dt_bias,
            d_skip,
        ) = pullback(d_mixer)
        d_gate_x_low = jnp.stack([d_gate, d_xin], 1).astype(jnp.bfloat16)
        d_shared_low = jnp.concatenate([d_bc, place(d_dt, head_start, HEADS, 1)], 1).astype(
            jnp.bfloat16
        )
        in_grads[layer_number] = lax.dot_general(
            gathered, d_gate_x_low, (((0,), (0,)), ((), ())), preferred_element_type=jnp.float32
        )
        shared_grads[layer_number] = lax.dot_general(
            gathered, d_shared_low, (((0,), (0,)), ((), ())), preferred_element_type=jnp.float32
        )
        from_gate = lax.dot_general(
            d_gate_x_low, w_in, (((1, 2), (1, 2)), ((), ())), preferred_element_type=jnp.float32
        )
        from_shared = lax.dot_general(
            d_shared_low, w_shared, (((1,), (1,)), ((), ())), preferred_element_type=jnp.float32
        )
        d_normed = lax.psum_scatter(
            from_gate + from_shared, "tensor", scatter_dimension=0, tiled=True
        )
        scaled_in = layer_in * inverse_in
        d_in_gain = jnp.sum(d_normed * scaled_in, 0)
        d_scaled_in = d_normed * in_gain
        grad_resid = grad_resid + inverse_in * (
            d_scaled_in - scaled_in * jnp.mean(d_scaled_in * scaled_in, -1, keepdims=True)
        )
        small_grads[layer_number] = jnp.concatenate(
            [
                place(d_conv_x_w, col_start, INNER, 1).reshape(KERNEL * INNER),
                place(d_conv_x_b, col_start, INNER, 0),
                place(d_norm_gain, col_start, INNER, 0),
                d_conv_s_w.reshape(KERNEL * 2 * STATE),
                d_conv_s_b,
                place(d_a_log, head_start, HEADS, 0),
                place(d_dt_bias, head_start, HEADS, 0),
                place(d_skip, head_start, HEADS, 0),
                d_in_gain,
            ]
        )
    in_grad_shard, out_grad_shard = (
        lax.psum_scatter(
            jnp.stack(in_grads).astype(jnp.bfloat16), "dp", scatter_dimension=1, tiled=True
        ).astype(jnp.float32),
        lax.psum_scatter(
            jnp.stack(out_grads).astype(jnp.bfloat16), "dp", scatter_dimension=1, tiled=True
        ).astype(jnp.float32),
    )
    shared_total, small_grad = lax.psum(
        (jnp.stack(shared_grads), jnp.stack(small_grads)), ("dp", "tensor")
    )
    in_momentum_new = muon_decay * in_momentum + in_grad_shard
    out_momentum_new = muon_decay * out_momentum + out_grad_shard
    block_count = 3 * LAYERS
    stacked = jnp.concatenate(
        [jnp.transpose(in_momentum_new, (0, 2, 1, 3)), out_momentum_new[:, None]], 1
    )
    stacked = stacked.reshape(block_count, shard_rows, local_cols)
    dp_count = lax.axis_size("dp")
    slots = jnp.concatenate(
        [stacked, jnp.zeros((dp_count - block_count, shard_rows, local_cols), jnp.float32)], 0
    )
    whole = lax.all_to_all(
        slots.astype(jnp.bfloat16), "dp", split_axis=0, concat_axis=1, tiled=True
    ).astype(slots.dtype)[0]
    turned = orthogonal(whole.T).T
    returned = lax.all_to_all(
        turned[None].astype(jnp.bfloat16), "dp", split_axis=1, concat_axis=0, tiled=True
    ).astype(jnp.float32)[:block_count]
    returned = returned * (D / local_cols) ** 0.5
    updates = returned.reshape(LAYERS, 3, shard_rows, local_cols)
    in_weight_new = in_weight.astype(jnp.float32) - muon_rate * jnp.transpose(
        updates[:, :2], (0, 2, 1, 3)
    )
    out_weight_new = out_weight.astype(jnp.float32) - muon_rate * updates[:, 2]
    shared_momentum_new = muon_decay * shared_momentum + shared_total
    shared_updates = []
    for layer_number in range(LAYERS):
        shared_updates.append(orthogonal(shared_momentum_new[layer_number].T).T)
    shared_turned = jnp.stack(shared_updates)
    shared_weight_new = shared_weight.astype(jnp.float32) - muon_rate * (
        shared_turned * (D / SSM_COLS) ** 0.5
    )
    first_new = beta_first * small_first + (1.0 - beta_first) * small_grad
    small_second_new = beta_second * small_second + (1.0 - beta_second) * small_grad * small_grad
    small_new = small_params - adam_rate * (first_new / (1.0 - beta_first**STEP)) / (
        jnp.sqrt(small_second_new / (1.0 - beta_second**STEP)) + 1e-08
    )
    return (
        residual,
        grad_resid,
        small_grad,
        small_second_new,
        small_new,
        in_momentum_new,
        in_weight_new,
        out_momentum_new,
        out_weight_new,
        shared_momentum_new,
        shared_weight_new,
    )


def solution(mesh):
    placed = (
        P(("dp", "tensor"), None),
        P(None, "dp", None, "tensor"),
        P(None, "dp", "tensor"),
        P(),
        P(),
        P(None, "dp", None, "tensor"),
        P(None, "dp", "tensor"),
        P(),
        P(),
        P(),
        P(("dp", "tensor"), None),
    )
    return jax.shard_map(
        body,
        mesh=mesh,
        in_specs=placed,
        out_specs=(
            P(("dp", "tensor"), None),
            P(("dp", "tensor"), None),
            P(),
            P(),
            P(),
            P(None, "dp", None, "tensor"),
            P(None, "dp", None, "tensor"),
            P(None, "dp", "tensor"),
            P(None, "dp", "tensor"),
            P(),
            P(),
        ),
        check_vma=False,
    )
```

profile of v0, /device:TPU:0, one launch (start us, length us, event | category | flops | bytes accessed | tf_op | source)
XLA Modules:
  0.0 2377.1 jit_solution(15821681495674615435)
XLA Ops:
  22.5 56.1 %all-gather.13.cloned.1.call-done = bf16[1024,1536]{1,0:T(8,128)(2,1)} async-done(((bf16[256,1536]{1,0:T(8,128)(2,1)}), bf16[1024,1536]{1,0:T(8,128)(2,1)}) %all-gather.13.cloned.1.call-update) | async-done | bytes 3145744 | tf_op jit(solution)/shard_map/all_gather | solution.py:177
  87.9 30.9 %all-gather.21.cloned.1.call-done = bf16[1,1536,2,768]{3,1,2,0:T(8,128)(2,1)} async-done(((bf16[1,192,2,768]{3,1,2,0:T(8,128)(2,1)}), bf16[1,1536,2,768]{3,1,2,0:T(8,128)(2,1)}) %all-gather.21.cloned.1.call-update) | async-done | bytes 4718608 | tf_op jit(solution)/shard_map/all_gather | solution.py:147
  146.5 122.4 %while.88 = (s32[]{:T(128)}, f32[12,128,64]{1,2,0:T(8,128)S(1)}, f32[4,256,12,64]{1,0,3,2:T(4,128)}, f32[4,12,128,64]{2,3,1,0:T(8,128)}, f32[4,256,12]{1,2,0:T(8...) while((s32[]{:T(128)}, f32[12,128,64]{1,2,0:T(8,128)S(1)}, ...), condition=%wide.region_4.6_spmd.clone.clone, body=%wide.region_1.5_spmd.clone.clone.sunk | while | flops 1313839104 | bytes 10908259 | solution.py:104
  157.3 17.9 dynamic_update_slice.227
  187.9 17.9 dynamic_update_slice.227
  218.5 17.9 dynamic_update_slice.227
  249.1 17.9 dynamic_update_slice.227
  304.0 106.1 %reduce-scatter.7.cloned.1.call-done = f32[256,1536]{1,0:T(8,128)} async-done(((f32[1024,1536]{1,0:T(8,128)}), f32[256,1536]{1,0:T(8,128)}) %reduce-scatter.7.cloned.1.call-update) | async-done | bytes 1572880 | tf_op jit(solution)/shard_map/reduce_scatter | solution.py:201
  418.3 33.6 %all-gather.25.cloned.1.call-done = bf16[1,1536,2,768]{3,1,2,0:T(8,128)(2,1)} async-done(((bf16[1,192,2,768]{3,1,2,0:T(8,128)(2,1)}), bf16[1,1536,2,768]{3,1,2,0:T(8,128)(2,1)}) %all-gather.25.cloned.1.call-update) | async-done | bytes 4718608 | tf_op jit(solution)/shard_map/all_gather | solution.py:147
  451.9 65.5 %all-gather.15.cloned.1.call-done = bf16[1024,1536]{1,0:T(8,128)(2,1)} async-done(((bf16[256,1536]{1,0:T(8,128)(2,1)}), bf16[1024,1536]{1,0:T(8,128)(2,1)}) %all-gather.15.cloned.1.call-update) | async-done | bytes 3145744 | tf_op jit(solution)/shard_map/all_gather | solution.py:177
  552.3 122.5 %while.89 = (s32[]{:T(128)}, f32[12,128,64]{1,2,0:T(8,128)S(1)}, f32[4,256,12,64]{1,0,3,2:T(4,128)}, f32[4,12,128,64]{2,3,1,0:T(8,128)}, f32[4,256,12]{1,2,0:T(8...) while((s32[]{:T(128)}, f32[12,128,64]{1,2,0:T(8,128)S(1)}, ...), condition=%wide.region_12.14_spmd.clone.clone, body=%wide.region_9.13_spmd.clone.clone.sunk | while | flops 1313839104 | bytes 10908259 | solution.py:104
  734.6 205.1 %while.86 = (s32[]{:T(128)}, f32[12,128,64]{1,2,0:T(8,128)S(1)}, f32[4,256,12,64]{1,0,3,2:T(4,128)}, f32[4,256,128]{2,1,0:T(8,128)}, f32[4,256,128]{2,1,0:T(8,12...) while((s32[]{:T(128)}, f32[12,128,64]{1,2,0:T(8,128)S(1)}, ...), condition=%wide.region_31.33_spmd.clone, body=%wide.region_18.32_spmd.clone.sunk | while | flops 3038771200 | bytes 29374988 | solution.py:104
  999.3 101.0 %reduce-scatter.11.cloned.1.call-done = f32[256,1536]{1,0:T(8,128)} async-done(((f32[1024,1536]{1,0:T(8,128)}), f32[256,1536]{1,0:T(8,128)}) %reduce-scatter.11.cloned.1.call-update) | async-done | bytes 1572880 | tf_op jit(solution)/shard_map/reduce_scatter | solution.py:267
  1102.8 111.0 %reduce-scatter.9.cloned.1.call-done = f32[256,1536]{1,0:T(8,128)} async-done(((f32[1024,1536]{1,0:T(8,128)}), f32[256,1536]{1,0:T(8,128)}) %reduce-scatter.9.cloned.1.call-update) | async-done | bytes 1572880 | tf_op jit(solution)/shard_map/reduce_scatter | solution.py:201
  1218.2 64.1 %all-gather.19.cloned.1.call-done = bf16[1024,1536]{1,0:T(8,128)(2,1)} async-done(((bf16[256,1536]{1,0:T(8,128)(2,1)}), bf16[1024,1536]{1,0:T(8,128)(2,1)}) %all-gather.19.cloned.1.call-update) | async-done | bytes 3145744 | tf_op jit(solution)/shard_map/all_gather | solution.py:229
  1318.8 205.0 %while.87 = (s32[]{:T(128)}, f32[12,128,64]{1,2,0:T(8,128)S(1)}, f32[4,256,12,64]{1,0,3,2:T(4,128)}, f32[4,256,128]{2,1,0:T(8,128)}, f32[4,256,128]{2,1,0:T(8,12...) while((s32[]{:T(128)}, f32[12,128,64]{1,2,0:T(8,128)S(1)}, ...), condition=%wide.region_49.51_spmd.clone, body=%wide.region_36.50_spmd.clone.sunk | while | flops 3038771200 | bytes 29374988 | solution.py:104
  1350.1 17.9 dynamic_update_slice.223
  1503.5 17.9 dynamic_update_slice.223
  1628.2 56.5 %reduce-scatter.13.cloned.1.call-done = f32[256,1536]{1,0:T(8,128)} async-done(((f32[1024,1536]{1,0:T(8,128)}), f32[256,1536]{1,0:T(8,128)}) %reduce-scatter.13.cloned.1.call-update) | async-done | bytes 1572880 | tf_op jit(solution)/shard_map/reduce_scatter | solution.py:267
  1687.6 55.0 %reduce-scatter.17.cloned.1.call-done = bf16[2,192,768]{2,1,0:T(8,128)(2,1)} async-done(((bf16[2,1536,768]{2,1,0:T(8,128)(2,1)}), bf16[2,192,768]{2,1,0:T(8,128)(2,1)}) %reduce-scatter.17.cloned.1.call-update) | async-done | bytes 589840 | tf_op jit(solution)/shard_map/reduce_scatter | solution.py:293
  1747.1 75.8 %reduce-scatter.15.cloned.1.call-done = bf16[2,192,2,768]{3,1,2,0:T(8,128)(2,1)} async-done(((bf16[2,1536,2,768]{3,1,2,0:T(8,128)(2,1)}), bf16[2,192,2,768]{3,1,2,0:T(8,128)(2,1)}) %reduce-scatter.15.cloned.1.call-update) | async-done | bytes 1179664 | tf_op jit(solution)/shard_map/reduce_scatter | solution.py:290
  1834.9 145.4 %all-reduce.48.cloned.1.call-done = (f32[2,21392]{1,0:T(2,128)}, f32[2,1536,304]{1,2,0:T(8,128)}) async-done(((f32[2,21392]{1,0:T(2,128)}, f32[2,1536,304]{1,2,0:T(8,128)}), (f32[2,21392]{1,0:T(2,128)}, f32[2,1536,304]{1,2,0:T(8,128)})) %all-reduce.48.cloned.1.call-update) | async-done | bytes 3906704 | tf_op jit(solution)/shard_map/psum | solution.py:297
  2246.6 25.7 %fusion.216 = bf16[1,1536,768]{1,2,0:T(8,128)(2,1)} fusion(f32[768,1536]{1,0:T(8,128)} %fusion.233, f32[768,1536]{1,0:T(8,128)} %copy-done.22, f32[768,1536]{1,0:T(8,128)} %get-tuple-element.1656, f32[1536,768]{0,1:T(8,128)} %copy.367, f32[768,1536]{1,0:T(8,128)} %copy-done.21, f32[768,768]{1,0:T(8,128)} %fusion.407, f32[768,768]{1,0:T(8,128)} %copy-done.18, ...), kind=kOutput, calls=%fused_computation.346 | convolution fusion | flops 10889920512 | bytes 35389440 | tf_op jit(solution)/shard_map/dot_general | solution.py:114
  2284.9 25.7 %reduce.66 = bf16[1536,768]{1,0:T(8,128)(2,1)} reduce(bf16[1536,1,768]{2,1,0:T(2,128)(2,1)} %bitcast.1024, bf16[]{:T(256)} %broadcast.652), dimensions={1}, to_apply=%bitcast.658.reduce_sub_computation | reduce | bytes 4718594
  (1349 shorter events, 1294.5 us)
Async XLA Ops:
  7.2 71.5 %all-gather.13.cloned.1.call-start = ((), (), s32[]{:S(2)}) async-start(), calls=%async_computation.8 | async-start | bytes 3932160 | tf_op jit(solution)/shard_map/all_gather | solution.py:177
  8.2 403.6 %copy-start.99 = (f32[1536]{0:T(1024)}, f32[1536]{0:T(1024)S(1)}, u32[]{:S(2)}) copy-start(f32[1536]{0:T(1024)S(1)} %get-tuple-element.1414) | copy-start | bytes 18436
  12.3 106.4 %all-gather.21.cloned.1.call-start = ((), (), s32[]{:S(2)}) async-start(), calls=%async_computation.18 | async-start | bytes 5308416 | tf_op jit(solution)/shard_map/all_gather | solution.py:147
  14.9 279.1 %all-gather.23.cloned.1.call-start = ((), (), s32[]{:S(2)}) async-start(), calls=%async_computation.19 | async-start | bytes 2654208 | tf_op jit(solution)/shard_map/all_gather | solution.py:148
  16.9 393.2 %reduce-scatter.7.cloned.1.call-start = ((), (), s32[]{:S(2)}) async-start(), calls=%async_computation.9 | async-start | bytes 7864320 | tf_op jit(solution)/shard_map/reduce_scatter | solution.py:201
  21.2 255.7 %copy-start.101 = (f32[768]{0:T(1024)}, f32[768]{0:T(1024)S(1)}, u32[]{:S(2)}) copy-start(f32[768]{0:T(1024)S(1)} %mul.1733) | copy-start | bytes 9220
  302.0 149.9 %all-gather.25.cloned.1.call-start = ((), (), s32[]{:S(2)}) async-start(), calls=%async_computation.20 | async-start | bytes 5308416 | tf_op jit(solution)/shard_map/all_gather | solution.py:147
  303.9 213.5 %all-gather.15.cloned.1.call-start = ((), (), s32[]{:S(2)}) async-start(), calls=%async_computation.10 | async-start | bytes 3932160 | tf_op jit(solution)/shard_map/all_gather | solution.py:177
  414.0 283.3 %all-gather.27.cloned.1.call-start = ((), (), s32[]{:S(2)}) async-start(), calls=%async_computation.21 | async-start | bytes 2654208 | tf_op jit(solution)/shard_map/all_gather | solution.py:148
  414.8 282.6 %all-gather.17.cloned.1.call-start = ((), (), s32[]{:S(2)}) async-start(), calls=%async_computation.12 | async-start | bytes 3932160 | tf_op jit(solution)/shard_map/all_gather | solution.py:229
  415.8 684.5 %reduce-scatter.11.cloned.1.call-start = ((), (), s32[]{:S(2)}) async-start(), calls=%async_computation.13 | async-start | bytes 7864320 | tf_op jit(solution)/shard_map/reduce_scatter | solution.py:267
  416.7 299.0 %copy-start.104 = (f32[768]{0:T(1024)}, f32[768]{0:T(1024)S(1)}, u32[]{:S(2)}) copy-start(f32[768]{0:T(1024)S(1)} %mul.1781) | copy-start | bytes 9220
  417.4 298.3 %copy-start.147 = (f32[768]{0:T(1024)}, f32[768]{0:T(1024)S(1)}, u32[]{:S(2)}) copy-start(f32[768]{0:T(1024)S(1)} %fusion.331) | copy-start | bytes 9220
  991.0 222.8 %reduce-scatter.9.cloned.1.call-start = ((), (), s32[]{:S(2)}) async-start(), calls=%async_computation.11 | async-start | bytes 7864320 | tf_op jit(solution)/shard_map/reduce_scatter | solution.py:201
  999.2 214.6 %copy-start.51 = (f32[256,1536]{1,0:T(8,128)S(1)}, f32[256,1536]{1,0:T(8,128)}, u32[]{:S(2)}) copy-start(f32[256,1536]{1,0:T(8,128)} %param.30) | copy-start | bytes 4718596
  999.2 283.1 %all-gather.19.cloned.1.call-start = ((), (), s32[]{:S(2)}) async-start(), calls=%async_computation.14 | async-start | bytes 3932160 | tf_op jit(solution)/shard_map/all_gather | solution.py:229
  1102.8 179.5 %copy-start.137 = (f32[1024]{0:T(1024)S(1)}, f32[1024]{0:T(1024)}, u32[]{:S(2)}) copy-start(f32[1024]{0:T(1024)} %copy-done.136) | copy-start | bytes 12292
  1102.8 179.5 %copy-start.145 = (f32[768]{0:T(1024)S(1)}, f32[768]{0:T(1024)}, u32[]{:S(2)}) copy-start(f32[768]{0:T(1024)} %fusion.329) | copy-start | bytes 9220
  1218.1 466.7 %reduce-scatter.13.cloned.1.call-start = ((), (), s32[]{:S(2)}) async-start(), calls=%async_computation.15 | async-start | bytes 7864320 | tf_op jit(solution)/shard_map/reduce_scatter | solution.py:267
  1575.0 167.6 %reduce-scatter.17.cloned.1.call-start = ((), (), s32[]{:S(2)}) async-start(), calls=%async_computation.17 | async-start | bytes 5308416 | tf_op jit(solution)/shard_map/reduce_scatter | solution.py:293
  1587.4 235.5 %reduce-scatter.15.cloned.1.call-start = ((), (), s32[]{:S(2)}) async-start(), calls=%async_computation.16 | async-start | bytes 10616832 | tf_op jit(solution)/shard_map/reduce_scatter | solution.py:290
  1613.5 366.7 %all-reduce.48.cloned.1.call-start = ((), (), s32[]{:S(2)}) async-start(), calls=%async_computation.22 | async-start | bytes 7815168 | tf_op jit(solution)/shard_map/psum | solution.py:297
  1827.1 239.1 %all-to-all-start = ((bf16[8,192,768]{2,1,0:T(8,128)(2,1)}), bf16[8,192,768]{2,1,0:T(8,128)(2,1)}, u32[]{:S(2)}, u32[]{:S(2)}) async-start(bf16[8,192,768]{2,1,0:T(8,128)(2,1)} %concatenate.42), calls=%async_computation.6 | async-start | bytes 4718592 | tf_op jit(solution)/shard_map/all_to_all | solution.py:311
  2316.6 33.9 %all-to-all-start.1 = ((bf16[8,2,73728]{2,1,0:T(2,128)(2,1)}), bf16[8,2,73728]{2,1,0:T(2,128)(2,1)}, u32[]{:S(2)}, u32[]{:S(2)}) async-start(bf16[8,2,73728]{2,1,0:T(2,128)(2,1)} %reshape.998), calls=%async_computation.7 | async-start | bytes 4718592 | tf_op jit(solution)/shard_map/all_to_all | solution.py:315
  (231 other events, 3855.7 us)
Sparse Core Ops, SparseCore 0:
  12.4 66.1 all-gather.12
  81.1 37.5 all-gather.20
  121.2 29.0 all-gather.22
  302.1 107.9 reduce-scatter.6
  412.4 39.4 all-gather.24
  453.9 63.4 all-gather.14
  519.3 27.6 all-gather.26
  549.2 63.4 all-gather.16
  991.1 109.1 reduce-scatter.10
  1102.4 111.2 reduce-scatter.8
  1218.2 64.0 all-gather.18
  1575.1 109.5 reduce-scatter.12
  1688.2 54.3 reduce-scatter.16
  1746.4 76.4 reduce-scatter.14
  1830.5 149.6 all-reduce.47
where the time goes:
time: 2390 us; the launch traced here: 2380 us
  waiting for transfers between devices  915 us (38%)
  matrix products  580 us (24%)
  local copies, waits for them, and re-layouts  568 us (24%)
  other arithmetic  242 us (10%)
  blocking collectives  39.6 us (2%)
    dynamic_update_slice x64, local copies, waits for them, and re-layouts, mixer_core(): last_state, outputs = lax.scan(jax.checkpoint(span_step), initial, pieces)  323 us
    reduce_scatter x2, waiting for transfers between devices, body(): lax.psum_scatter(lax.dot_general(scaled_low, w_out, (((1,), (1,)), ((), (...  217 us
    reduce_scatter x2, waiting for transfers between devices, body(): lax.psum_scatter(from_gate + from_shared, 'tensor', scatter_dimension=0,...  158 us
    psum x1, waiting for transfers between devices, body(): lax.psum((jnp.stack(shared_grads), jnp.stack(small_grads)), ('dp', 'tenso...  145 us
    dot_general x15, matrix products, orthogonal(): current = coef_first * current + jnp.dot(poly, current, precision=highest)  123 us
    all_gather x2, waiting for transfers between devices, body(): gathered = lax.all_gather(normed_low, 'tensor', axis=0, tiled=True)  122 us
    dot_general x24, matrix products, span_step(): inside = jnp.einsum('hts,hsp->htp', mixing, head_values, precision=highest)  105 us
    dot_general x15, matrix products, orthogonal(): gram = jnp.dot(current, current.T, precision=highest)  104 us
  transfers between devices with their start and end apart: 17, of which 13 were waited for; matrix products, arithmetic and copies ran while one was open for 22% of the time, Pallas kernels for 0%

commit v1 on v0

v1 whole, which is shorter than its diff:
```python
import functools

import jax
import jax.numpy as jnp
from jax import lax
from jax.experimental import pallas as pl
from jax.experimental.pallas import tpu as pltpu
from jax.sharding import PartitionSpec as P

D = 1536
INNER = 3072
HEADS = 48
STATE = 128
KERNEL = 4
SPAN = 256
LAYERS = 2
STEP = 10
SSM_COLS = 304
WIDTH = INNER // HEADS
LANES = 128
SHARED_COLS = 2 * STATE + LANES
HALO = 8

epsilon = 1e-05
highest = lax.Precision.HIGHEST
coef_first = 3.4445
coef_second = -4.775
coef_third = 2.0315
muon_decay = 0.95
muon_rate = 0.2
beta_first = 0.9
beta_second = 0.95
adam_rate = 0.2

MESH = pl.DeviceIdType.MESH
NN = (((1,), (0,)), ((), ()))
NT = (((1,), (1,)), ((), ()))
TN = (((0,), (0,)), ((), ()))
f32 = jnp.float32
bf16 = jnp.bfloat16


def dot(left, right, dims=NN):
    return lax.dot_general(left, right, dims, preferred_element_type=f32)


def dot_exact(left, right, dims=NN):
    return lax.dot_general(left, right, dims, precision=highest, preferred_element_type=f32)


def sigmoid(v):
    return 0.5 * jnp.tanh(0.5 * v) + 0.5


def softplus(v):
    small = jnp.exp(-jnp.abs(v))
    series = small * (1.0 - small * (0.5 - small * (1.0 / 3.0 - small * 0.25)))
    return jnp.maximum(v, 0.0) + jnp.where(small < 0.01, series, jnp.log(1.0 + small))


def steps_of(raw_in, ph_ref):
    raw = raw_in + ph_ref[1:2, :]
    timestep = softplus(raw)
    decay = -jnp.exp(ph_ref[0:1, :])
    log_decay = timestep * decay
    rows = lax.broadcasted_iota(jnp.int32, (SPAN, SPAN), 0)
    cols = lax.broadcasted_iota(jnp.int32, (SPAN, SPAN), 1)
    lower = jnp.where(rows >= cols, 1.0, 0.0).astype(f32)
    cumulative = dot_exact(lower, log_decay)
    return raw, timestep, decay, log_decay, cumulative, lower


def pair_of(table, pair, low_half):
    return jnp.where(low_half, table[:, 2 * pair : 2 * pair + 1], table[:, 2 * pair + 1 : 2 * pair + 2])


def conv_of(pad, lanes, weights, first):
    total = weights[4:5, lanes] + weights[0:1, lanes] * pad[first : first + SPAN, lanes]
    for tap in range(1, KERNEL):
        total = total + weights[tap : tap + 1, lanes] * pad[first + tap : first + tap + SPAN, lanes]
    return total


def head_sums(values, owner):
    high = values.astype(bf16)
    low = (values - high.astype(f32)).astype(bf16)
    return dot(jnp.concatenate([high, low], 1), owner)


def matmul_into(target, left, right, dims, width, piece):
    for at in range(0, width, piece):
        cols = slice(at, min(at + piece, width))
        mine = right[:, cols] if dims == NN else right[cols, :]
        target[:, cols] = dot(left, mine, dims).astype(target.dtype)


def forward_kernel(
    g_ref, w_ref, wo_ref, px_ref, ps_ref, ph_ref, proj_ref, yt_ref, p_ref, sq_ref, st_ref, state, xpad, spad, gained
):
    step = pl.program_id(0)
    columns = yt_ref.shape[1]
    pairs = columns // LANES

    @pl.when(step == 0)
    def _():
        state[...] = jnp.zeros_like(state)
        xpad[0:HALO, :] = jnp.zeros((HALO, columns), f32)
        spad[0:HALO, :] = jnp.zeros((HALO, 2 * STATE), f32)

    @pl.when(step > 0)
    def _():
        xpad[0:HALO, :] = xpad[SPAN : SPAN + HALO, :]
        spad[0:HALO, :] = spad[SPAN : SPAN + HALO, :]

    matmul_into(proj_ref, g_ref[...], w_ref, NN, 2 * columns + SHARED_COLS, 2 * LANES)
    xpad[HALO:, :] = proj_ref[:, columns : 2 * columns]
    spad[HALO:, :] = proj_ref[:, 2 * columns : 2 * columns + 2 * STATE]
    first = HALO - KERNEL + 1
    pre_s = conv_of(spad, slice(None), ps_ref, first)
    bc = pre_s * sigmoid(pre_s)
    b_low, c_low = bc[:, :STATE].astype(bf16), bc[:, STATE:].astype(bf16)
    raw, timestep, decay, log_decay, cumulative, lower = steps_of(proj_ref[:, 2 * columns + 2 * STATE :], ph_ref)
    turned = cumulative.T
    grown = jnp.exp(cumulative)
    tail = jnp.exp(cumulative[SPAN - 1 : SPAN, :] - cumulative)
    scores = dot(c_low, b_low, NT) * lower
    low_half = lax.broadcasted_iota(jnp.int32, (SPAN, LANES), 1) < WIDTH
    squares = jnp.zeros((SPAN, LANES), f32)
    half = SPAN // 2
    for pair in range(pairs):
        lanes = slice(pair * LANES, (pair + 1) * LANES)
        pre = conv_of(xpad, lanes, px_ref, first)
        xc = pre * sigmoid(pre)
        u = xc * pair_of(timestep, pair, low_half)
        u_low = u.astype(bf16)
        mine = [jnp.where(low_half == (side == 0), u_low, jnp.zeros_like(u_low)) for side in range(2)]
        inside = []
        for rows, count in ((slice(0, half), half), (slice(half, SPAN), SPAN)):
            both = jnp.zeros((half, LANES), f32)
            for side in range(2):
                head = 2 * pair + side
                spread = cumulative[rows, head : head + 1] - turned[head : head + 1, :count]
                mixing = (scores[rows, :count] * jnp.exp(jnp.minimum(spread, 0.0))).astype(bf16)
                both = both + dot(mixing, mine[side][:count])
            inside.append(both)
        held = state[:, lanes]
        held_low = held.astype(bf16)
        st_ref[0, :, lanes] = held_low
        grown_pair = pair_of(grown, pair, low_half)
        carried = dot(c_low, held_low) * grown_pair
        tail_u = (pair_of(tail, pair, low_half) * u).astype(bf16)
        state[:, lanes] = grown_pair[SPAN - 1 : SPAN, :] * held + dot(b_low, tail_u, TN)
        total = jnp.concatenate(inside, 0) + carried + px_ref[6:7, lanes] * xc
        yt_ref[:, lanes] = total
        gate = proj_ref[:, lanes]
        mixed = total * gate * sigmoid(gate)
        gained[:, lanes] = (mixed * px_ref[5:6, lanes]).astype(bf16)
        squares = squares + mixed * mixed
    sq_ref[0] = dot_exact(jnp.ones((8, LANES), f32), squares, NT)
    matmul_into(p_ref, gained[...], wo_ref, NT, D, 2 * LANES)


def backward_kernel(
    dr_ref,
    w_ref,
    wo_ref,
    gate_ref,
    x_ref,
    xh_ref,
    sh_ref,
    shh_ref,
    yt_ref,
    st_ref,
    rd_ref,
    px_ref,
    ps_ref,
    ph_ref,
    dall_ref,
    scaled_ref,
    p_ref,
    gx_ref,
    gs_ref,
    gh_ref,
    dstate,
    xpad,
    spad,
    dxpad,
    dspad,
    dsc,
):
    step = pl.program_id(0)
    steps = pl.num_programs(0)
    columns = x_ref.shape[1]
    pairs = columns // LANES

    @pl.when(step == 0)
    def _():
        dstate[...] = jnp.zeros_like(dstate)
        dxpad[SPAN:, :] = jnp.zeros((HALO, columns), f32)
        dspad[SPAN:, :] = jnp.zeros((HALO, 2 * STATE), f32)
        gx_ref[...] = jnp.zeros_like(gx_ref)
        gs_ref[...] = jnp.zeros_like(gs_ref)
        gh_ref[...] = jnp.zeros_like(gh_ref)

    @pl.when(step > 0)
    def _():
        dxpad[SPAN:, :] = dxpad[0:HALO, :]
        dspad[SPAN:, :] = dspad[0:HALO, :]

    matmul_into(dsc, dr_ref[...], wo_ref, NN, columns, 2 * LANES)
    before = jnp.where(step < steps - 1, 1.0, 0.0).astype(f32)
    xpad[0:HALO, :] = xh_ref[...] * before
    spad[0:HALO, :] = shh_ref[:, : 2 * STATE] * before
    xpad[HALO:, :] = x_ref[...]
    spad[HALO:, :] = sh_ref[:, : 2 * STATE]
    first = HALO - KERNEL + 1
    pre_s = conv_of(spad, slice(None), ps_ref, first)
    sig_s = sigmoid(pre_s)
    bc = pre_s * sig_s
    b_low, c_low = bc[:, :STATE].astype(bf16), bc[:, STATE:].astype(bf16)
    raw, timestep, decay, log_decay, cumulative, lower = steps_of(sh_ref[:, 2 * STATE :], ph_ref)
    turned = cumulative.T
    grown = jnp.exp(cumulative)
    tail = jnp.exp(cumulative[SPAN - 1 : SPAN, :] - cumulative)
    upper = lower.T
    scores = dot(b_low, c_low, NT) * upper
    low_half = lax.broadcasted_iota(jnp.int32, (SPAN, LANES), 1) < WIDTH
    inverse = rd_ref[:, 0:1]
    dots = rd_ref[:, 1:2] * (1.0 / INNER)
    head_row = lax.rem(lax.broadcasted_iota(jnp.int32, (2 * LANES, LANES), 0), LANES) // WIDTH
    head_col = lax.broadcasted_iota(jnp.int32, (2 * LANES, LANES), 1)

    half = SPAN // 2
    d_scores = [jnp.zeros((half, SPAN), f32), jnp.zeros((half, half), f32)]
    d_b = jnp.zeros((SPAN, STATE), f32)
    d_c = jnp.zeros((SPAN, STATE), f32)
    d_cum = jnp.zeros((SPAN, LANES), f32)
    d_step = jnp.zeros((SPAN, LANES), f32)
    d_last = jnp.zeros((8, LANES), f32)
    for pair in range(pairs):
        lanes = slice(pair * LANES, (pair + 1) * LANES)
        owner = jnp.where(head_row + 2 * pair == head_col, 1.0, 0.0).astype(bf16)
        pre = conv_of(xpad, lanes, px_ref, first)
        sig = sigmoid(pre)
        xc = pre * sig
        step_pair = pair_of(timestep, pair, low_half)
        u = xc * step_pair
        u_low = u.astype(bf16)
        gate = gate_ref[:, lanes]
        sig_gate = sigmoid(gate)
        silu = gate * sig_gate
        total = yt_ref[:, lanes]
        gain = px_ref[5:6, lanes]
        sn = total * silu * inverse
        scaled_ref[:, lanes] = (sn * gain).astype(bf16)
        d_scaled = dsc[:, lanes]
        gx_ref[5:6, lanes] += jnp.sum(d_scaled * sn, 0, keepdims=True)
        d_mixed = inverse * (d_scaled * gain - sn * dots)
        dall_ref[:, lanes] = (
            d_mixed * total * (sig_gate * (1.0 + gate * (1.0 - sig_gate)))
        ).astype(bf16)
        dy = d_mixed * silu
        skip = px_ref[6:7, lanes]
        gx_ref[6:7, lanes] += jnp.sum(dy * xc, 0, keepdims=True)
        dy_low = dy.astype(bf16)
        mine = [jnp.where(low_half == (side == 0), dy_low, jnp.zeros_like(dy_low)) for side in range(2)]
        du = []
        for block, start in ((0, 0), (1, half)):
            rows = slice(start, start + half)
            both = jnp.zeros((half, LANES), f32)
            for side in range(2):
                head = 2 * pair + side
                spread = turned[head : head + 1, start:] - cumulative[rows, head : head + 1]
                mask = jnp.exp(jnp.minimum(spread, 0.0))
                mixing = (scores[rows, start:] * mask).astype(bf16)
                both = both + dot(mixing, mine[side][start:])
                d_scores[block] = d_scores[block] + dot(u_low[rows], mine[side][start:], NT) * mask
            du.append(both)
        held_low = st_ref[0, :, lanes]
        grown_pair = pair_of(grown, pair, low_half)
        last_pair = grown_pair[SPAN - 1 : SPAN, :]
        d_after = dstate[:, lanes]
        d_after_low = d_after.astype(bf16)
        grown_dy = (grown_pair * dy).astype(bf16)
        d_c = d_c + dot(grown_dy, held_low, NT)
        tail_pair = pair_of(tail, pair, low_half)
        du_tail = tail_pair * dot(b_low, d_after_low)
        d_b = d_b + dot((tail_pair * u).astype(bf16), d_after_low, NT)
        dstate[:, lanes] = last_pair * d_after + dot(c_low, grown_dy, TN)
        du = jnp.concatenate(du, 0) + du_tail
        u_round = u_low.astype(f32)
        y = total - skip * xc
        d_cum = d_cum + head_sums(dy_low.astype(f32) * y - u_round * du, owner)
        d_step = d_step + head_sums(xc * du, owner)
        ends = jnp.sum(u_round * du_tail, 0, keepdims=True) + last_pair * jnp.sum(
            d_after * held_low.astype(f32), 0, keepdims=True
        )
        d_last = d_last + head_sums(jnp.broadcast_to(ends, (8, LANES)), owner)
        d_pre = (skip * dy + step_pair * du) * (sig * (1.0 + pre * (1.0 - sig)))
        dxpad[0:SPAN, lanes] = d_pre
        d_x = px_ref[KERNEL - 1 : KERNEL, lanes] * d_pre
        gx_ref[4:5, lanes] += jnp.sum(d_pre, 0, keepdims=True)
        for tap in range(KERNEL):
            gx_ref[tap : tap + 1, lanes] += jnp.sum(
                d_pre * xpad[first + tap : first + tap + SPAN, lanes], 0, keepdims=True
            )
            if tap < KERNEL - 1:
                ahead = KERNEL - 1 - tap
                d_x = d_x + px_ref[tap : tap + 1, lanes] * dxpad[ahead : ahead + SPAN, lanes]
        dall_ref[:, columns + pair * LANES : columns + (pair + 1) * LANES] = d_x.astype(bf16)
    d_log = dot_exact(upper, d_cum) + d_last[0:1, :]
    d_raw = (d_step + d_log * decay) * sigmoid(raw)
    gh_ref[0:1, :] += jnp.sum(d_log * log_decay, 0, keepdims=True)
    gh_ref[1:2, :] += jnp.sum(d_raw, 0, keepdims=True)
    d_scores = jnp.concatenate(
        [d_scores[0], jnp.concatenate([jnp.zeros((half, half), f32), d_scores[1]], 1)], 0
    )
    d_scores_low = (d_scores * upper).astype(bf16)
    d_b = d_b + dot(d_scores_low, c_low)
    d_c = d_c + dot(d_scores_low, b_low, TN)
    slope_s = sig_s * (1.0 + pre_s * (1.0 - sig_s))
    d_pre_s = jnp.concatenate([d_b, d_c], 1) * slope_s
    dspad[0:SPAN, :] = d_pre_s
    d_s = ps_ref[KERNEL - 1 : KERNEL, :] * d_pre_s
    gs_ref[4:5, :] += jnp.sum(d_pre_s, 0, keepdims=True)
    for tap in range(KERNEL):
        gs_ref[tap : tap + 1, :] += jnp.sum(
            d_pre_s * spad[first + tap : first + tap + SPAN, :], 0, keepdims=True
        )
        if tap < KERNEL - 1:
            ahead = KERNEL - 1 - tap
            d_s = d_s + ps_ref[tap : tap + 1, :] * dspad[ahead : ahead + SPAN, :]
    dall_ref[:, 2 * columns : 2 * columns + 2 * STATE] = d_s.astype(bf16)
    dall_ref[:, 2 * columns + 2 * STATE :] = d_raw.astype(bf16)
    matmul_into(p_ref, dall_ref[...], w_ref, NT, D, 2 * LANES)


def resident(shape):
    return pl.BlockSpec(shape, lambda i: (0, 0), pipeline_mode=pl.Buffered(1))


def mixer_forward(gathered, w_in, w_out, px, ps, ph):
    length, columns = gathered.shape[0], px.shape[1]
    spans = length // SPAN
    width = 2 * columns + SHARED_COLS
    here = lambda i: (i, 0)
    return pl.pallas_call(
        forward_kernel,
        grid=(spans,),
        in_specs=[
            pl.BlockSpec((SPAN, D), here),
            resident((D, width)),
            resident((D, columns)),
            resident((8, columns)),
            resident((8, 2 * STATE)),
            resident((8, LANES)),
        ],
        out_specs=[
            pl.BlockSpec((SPAN, width), here),
            pl.BlockSpec((SPAN, columns), here),
            pl.BlockSpec((SPAN, D), here),
            pl.BlockSpec((1, 8, SPAN), lambda i: (i, 0, 0)),
            pl.BlockSpec((1, STATE, columns), lambda i: (i, 0, 0)),
        ],
        out_shape=[
            jax.ShapeDtypeStruct((length, width), f32),
            jax.ShapeDtypeStruct((length, columns), f32),
            jax.ShapeDtypeStruct((length, D), bf16),
            jax.ShapeDtypeStruct((spans, 8, SPAN), f32),
            jax.ShapeDtypeStruct((spans, STATE, columns), bf16),
        ],
        scratch_shapes=[
            pltpu.VMEM((STATE, columns), f32),
            pltpu.VMEM((SPAN + HALO, columns), f32),
            pltpu.VMEM((SPAN + HALO, 2 * STATE), f32),
            pltpu.VMEM((SPAN, columns), bf16),
        ],
        compiler_params=pltpu.CompilerParams(vmem_limit_bytes=56 * 2**20),
        cost_estimate=pl.CostEstimate(flops=10 * 10**9, bytes_accessed=32 * 2**20, transcendentals=0),
    )(gathered, w_in, w_out, px, ps, ph)


def mixer_backward(d_rows, w_in, w_out, projected, total, states, rd, px, ps, ph):
    length, columns = total.shape
    spans = length // SPAN
    width = 2 * columns + SHARED_COLS
    here = lambda i: (spans - 1 - i, 0)
    blocks = SPAN // HALO
    halo = lambda i: jnp.maximum((spans - 1 - i) * blocks - 1, 0)
    tail_block = 2 * columns // SHARED_COLS
    return pl.pallas_call(
        backward_kernel,
        grid=(spans,),
        in_specs=[
            pl.BlockSpec((SPAN, D), here),
            resident((D, width)),
            resident((D, columns)),
            pl.BlockSpec((SPAN, columns), here),
            pl.BlockSpec((SPAN, columns), lambda i: (spans - 1 - i, 1)),
            pl.BlockSpec((HALO, columns), lambda i: (halo(i), 1)),
            pl.BlockSpec((SPAN, SHARED_COLS), lambda i: (spans - 1 - i, tail_block)),
            pl.BlockSpec((HALO, SHARED_COLS), lambda i: (halo(i), tail_block)),
            pl.BlockSpec((SPAN, columns), here),
            pl.BlockSpec((1, STATE, columns), lambda i: (spans - 1 - i, 0, 0)),
            pl.BlockSpec((SPAN, 2), here),
            resident((8, columns)),
            resident((8, 2 * STATE)),
            resident((8, LANES)),
        ],
        out_specs=[
            pl.BlockSpec((SPAN, width), here),
            pl.BlockSpec((SPAN, columns), here),
            pl.BlockSpec((SPAN, D), here),
            pl.BlockSpec((8, columns), lambda i: (0, 0)),
            pl.BlockSpec((8, 2 * STATE), lambda i: (0, 0)),
            pl.BlockSpec((8, LANES), lambda i: (0, 0)),
        ],
        out_shape=[
            jax.ShapeDtypeStruct((length, width), bf16),
            jax.ShapeDtypeStruct((length, columns), bf16),
            jax.ShapeDtypeStruct((length, D), bf16),
            jax.ShapeDtypeStruct((8, columns), f32),
            jax.ShapeDtypeStruct((8, 2 * STATE), f32),
            jax.ShapeDtypeStruct((8, LANES), f32),
        ],
        scratch_shapes=[
            pltpu.VMEM((STATE, columns), f32),
            pltpu.VMEM((SPAN + HALO, columns), f32),
            pltpu.VMEM((SPAN + HALO, 2 * STATE), f32),
            pltpu.VMEM((SPAN + HALO, columns), f32),
            pltpu.VMEM((SPAN + HALO, 2 * STATE), f32),
            pltpu.VMEM((SPAN, columns), f32),
        ],
        compiler_params=pltpu.CompilerParams(vmem_limit_bytes=56 * 2**20),
        cost_estimate=pl.CostEstimate(flops=16 * 10**9, bytes_accessed=48 * 2**20, transcendentals=0),
    )(
        d_rows,
        w_in,
        w_out,
        projected,
        projected,
        projected,
        projected,
        projected,
        total,
        states,
        rd,
        px,
        ps,
        ph,
    )


def kernels_fit():
    return lax.axis_size("tensor") == 4 and lax.axis_size("dp") == 8


def neighbours():
    index = lax.axis_index("dp")
    core = lax.rem(index, 2)
    across = lax.rem(lax.div(index, 2), 2)
    along = lax.div(index, 4)
    return index, core, index + 1 - 2 * core, index + 2 - 4 * across, index + 4 - 8 * along


def greet(others):
    barrier = pltpu.get_barrier_semaphore()
    for other in others:
        pl.semaphore_signal(barrier, inc=1, device_id=other, device_id_type=MESH)
    pl.semaphore_wait(barrier, len(others))


def remote(source, target, send_sem, recv_sem, slot, where):
    return pltpu.make_async_remote_copy(
        src_ref=source,
        dst_ref=target,
        send_sem=send_sem.at[slot],
        recv_sem=recv_sem.at[slot],
        device_id=where,
        device_id_type=MESH,
    )


class Line:
    def __init__(self, side):
        me = lax.axis_index("tensor")
        self.side = side
        self.me = me
        self.pos = me if side == 0 else 3 - me
        self.next = {"tensor": lax.rem(me + (1 if side == 0 else 3), 4)}

    def chunk(self, ahead):
        return self.me + ahead if self.side == 0 else self.me - ahead


def rows_at(ref, chunk, count):
    return ref.at[pl.ds(pl.multiple_of(chunk * count, count), count), :]


class LineCopy:
    def __init__(self, lines, source, place, local_sem, send_sem, recv_sem):
        self.lines, self.source, self.place = lines, source, place
        self.send_sem, self.recv_sem = send_sem, recv_sem
        self.own = pltpu.make_async_copy(source, place(lines[0].me), local_sem)

    def outgoing(self, line, time):
        place = self.place(line.chunk(-time))
        source = self.source if time == 0 else place
        return remote(source, place, self.send_sem, self.recv_sem, 3 * line.side + time, line.next)

    def start(self):
        for line in self.lines:

            @pl.when(line.pos < 3)
            def _(line=line):
                self.outgoing(line, 0).start()

        self.own.start()

    def step(self, time):
        for line in self.lines:

            @pl.when(line.pos >= time)
            def _(line=line):
                place = self.place(line.chunk(-time))
                slot = 3 * line.side + time - 1
                remote(place, place, self.send_sem, self.recv_sem, slot, line.next).wait_recv()

            if time < 3:

                @pl.when(jnp.logical_and(line.pos >= time, line.pos < 3))
                def _(line=line):
                    self.outgoing(line, time).start()

    def finish(self):
        for time in range(3):
            for line in self.lines:

                @pl.when(jnp.logical_and(line.pos >= time, line.pos < 3))
                def _(line=line):
                    self.outgoing(line, time).wait_send()

        self.own.wait()


class SquareCopy:
    def __init__(self, source, result, local_sem, send_sem, recv_sem):
        self.source, self.result = source, result
        self.send_sem, self.recv_sem = send_sem, recv_sem
        self.rows = source.shape[0]
        self.split = near_rows(self.rows)
        self.index, core, self.sibling, self.by_x, self.by_y = neighbours()
        self.own = pltpu.make_async_copy(source, self.place(self.index, None), local_sem)

    def place(self, owner, side):
        start, count = {None: (0, self.rows), 0: (0, self.split), 1: (self.split, self.rows - self.split)}[side]
        return self.result.at[pl.ds(pl.multiple_of(owner * self.rows + start, 16), count), :]

    def copy(self, slot):
        near, far = self.source.at[pl.ds(0, self.split), :], self.source.at[pl.ds(self.split, self.rows - self.split), :]
        by_x, by_y = self.by_x, self.by_y
        source, owner, side, where = {
            0: (near, self.index, 0, by_x),
            1: (far, self.index, 1, by_y),
            2: (far, self.index, 1, by_x),
            3: (near, self.index, 0, by_y),
            4: (None, by_x, 0, by_y),
            5: (None, by_y, 1, by_x),
            6: (self.source, self.index, None, self.sibling),
            7: (None, by_x, None, self.sibling),
            8: (None, by_y, None, self.sibling),
            9: (None, by_x + by_y - self.index, None, self.sibling),
        }[slot]
        target = self.place(owner, side)
        return remote(target if source is None else source, target, self.send_sem, self.recv_sem, slot, {"dp": where})

    def start(self):
        for slot in (0, 1, 2, 3, 6):
            self.copy(slot).start()
        self.own.start()

    def relay(self):
        self.copy(0).wait_recv()
        self.copy(4).start()
        self.copy(1).wait_recv()
        self.copy(5).start()

    def forward(self):
        self.copy(2).wait_recv()
        self.copy(7).start()
        self.copy(3).wait_recv()
        self.copy(8).start()

    def last(self):
        self.copy(4).wait_recv()
        self.copy(5).wait_recv()
        self.copy(9).start()

    def finish(self):
        for slot in range(6, 10):
            self.copy(slot).wait_recv()
        for slot in range(10):
            self.copy(slot).wait_send()
        self.own.wait()


def first_kernel(x_ref, w_ref, v_ref, ox_ref, ow_ref, ov_ref, *sems):
    lines = (Line(0), Line(1))
    rows = x_ref.shape[0]
    me = lax.axis_index("tensor")
    index, core, sibling, by_x, by_y = neighbours()
    greet([{"tensor": lax.rem(me + 1, 4)}, {"tensor": lax.rem(me + 3, 4)}, {"dp": sibling}, {"dp": by_x}, {"dp": by_y}])
    tokens = LineCopy(lines, x_ref, lambda chunk: rows_at(ox_ref, chunk, rows), *sems[:3])
    weights = [SquareCopy(w_ref, ow_ref, *sems[3:6]), SquareCopy(v_ref, ov_ref, *sems[6:])]
    tokens.start()
    for each in weights:
        each.start()
    for each in weights:
        each.relay()
    tokens.step(1)
    for each in weights:
        each.forward()
    tokens.step(2)
    for each in weights:
        each.last()
    tokens.step(3)
    for each in weights:
        each.finish()
    tokens.finish()


def gather_first(rows, w_rows, v_rows):
    if not kernels_fit():
        return (
            lax.all_gather(rows, "tensor", axis=0, tiled=True),
            lax.all_gather(w_rows, "dp", axis=0, tiled=True),
            lax.all_gather(v_rows, "dp", axis=0, tiled=True),
        )
    anywhere = pl.BlockSpec(memory_space=pl.ANY)
    larger = lambda v, times: jax.ShapeDtypeStruct((times * v.shape[0], v.shape[1]), v.dtype)
    sems = lambda count: [
        pltpu.SemaphoreType.DMA,
        pltpu.SemaphoreType.DMA((count,)),
        pltpu.SemaphoreType.DMA((count,)),
    ]
    return pl.pallas_call(
        first_kernel,
        out_shape=(larger(rows, 4), larger(w_rows, 8), larger(v_rows, 8)),
        in_specs=[anywhere] * 3,
        out_specs=(anywhere,) * 3,
        scratch_shapes=[*sems(6), *sems(10), *sems(10)],
        compiler_params=pltpu.CompilerParams(collective_id=6, has_side_effects=True),
        cost_estimate=pl.CostEstimate(flops=0, bytes_accessed=150 * 2**20, transcendentals=0),
    )(rows, w_rows, v_rows)


def gather_tokens(rows, small):
    if not kernels_fit():
        return lax.all_gather(rows, "tensor", axis=0, tiled=True), lax.all_gather(small, "tensor", axis=0)
    count, columns = rows.shape
    vmem = pl.BlockSpec(memory_space=pltpu.VMEM)
    anywhere = pl.BlockSpec(memory_space=pl.ANY)
    return pl.pallas_call(
        gather_kernel,
        out_shape=(
            jax.ShapeDtypeStruct((4 * count, columns), rows.dtype),
            jax.ShapeDtypeStruct((4, *small.shape), small.dtype),
        ),
        in_specs=[anywhere, vmem],
        out_specs=(anywhere, vmem),
        scratch_shapes=[
            pltpu.SemaphoreType.DMA,
            pltpu.SemaphoreType.DMA,
            pltpu.SemaphoreType.DMA((6,)),
            pltpu.SemaphoreType.DMA((6,)),
            pltpu.SemaphoreType.DMA((6,)),
            pltpu.SemaphoreType.DMA((6,)),
        ],
        compiler_params=pltpu.CompilerParams(collective_id=0, has_side_effects=True),
        cost_estimate=pl.CostEstimate(flops=0, bytes_accessed=150 * 2**20, transcendentals=0),
    )(rows, small)


class LineSum:
    def __init__(self, lines, p_ref, o_ref, came, send_sem, recv_sem, first_row=0):
        self.lines, self.p_ref, self.o_ref, self.came = lines, p_ref, o_ref, came
        self.send_sem, self.recv_sem = send_sem, recv_sem
        self.first_row, self.count = first_row, came.shape[1]
        self.rows = p_ref.shape[0] // 4

    def part(self, chunk):
        start = pl.multiple_of(chunk * self.rows + self.first_row, self.count)
        return self.p_ref.at[pl.ds(start, self.count), :]

    def copy(self, line, time, first):
        slot = 3 * line.side + time
        target = self.came.at[slot]
        source = self.part(line.chunk(3 - time)) if first else self.came.at[slot - 1]
        return remote(source, target, self.send_sem, self.recv_sem, slot, line.next)

    def start(self, times=(0, 1, 2)):
        for line in self.lines:

            @pl.when(line.pos == 0)
            def _(line=line):
                for time in times:
                    self.copy(line, time, True).start()

    def step(self, time):
        for line in self.lines:

            @pl.when(jnp.logical_and(line.pos > 0, line.pos <= time))
            def _(line=line):
                slot = 3 * line.side + time - 1
                place = self.came.at[slot]
                remote(place, place, self.send_sem, self.recv_sem, slot, line.next).wait_recv()

            if time < 3:

                @pl.when(jnp.logical_and(line.pos > 0, line.pos <= time))
                def _(line=line):
                    slot = 3 * line.side + time - 1
                    mine = self.part(line.chunk(3 - time))[...]
                    self.came[slot] = (self.came[slot].astype(f32) + mine.astype(f32)).astype(bf16)
                    self.copy(line, time, False).start()

    def own(self):
        place = pl.ds(self.first_row, self.count)
        self.o_ref[place, :] = self.part(self.lines[0].me)[...].astype(f32)
        for line in self.lines:

            @pl.when(line.pos > 0)
            def _(line=line):
                self.o_ref[place, :] += self.came[3 * line.side + 2].astype(f32)

    def finish(self):
        for line in self.lines:

            @pl.when(line.pos == 0)
            def _(line=line):
                for time in range(3):
                    self.copy(line, time, True).wait_send()

            for time in range(1, 3):

                @pl.when(jnp.logical_and(line.pos > 0, line.pos <= time))
                def _(line=line):
                    self.copy(line, time, False).wait_send()


class Pass:
    def __init__(self, lines, p_ref, o_ref, came, x_ref, ox_ref, sems, work):
        half = came.shape[2]
        self.work = work
        self.sums, self.copies = [], []
        for part in range(2):
            sum_send, sum_recv, copy_local, copy_send, copy_recv = sems[5 * part : 5 * part + 5]
            first_row = part * half
            self.sums.append(LineSum(lines, p_ref, o_ref, came.at[part], sum_send, sum_recv, first_row))
            place = lambda chunk, first_row=first_row: ox_ref.at[
                pl.ds(pl.multiple_of(chunk * 2 * half + first_row, half), half), :
            ]
            source = x_ref.at[pl.ds(first_row, half), :]
            self.copies.append(LineCopy(lines, source, place, copy_local, copy_send, copy_recv))

    def start(self):
        self.sums[0].start()
        self.sums[1].start((0,))

    def turn(self, part):
        self.sums[part].step(3)
        self.sums[part].own()
        self.work(part)
        self.copies[part].start()

    def between(self):
        self.sums[1].start((1, 2))
        self.sums[1].step(1)

    def across(self):
        self.copies[0].step(1)
        self.sums[1].step(2)
        self.copies[0].step(2)

    def last(self):
        self.copies[0].step(3)
        for time in range(1, 4):
            self.copies[1].step(time)

    def finish(self):
        for each in (*self.sums, *self.copies):
            each.finish()


def pass_sems():
    line = pltpu.SemaphoreType.DMA((6,))
    return [line, line, pltpu.SemaphoreType.DMA, line, line] * 2


def column_of(row, count):
    return jnp.broadcast_to(row, (LANES, count)).T[:, 0:1]


def forward_pass_kernel(
    p_any,
    q_ref,
    r_ref,
    gain_ref,
    or_ref,
    ob_ref,
    oi_ref,
    ox_ref,
    p_ref,
    normed,
    came,
    came_q,
    fetch_sem,
    small_send,
    small_recv,
    *sems,
):
    lines = (Line(0), Line(1))
    me = lax.axis_index("tensor")
    others = [{"tensor": lax.rem(me + ahead, 4)} for ahead in (1, 2, 3)]
    fetch = pltpu.make_async_copy(p_any, p_ref, fetch_sem)
    fetch.start()
    greet(others)
    small = [
        remote(q_ref.at[lax.rem(me + slot + 1, 4)], came_q.at[slot], small_send, small_recv, slot, other)
        for slot, other in enumerate(others)
    ]
    for copy in small:
        copy.start()
    count = r_ref.shape[0]
    half = count // 2

    def work(part):
        rows = slice(part * half, (part + 1) * half)
        branch = ob_ref[rows, :] * column_of(oi_ref[0:1, rows], half)
        ob_ref[rows, :] = branch
        fresh = r_ref[rows, :] + branch
        or_ref[rows, :] = fresh
        inverse = lax.rsqrt(jnp.mean(fresh * fresh, -1, keepdims=True) + epsilon)
        normed[rows, :] = (fresh * inverse * gain_ref[0:1, :]).astype(bf16)

    line_pass = Pass(lines, p_ref, ob_ref, came, normed, ox_ref, sems, work)
    fetch.wait()
    line_pass.start()
    for copy in small:
        copy.wait_recv()
    oi_ref[...] = lax.rsqrt((q_ref[me] + came_q[0] + came_q[1] + came_q[2]) * (1.0 / INNER) + epsilon)
    line_pass.sums[0].step(1)
    line_pass.sums[0].step(2)
    line_pass.turn(0)
    line_pass.between()
    line_pass.across()
    line_pass.turn(1)
    line_pass.last()
    line_pass.finish()
    for copy in small:
        copy.wait_send()


def forward_pass(partial, squares, residual, in_gain):
    count, columns = residual.shape
    if not kernels_fit():
        summed, side = scatter_tokens(partial, squares)
        scale = lax.rsqrt(side / INNER + epsilon)
        branch = summed * scale[0][:, None]
        fresh = residual + branch
        inverse = lax.rsqrt(jnp.mean(fresh * fresh, -1, keepdims=True) + epsilon)
        normed = (fresh * inverse * in_gain).astype(bf16)
        return fresh, branch, scale, lax.all_gather(normed, "tensor", axis=0, tiled=True)
    vmem = pl.BlockSpec(memory_space=pltpu.VMEM)
    anywhere = pl.BlockSpec(memory_space=pl.ANY)
    return pl.pallas_call(
        forward_pass_kernel,
        out_shape=(
            jax.ShapeDtypeStruct((count, columns), f32),
            jax.ShapeDtypeStruct((count, columns), f32),
            jax.ShapeDtypeStruct((8, count), f32),
            jax.ShapeDtypeStruct((4 * count, columns), bf16),
        ),
        in_specs=[anywhere, vmem, vmem, vmem],
        out_specs=(vmem, vmem, vmem, anywhere),
        scratch_shapes=[
            pltpu.VMEM(partial.shape, bf16),
            pltpu.VMEM((count, columns), bf16),
            pltpu.VMEM((2, 6, count // 2, columns), bf16),
            pltpu.VMEM((3, 8, count), f32),
            pltpu.SemaphoreType.DMA,
            pltpu.SemaphoreType.DMA((3,)),
            pltpu.SemaphoreType.DMA((3,)),
            *pass_sems(),
        ],
        compiler_params=pltpu.CompilerParams(
            collective_id=2, has_side_effects=True, vmem_limit_bytes=40 * 2**20
        ),
        cost_estimate=pl.CostEstimate(flops=0, bytes_accessed=250 * 2**20, transcendentals=0),
    )(partial, squares, residual, jnp.broadcast_to(in_gain[None], (8, columns)))


def scatter_kernel(
    p_ref,
    q_ref,
    x_ref,
    o_ref,
    oq_ref,
    ox_ref,
    rd_ref,
    came,
    came_q,
    send_sem,
    recv_sem,
    small_send,
    small_recv,
    local_sem,
    copy_send,
    copy_recv,
    scalars,
    rd_local,
    rd_send,
    rd_recv,
):
    lines = (Line(0), Line(1))
    me = lax.axis_index("tensor")
    others = [{"tensor": lax.rem(me + ahead, 4)} for ahead in (1, 2, 3)]
    greet(others)
    small = [
        remote(q_ref.at[lax.rem(me + slot + 1, 4)], came_q.at[slot], small_send, small_recv, slot, other)
        for slot, other in enumerate(others)
    ]
    for copy in small:
        copy.start()
    rows = x_ref.shape[0]
    place = lambda chunk: rows_at(ox_ref, chunk, rows)
    total = LineSum(lines, p_ref, o_ref, came, send_sem, recv_sem)
    streams = [LineCopy(lines, x_ref, place, local_sem, copy_send, copy_recv), total]
    for stream in streams:
        stream.start()
    for copy in small:
        copy.wait_recv()
    oq_ref[...] = q_ref[me] + came_q[0] + came_q[1] + came_q[2]
    for time in range(1, 4):
        for stream in streams:
            stream.step(time)
    total.own()
    inverse = lax.rsqrt(oq_ref[...] * (1.0 / INNER) + epsilon)
    products = x_ref[...].astype(f32) * o_ref[...]
    dots = dot_exact(jnp.ones((8, products.shape[1]), f32), products, NT) * inverse
    first_row = lax.broadcasted_iota(jnp.int32, scalars.shape, 0) == 0
    scalars[...] = jnp.where(first_row, inverse, dots)
    copies = [remote(scalars, rd_ref.at[me], rd_send, rd_recv, slot, other) for slot, other in enumerate(others)]
    copies.append(pltpu.make_async_copy(scalars, rd_ref.at[me], rd_local))
    for copy in copies:
        copy.start()
    for stream in streams:
        stream.finish()
    for copy in small:
        copy.wait_send()
    for copy in copies:
        copy.wait()


def scatter_tokens(partial, extra, rows=None):
    if not kernels_fit():
        total = lax.psum_scatter(partial, "tensor", scatter_dimension=0, tiled=True).astype(f32)
        flat = jnp.transpose(extra, (0, 2, 1)).reshape(partial.shape[0], 8)
        side = lax.psum_scatter(flat, "tensor", scatter_dimension=0, tiled=True).T
        if rows is None:
            return total, side
        inverse = lax.rsqrt(side / INNER + epsilon)
        dots = jnp.sum(rows.astype(f32) * total, -1)[None] * inverse
        scalars = jnp.concatenate([inverse[:1], dots[1:]])
        return (
            total,
            side,
            lax.all_gather(rows, "tensor", axis=0, tiled=True),
            lax.all_gather(scalars, "tensor", axis=0),
        )
    count, columns = partial.shape[0] // 4, partial.shape[1]
    vmem = pl.BlockSpec(memory_space=pltpu.VMEM)
    anywhere = pl.BlockSpec(memory_space=pl.ANY)
    return pl.pallas_call(
        scatter_kernel,
        out_shape=(
            jax.ShapeDtypeStruct((count, columns), f32),
            jax.ShapeDtypeStruct((8, count), f32),
            jax.ShapeDtypeStruct((4 * rows.shape[0], rows.shape[1]), rows.dtype),
            jax.ShapeDtypeStruct((4, 8, count), f32),
        ),
        in_specs=[vmem] * 3,
        out_specs=(vmem, vmem, anywhere, vmem),
        scratch_shapes=[
            pltpu.VMEM((6, count, columns), bf16),
            pltpu.VMEM((3, 8, count), f32),
            pltpu.SemaphoreType.DMA((6,)),
            pltpu.SemaphoreType.DMA((6,)),
            pltpu.SemaphoreType.DMA((3,)),
            pltpu.SemaphoreType.DMA((3,)),
            pltpu.SemaphoreType.DMA,
            pltpu.SemaphoreType.DMA((6,)),
            pltpu.SemaphoreType.DMA((6,)),
            pltpu.VMEM((8, count), f32),
            pltpu.SemaphoreType.DMA,
            pltpu.SemaphoreType.DMA((3,)),
            pltpu.SemaphoreType.DMA((3,)),
        ],
        compiler_params=pltpu.CompilerParams(
            collective_id=5, has_side_effects=True, vmem_limit_bytes=32 * 2**20
        ),
        cost_estimate=pl.CostEstimate(flops=0, bytes_accessed=150 * 2**20, transcendentals=0),
    )(partial, extra, rows)


def near_rows(rows):
    return -(-rows // 32) * 16


class SquareSum:
    def __init__(self, g_ref, sib, relay, came, send_sem, recv_sem):
        self.g_ref, self.sib, self.relay, self.came = g_ref, sib, relay, came
        self.send_sem, self.recv_sem = send_sem, recv_sem
        self.rows = sib.shape[1]
        self.index, self.core, self.sibling, self.by_x, self.by_y = neighbours()
        self.chip = lax.div(self.index, 2)
        self.chip_x, self.chip_y = lax.div(self.by_x, 2), lax.div(self.by_y, 2)
        self.chip_far = 3 - self.chip
        split = near_rows(self.rows)
        self.near = pl.ds(0, split)
        self.far = pl.ds(split, self.rows - split)

    def send(self, source, target, slot, where):
        return remote(source, target, self.send_sem, self.recv_sem, slot, {"dp": where})

    def to_sibling(self, chip):
        theirs = 2 * chip + 1 - self.core
        return self.send(rows_at(self.g_ref, theirs, self.rows), self.sib.at[chip], chip, self.sibling)

    def start(self):
        for chip in range(4):
            self.to_sibling(chip).start()

    def add(self, chip):
        self.sib[chip] = (
            self.sib[chip].astype(f32) + rows_at(self.g_ref, 2 * chip + self.core, self.rows)[...].astype(f32)
        ).astype(bf16)

    def copy(self, slot):
        sib, far, near_half, far_half = self.sib, self.chip_far, self.near, self.far
        source, target, where = {
            4: (sib.at[far, near_half, :], self.relay.at[near_half, :], self.by_x),
            5: (sib.at[far, far_half, :], self.relay.at[far_half, :], self.by_y),
            6: (sib.at[self.chip_x, near_half, :], self.came.at[0, near_half, :], self.by_x),
            7: (sib.at[self.chip_y, far_half, :], self.came.at[1, far_half, :], self.by_y),
            8: (sib.at[self.chip_x, far_half, :], self.came.at[0, far_half, :], self.by_x),
            9: (sib.at[self.chip_y, near_half, :], self.came.at[1, near_half, :], self.by_y),
        }[slot]
        return self.send(source, target, slot, where)

    def cores(self):
        for chip in range(4):
            self.to_sibling(chip).wait_recv()
        self.add(self.chip_far)
        self.copy(4).start()
        self.copy(5).start()
        self.add(self.chip_x)
        self.copy(6).start()
        self.add(self.chip_y)
        self.copy(7).start()

    def join(self):
        self.copy(4).wait_recv()
        near = (self.sib[self.chip_y, self.near, :].astype(f32) + self.relay[self.near, :].astype(f32)).astype(bf16)
        self.sib[self.chip_y, self.near, :] = near
        self.copy(9).start()
        self.copy(5).wait_recv()
        far = (self.sib[self.chip_x, self.far, :].astype(f32) + self.relay[self.far, :].astype(f32)).astype(bf16)
        self.sib[self.chip_x, self.far, :] = far
        self.copy(8).start()

    def finish(self):
        for slot in range(6, 10):
            self.copy(slot).wait_recv()
        own = rows_at(self.g_ref, self.index, self.rows)[...].astype(f32) + self.sib[self.chip].astype(f32)
        for slot in range(4, 10):
            self.copy(slot).wait_send()
        for chip in range(4):
            self.to_sibling(chip).wait_send()
        return own + (self.came[0].astype(f32) + self.came[1].astype(f32))


def exchange_kernel(
    p_any,
    x_any,
    d_any,
    dr_any,
    sc_any,
    mi_ref,
    mo_ref,
    *refs,
    follows,
):
    if follows:
        (l_ref, r_ref, gain_ref, b_ref, i_ref), refs = refs[:5], refs[5:]
    (o_ref, ni_ref, no_ref, slots_ref, os_ref), refs = refs[:5], refs[5:]
    if follows:
        (or_ref, og_ref, ox_ref, rd_ref), refs = refs[:4], refs[4:]
    (p_ref, x_ref, d_ref, dr_ref, sc_ref, g_ref, h_ref, s_ref, fetch_sem), refs = refs[:9], refs[9:]
    square, refs = refs[:15], refs[15:]
    lines = (Line(0), Line(1))
    me = lax.axis_index("tensor")
    index, core, sibling, by_x, by_y = neighbours()
    fetches = [
        pltpu.make_async_copy(source, target, fetch_sem.at[slot])
        for slot, (source, target) in enumerate(
            ((p_any, p_ref), (x_any, x_ref), (d_any, d_ref), (dr_any, dr_ref), (sc_any, sc_ref))
        )
    ]
    for fetch in fetches:
        fetch.start()
    greet([{"tensor": lax.rem(me + 1, 4)}, {"tensor": lax.rem(me + 3, 4)}, {"dp": sibling}, {"dp": by_x}, {"dp": by_y}])
    sums = [SquareSum(ref, *square[5 * at : 5 * at + 5]) for at, ref in enumerate((g_ref, h_ref, s_ref))]
    if follows:
        came, low_grad, scalars, rd_local, rd_send, rd_recv, *line_sems = refs
        half = o_ref.shape[0] // 2
        og_ref[...] = jnp.zeros_like(og_ref)

        def work(part):
            rows = slice(part * half, (part + 1) * half)
            d_normed = o_ref[rows, :]
            layer_in = l_ref[rows, :]
            inverse = lax.rsqrt(jnp.mean(layer_in * layer_in, -1, keepdims=True) + epsilon)
            scaled = layer_in * inverse
            og_ref[0:1, :] += jnp.sum(d_normed * scaled, 0, keepdims=True)
            d_scaled = d_normed * gain_ref[0:1, :]
            fresh = r_ref[rows, :] + inverse * (d_scaled - scaled * jnp.mean(d_scaled * scaled, -1, keepdims=True))
            or_ref[rows, :] = fresh
            low = fresh.astype(bf16)
            low_grad[rows, :] = low
            products = low.astype(f32) * b_ref[rows, :]
            dots = dot_exact(jnp.ones((8, products.shape[1]), f32), products, NT)
            first_row = lax.broadcasted_iota(jnp.int32, dots.shape, 0) == 0
            scalars[:, rows] = jnp.where(first_row, i_ref[:, rows], dots)

        line_pass = Pass(lines, p_ref, o_ref, came, low_grad, ox_ref, line_sems, work)
        total = line_pass.sums[0]
        small = LineCopy(lines, scalars, lambda chunk: rd_ref.at[chunk], rd_local, rd_send, rd_recv)
    else:
        total = LineSum(lines, p_ref, o_ref, *refs)
    fetches[0].wait()
    if follows:
        line_pass.start()
    else:
        total.start()
    for fetch in fetches[1:]:
        fetch.wait()
    width = mo_ref.shape[1]
    share = x_ref.shape[1] // 4

    def grads(chip):
        rows = slice(chip * share, (chip + 1) * share)
        left = x_ref[:, rows]
        for at in range(0, 2 * width, 2 * LANES):
            cols = slice(at, at + 2 * LANES)
            g_ref[rows, cols] = dot(left, d_ref[:, cols], TN).astype(bf16)
        sums[0].to_sibling(chip).start()
        left = dr_ref[:, rows]
        for at in range(0, width, 2 * LANES):
            cols = slice(at, at + 2 * LANES)
            h_ref[rows, cols] = dot(left, sc_ref[:, cols], TN).astype(bf16)
        sums[1].to_sibling(chip).start()

    grads(0)
    grads(1)
    total.step(1)
    grads(2)
    grads(3)
    heads = HEADS // 4
    to = lax.broadcasted_iota(jnp.int32, (LANES, LANES), 0)
    source = lax.broadcasted_iota(jnp.int32, (LANES, LANES), 1)
    moved = jnp.where(jnp.logical_and(to == source + me * heads, source < heads), 1.0, 0.0).astype(bf16)
    both = d_ref[:, 2 * width : 2 * width + 2 * STATE]
    steps = d_ref[:, 2 * width + 2 * STATE :]
    for at in range(0, s_ref.shape[1], 2 * LANES):
        cols = slice(at, at + 2 * LANES)
        s_ref[: 2 * STATE, cols] = dot(both, x_ref[:, cols], TN).astype(bf16)
        s_ref[2 * STATE :, cols] = dot(moved, dot(steps, x_ref[:, cols], TN).astype(bf16)).astype(bf16)
    sums[2].start()
    if follows:
        total.step(2)
    for each in sums:
        each.cores()
    if follows:
        line_pass.turn(0)
        line_pass.between()
    for each in sums:
        each.join()
    if follows:
        line_pass.across()
        line_pass.turn(1)
        small.start()
    else:
        total.step(2)
    in_grad = sums[0].finish()
    for side in range(2):
        fresh = muon_decay * mi_ref[side] + in_grad[:, side * width : (side + 1) * width]
        ni_ref[side] = fresh
        slots_ref[side] = fresh.astype(bf16)
    fresh = muon_decay * mo_ref[...] + sums[1].finish()
    no_ref[...] = fresh
    slots_ref[2] = fresh.astype(bf16)
    os_ref[...] = sums[2].finish()
    if follows:
        line_pass.last()
        for time in range(1, 4):
            small.step(time)
        line_pass.finish()
        small.finish()
    else:
        total.step(3)
        total.own()
        total.finish()


def exchange(partial, gathered, d_all, d_rows, scaled_low, in_momentum, out_momentum, following=None):
    rows, width = out_momentum.shape
    if not kernels_fit():
        heads = HEADS // lax.axis_size("tensor")
        in_grad = dot(gathered, d_all[:, : 2 * width], TN).astype(bf16)
        out_grad = dot(d_rows, scaled_low, TN).astype(bf16)
        shared_grad = dot(d_all[:, 2 * width :], gathered, TN).astype(bf16)
        steps_grad = lax.dynamic_update_slice_in_dim(
            jnp.zeros((LANES, D), bf16),
            shared_grad[2 * STATE : 2 * STATE + heads],
            lax.axis_index("tensor") * heads,
            0,
        )
        shared_grad = jnp.concatenate([shared_grad[: 2 * STATE], steps_grad], 0)
        add = lambda v: lax.psum_scatter(v, "dp", scatter_dimension=0, tiled=True).astype(f32)
        in_sum = add(in_grad)
        in_new = muon_decay * in_momentum + jnp.stack([in_sum[:, :width], in_sum[:, width:]])
        out_new = muon_decay * out_momentum + add(out_grad)
        d_normed = lax.psum_scatter(partial, "tensor", scatter_dimension=0, tiled=True).astype(f32)
        results = (
            d_normed,
            in_new,
            out_new,
            jnp.concatenate([in_new, out_new[None]]).astype(bf16),
            add(shared_grad),
        )
        if following is None:
            return results
        layer_in, grad_resid, in_gain, branch, scale = following
        grad_resid, d_in_gain = input_step(d_normed, layer_in, grad_resid, in_gain)
        d_branch = grad_resid.astype(bf16)
        dots = jnp.sum(d_branch.astype(f32) * branch, -1)
        scalars = jnp.concatenate([scale[:1], jnp.broadcast_to(dots[None], (7, dots.shape[0]))])
        return (
            *results,
            grad_resid,
            d_in_gain,
            lax.all_gather(d_branch, "tensor", axis=0, tiled=True),
            lax.all_gather(scalars, "tensor", axis=0),
        )
    count, columns = partial.shape[0] // 4, partial.shape[1]
    vmem = pl.BlockSpec(memory_space=pltpu.VMEM)
    anywhere = pl.BlockSpec(memory_space=pl.ANY)
    fetched = (partial, gathered, d_all, d_rows, scaled_low)
    square = []
    shapes = ((D, 2 * width), (D, width), (SHARED_COLS, D))
    for tall, wide in shapes:
        square += [
            pltpu.VMEM((4, tall // 8, wide), bf16),
            pltpu.VMEM((tall // 8, wide), bf16),
            pltpu.VMEM((2, tall // 8, wide), bf16),
            pltpu.SemaphoreType.DMA((10,)),
            pltpu.SemaphoreType.DMA((10,)),
        ]
    line = pltpu.SemaphoreType.DMA((6,))
    out_shape = [
        jax.ShapeDtypeStruct((count, columns), f32),
        jax.ShapeDtypeStruct((2, rows, width), f32),
        jax.ShapeDtypeStruct((rows, width), f32),
        jax.ShapeDtypeStruct((3, rows, width), bf16),
        jax.ShapeDtypeStruct((SHARED_COLS // 8, D), f32),
    ]
    out_specs = [vmem] * 5
    if following is None:
        more = ()
        scratch = [pltpu.VMEM((6, count, columns), bf16), line, line]
    else:
        layer_in, grad_resid, in_gain, branch, scale = following
        more = (layer_in, grad_resid, jnp.broadcast_to(in_gain[None], (8, columns)), branch, scale)
        out_shape += [
            jax.ShapeDtypeStruct((count, columns), f32),
            jax.ShapeDtypeStruct((8, columns), f32),
            jax.ShapeDtypeStruct((4 * count, columns), bf16),
            jax.ShapeDtypeStruct((4, 8, count), f32),
        ]
        out_specs += [vmem, vmem, anywhere, vmem]
        scratch = [
            pltpu.VMEM((2, 6, count // 2, columns), bf16),
            pltpu.VMEM((count, columns), bf16),
            pltpu.VMEM((8, count), f32),
            pltpu.SemaphoreType.DMA,
            line,
            line,
            *pass_sems(),
        ]
    results = pl.pallas_call(
        functools.partial(exchange_kernel, follows=following is not None),
        out_shape=tuple(out_shape),
        in_specs=[anywhere] * 5 + [vmem] * (2 + len(more)),
        out_specs=tuple(out_specs),
        scratch_shapes=[
            *[pltpu.VMEM(each.shape, bf16) for each in fetched],
            *[pltpu.VMEM(shape, bf16) for shape in shapes],
            pltpu.SemaphoreType.DMA((5,)),
            *square,
            *scratch,
        ],
        compiler_params=pltpu.CompilerParams(
            collective_id=3 if following is None else 7, has_side_effects=True, vmem_limit_bytes=62 * 2**20
        ),
        cost_estimate=pl.CostEstimate(flops=10**10, bytes_accessed=150 * 2**20, transcendentals=0),
    )(*fetched, in_momentum, out_momentum, *more)
    if following is None:
        return results
    return (*results[:6], results[6][0], *results[7:])


def input_step(d_normed, layer_in, grad_resid, in_gain):
    inverse = lax.rsqrt(jnp.mean(layer_in * layer_in, -1, keepdims=True) + epsilon)
    scaled_in = layer_in * inverse
    d_in_gain = jnp.sum(d_normed * scaled_in, 0)
    d_scaled_in = d_normed * in_gain
    grad_resid = grad_resid + inverse * (
        d_scaled_in - scaled_in * jnp.mean(d_scaled_in * scaled_in, -1, keepdims=True)
    )
    return grad_resid, d_in_gain


def tail_kernel(
    s_ref,
    v_ref,
    b_ref,
    os_ref,
    ov_ref,
    t_ref,
    whole,
    low,
    next_low,
    shifted,
    mine,
    came,
    vsum,
    vcame,
    send_sem,
    recv_sem,
    small_send,
    small_recv,
    block_send,
    block_recv,
    block_local,
):
    me = lax.axis_index("tensor")
    index, core, sibling, by_x, by_y = neighbours()
    beside = me + 1 - 2 * lax.rem(me, 2)
    beyond = lax.rem(me + 2, 4)
    others_dp = [lax.rem(index + ahead, 8) for ahead in range(1, 8)]
    greet([{"tensor": beside}, {"tensor": beyond}, *[{"dp": other} for other in others_dp]])
    blocks, rows = b_ref.shape[0], b_ref.shape[1]

    def block_to(owner):
        return pltpu.make_async_remote_copy(
            src_ref=b_ref.at[owner],
            dst_ref=whole.at[index],
            send_sem=block_send.at[owner],
            recv_sem=block_recv.at[index],
            device_id={"dp": owner},
            device_id_type=MESH,
        )

    for owner in range(blocks):

        @pl.when(index != owner)
        def _(owner=owner):
            block_to(owner).start()

        @pl.when(index == owner)
        def _(owner=owner):
            pltpu.make_async_copy(b_ref.at[owner], whole.at[owner], block_local.at[0]).start()

    @pl.when(index >= blocks)
    def _():
        for place in range(8):
            pltpu.make_async_copy(b_ref.at[place % blocks], whole.at[place], block_local.at[place]).start()

    mine[0] = s_ref[...].astype(bf16)
    first = remote(mine.at[0], came.at[0], send_sem, recv_sem, 0, {"tensor": beside})
    first.start()
    first.wait()
    mine[1] = (mine[0].astype(f32) + came[0].astype(f32)).astype(bf16)
    second = remote(mine.at[1], came.at[1], send_sem, recv_sem, 1, {"tensor": beyond})
    second.start()
    second.wait()
    os_ref[index] = (mine[1].astype(f32) + came[1].astype(f32)).astype(bf16)

    for owner in range(blocks):

        @pl.when(index == owner)
        def _(owner=owner):
            pltpu.make_async_copy(b_ref.at[owner], whole.at[owner], block_local.at[0]).wait()

    for sender in range(8):

        @pl.when(jnp.logical_and(index < blocks, index != sender))
        def _(sender=sender):
            place = whole.at[sender]
            remote(place, place, block_send, block_recv, sender, {"dp": sibling}).wait_recv()

    @pl.when(index >= blocks)
    def _():
        for place in range(8):
            pltpu.make_async_copy(b_ref.at[place % blocks], whole.at[place], block_local.at[place]).wait()

    half = s_ref.shape[0] // 2
    near, far, everything = pl.ds(0, half), pl.ds(half, half), pl.ds(0, 2 * half)

    def send(owner, part, slot, where):
        place = os_ref.at[owner, part, :]
        copy = remote(place, place, send_sem, recv_sem, slot, {"dp": where})
        copy.start()
        return copy

    def small(source, target, slot, where):
        copy = remote(source, target, small_send, small_recv, slot, where)
        copy.start()
        return copy

    vsum[0] = v_ref[...]
    pending = small(vsum.at[0], vcame.at[0], 0, {"dp": sibling})
    copies = [
        send(index, near, 2, by_x),
        send(index, far, 3, by_y),
        send(index, far, 4, by_x),
        send(index, near, 5, by_y),
        send(index, everything, 8, sibling),
    ]
    squares = jnp.zeros((1, 1), f32)
    for at in range(8):
        part = whole[at].astype(f32)
        squares = squares + jnp.sum(part * part)
    scale = 1.0 / (jnp.sqrt(squares) + 1e-07)
    for at in range(0, 8, 2):
        part = jnp.concatenate([whole[at], whole[at + 1]], 0).astype(f32) * scale
        low[:, at * rows : (at + 2) * rows] = part.T.astype(bf16)
    chains = [(low, next_low, shifted)]
    advance(chains, 0)
    pending.wait()
    vsum[1] = vsum[0] + vcame[0]
    pending = small(vsum.at[1], vcame.at[1], 1, {"dp": by_x})
    copies[0].wait_recv()
    copies.append(send(by_x, near, 6, by_y))
    copies[1].wait_recv()
    copies.append(send(by_y, far, 7, by_x))
    advance(chains, 1)
    pending.wait()
    vsum[2] = vsum[1] + vcame[1]
    pending = small(vsum.at[2], vcame.at[2], 2, {"dp": by_y})
    copies[2].wait_recv()
    copies.append(send(by_x, everything, 9, sibling))
    copies[3].wait_recv()
    copies.append(send(by_y, everything, 10, sibling))
    advance(chains, 0)
    pending.wait()
    ov_ref[me] = vsum[2] + vcame[2]
    pending = small(ov_ref.at[me], ov_ref.at[me], 3, {"tensor": beside})
    copies[5].wait_recv()
    copies[6].wait_recv()
    copies.append(send(by_x + by_y - index, everything, 11, sibling))
    advance(chains, 1)
    pending.wait()
    base = pl.ds(2 * lax.div(me, 2), 2)
    pending = small(ov_ref.at[base], ov_ref.at[base], 4, {"tensor": beyond})
    advance(chains, 0)
    for at in range(0, 8, 2):
        t_ref[at * rows : (at + 2) * rows, :] = next_low[:, at * rows : (at + 2) * rows].astype(f32).T.astype(bf16)
    pending.wait()
    for at in (4, 7, 8, 9):
        copies[at].wait_recv()
    for copy in copies:
        copy.wait_send()
    for owner in range(blocks):

        @pl.when(index != owner)
        def _(owner=owner):
            block_to(owner).wait_send()


def finish_blocks(shard, vector, blocks):
    rows, width = blocks.shape[1:]
    if not kernels_fit():
        count = lax.axis_size("dp")
        total = lax.psum(shard, "tensor").astype(bf16)
        padded = jnp.pad(blocks, ((0, count - blocks.shape[0]), (0, 0), (0, 0)))
        whole = lax.all_to_all(padded, "dp", split_axis=0, concat_axis=0, tiled=True)
        return (
            lax.all_gather(total, "dp", axis=0),
            lax.all_gather(lax.psum(vector, "dp"), "tensor", axis=0),
            orthogonal(whole.reshape(D, width), bf16),
        )
    vmem = pl.BlockSpec(memory_space=pltpu.VMEM)
    anywhere = pl.BlockSpec(memory_space=pl.ANY)
    return pl.pallas_call(
        tail_kernel,
        out_shape=(
            jax.ShapeDtypeStruct((8, *shard.shape), bf16),
            jax.ShapeDtypeStruct((4, *vector.shape), f32),
            jax.ShapeDtypeStruct((D, width), bf16),
        ),
        in_specs=[vmem, vmem, anywhere],
        out_specs=(vmem, vmem, vmem),
        scratch_shapes=[
            pltpu.VMEM((8, rows, width), bf16),
            pltpu.VMEM((width, D), bf16),
            pltpu.VMEM((width, D), bf16),
            pltpu.VMEM((width, width), bf16),
            pltpu.VMEM((2, *shard.shape), bf16),
            pltpu.VMEM((2, *shard.shape), bf16),
            pltpu.VMEM((3, *vector.shape), f32),
            pltpu.VMEM((3, *vector.shape), f32),
            pltpu.SemaphoreType.DMA((12,)),
            pltpu.SemaphoreType.DMA((12,)),
            pltpu.SemaphoreType.DMA((5,)),
            pltpu.SemaphoreType.DMA((5,)),
            pltpu.SemaphoreType.DMA((8,)),
            pltpu.SemaphoreType.DMA((8,)),
            pltpu.SemaphoreType.DMA((8,)),
        ],
        compiler_params=pltpu.CompilerParams(
            collective_id=4, has_side_effects=True, vmem_limit_bytes=56 * 2**20
        ),
        cost_estimate=pl.CostEstimate(flops=2 * 10**10, bytes_accessed=100 * 2**20, transcendentals=0),
    )(shard, vector, blocks)


def advance(chains, flip):
    poly_zero = coef_first + coef_second + coef_third
    poly_one = coef_second + 2.0 * coef_third

    def unit(at, count, size):
        rows = lax.broadcasted_iota(jnp.int32, (count, size), 0) + at
        return jnp.where(rows == lax.broadcasted_iota(jnp.int32, (count, size), 1), 1.0, 0.0).astype(f32)

    for *buffers, shifted in chains:
        source = buffers[flip]
        size = source.shape[0]
        for at in range(0, size, 256):
            count = min(256, size - at)
            gram = dot(source[at : at + count, :], source[...], NT)
            shifted[at : at + count, :] = (gram - unit(at, count, size)).astype(bf16)
    for *buffers, shifted in chains:
        source, target = buffers[flip], buffers[1 - flip]
        size = source.shape[0]
        for at in range(0, size, 256):
            count = min(256, size - at)
            mine = shifted[at : at + count, :]
            poly = (
                poly_zero * unit(at, count, size)
                + poly_one * mine.astype(f32)
                + coef_third * dot(mine, shifted[...])
            )
            target[at : at + count, :] = dot(poly.astype(bf16), source[...]).astype(bf16)


def iterate(chains):
    def twice(_, carry):
        advance(chains, 0)
        advance(chains, 1)
        return carry

    lax.fori_loop(0, 2, twice, 0)
    advance(chains, 0)


def orthogonal_kernel(m_ref, o_ref, low, next_low, shifted):
    turned = m_ref[...].astype(f32).T
    scale = 1.0 / (jnp.sqrt(jnp.sum(turned * turned)) + 1e-07)
    low[...] = (turned * scale).astype(bf16)
    iterate([(low, next_low, shifted)])
    o_ref[...] = next_low[...].astype(f32).T.astype(o_ref.dtype)


def shared_step_kernel(m_ref, w_ref, o_ref, low, next_low, shifted):
    for layer in range(LAYERS):
        momentum = m_ref[layer]
        scale = 1.0 / (jnp.sqrt(jnp.sum(momentum * momentum)) + 1e-07)
        low[layer, :SSM_COLS, :] = (momentum * scale).astype(bf16)
        low[layer, SSM_COLS:, :] = jnp.zeros((low.shape[1] - SSM_COLS, D), bf16)
    iterate([(low.at[layer], next_low.at[layer], shifted.at[layer]) for layer in range(LAYERS)])
    rate = muon_rate * (D / SSM_COLS) ** 0.5
    for layer in range(LAYERS):
        o_ref[layer] = w_ref[layer].astype(f32) - rate * next_low[layer, :SSM_COLS, :].astype(f32)


def shared_step(momentum, weight):
    vmem = pl.BlockSpec(memory_space=pltpu.VMEM)
    padded = -(-SSM_COLS // LANES) * LANES
    return pl.pallas_call(
        shared_step_kernel,
        out_shape=jax.ShapeDtypeStruct(momentum.shape, f32),
        in_specs=[vmem, vmem],
        out_specs=vmem,
        scratch_shapes=[
            pltpu.VMEM((LAYERS, padded, D), bf16),
            pltpu.VMEM((LAYERS, padded, D), bf16),
            pltpu.VMEM((LAYERS, padded, padded), bf16),
        ],
        compiler_params=pltpu.CompilerParams(vmem_limit_bytes=56 * 2**20),
        cost_estimate=pl.CostEstimate(
            flops=20 * padded * padded * (2 * D + padded), bytes_accessed=12 * D * padded, transcendentals=0
        ),
    )(momentum, weight)


def orthogonal(matrix, dtype):
    length, size = matrix.shape
    vmem = pl.BlockSpec(memory_space=pltpu.VMEM)
    return pl.pallas_call(
        orthogonal_kernel,
        out_shape=jax.ShapeDtypeStruct((length, size), dtype),
        in_specs=[vmem],
        out_specs=vmem,
        scratch_shapes=[
            pltpu.VMEM((size, length), bf16),
            pltpu.VMEM((size, length), bf16),
            pltpu.VMEM((size, size), bf16),
        ],
        compiler_params=pltpu.CompilerParams(vmem_limit_bytes=56 * 2**20),
        cost_estimate=pl.CostEstimate(
            flops=10 * size * size * (2 * length + size), bytes_accessed=6 * size * length, transcendentals=0
        ),
    )(matrix)


def body(
    resid_in,
    in_weight,
    out_weight,
    shared_weight,
    small_params,
    in_momentum,
    out_momentum,
    shared_momentum,
    small_first,
    small_second,
    resid_grad,
):
    tensor_index = lax.axis_index("tensor")
    tensor_count = lax.axis_size("tensor")
    local_cols = in_weight.shape[3]
    local_heads = HEADS // tensor_count
    col_start = tensor_index * local_cols
    head_start = tensor_index * local_heads
    shard_rows = in_weight.shape[1]
    own_tokens = resid_in.shape[0]
    length = own_tokens * tensor_count

    row_start = lax.axis_index("dp") * shard_rows
    channels = small_params[:, : (KERNEL + 2) * INNER].reshape(LAYERS, KERNEL + 2, INNER)
    channels = lax.dynamic_slice_in_dim(channels, col_start, local_cols, 2)
    states_at = (KERNEL + 2) * INNER
    heads_at = states_at + (KERNEL + 1) * 2 * STATE
    by_state = small_params[:, states_at:heads_at].reshape(LAYERS, KERNEL + 1, 2 * STATE)
    by_head = small_params[:, heads_at : heads_at + 3 * HEADS].reshape(LAYERS, 3, HEADS)
    by_head = lax.dynamic_slice_in_dim(by_head, head_start, local_heads, 2)
    in_gains = small_params[:, heads_at + 3 * HEADS :]
    skips = jnp.repeat(by_head[:, 2:], WIDTH, axis=2)
    px_all = jnp.concatenate([channels, skips, jnp.zeros((LAYERS, 1, local_cols), f32)], 1)
    ps_all = jnp.pad(by_state, ((0, 0), (0, 8 - KERNEL - 1), (0, 0)))
    ph_all = jnp.pad(by_head[:, :2], ((0, 0), (0, 6), (0, LANES - local_heads)))

    w_in, w_out = [], []
    for layer in range(LAYERS):
        shared_rows = lax.dynamic_slice_in_dim(shared_weight[layer], row_start, shard_rows, 0)
        steps_weight = lax.dynamic_slice_in_dim(shared_rows, 2 * STATE + head_start, local_heads, 1)
        w_rows = jnp.concatenate(
            [
                in_weight[layer, :, 0],
                in_weight[layer, :, 1],
                shared_rows[:, : 2 * STATE],
                jnp.pad(steps_weight, ((0, 0), (0, LANES - local_heads))),
            ],
            1,
        )
        w_in.append(w_rows)
        w_out.append(out_weight[layer])
    in_momentum_planes = jnp.transpose(in_momentum, (0, 2, 1, 3))

    residual = resid_in
    inverse_in = lax.rsqrt(jnp.mean(residual * residual, -1, keepdims=True) + epsilon)
    normed_low = (residual * inverse_in * in_gains[0]).astype(bf16)
    gathered, w_in[0], w_out[0] = gather_first(normed_low, w_in[0], w_out[0])
    held = lax.optimization_barrier((gathered, *w_in[1:], *w_out[1:]))
    gathered = held[0]
    for later in range(1, LAYERS):
        w_in[later] = lax.all_gather(held[later], "dp", axis=0, tiled=True)
        w_out[later] = lax.all_gather(held[LAYERS - 1 + later], "dp", axis=0, tiled=True)
    saved = []
    branches = [None] * LAYERS
    for layer in range(LAYERS):
        projected, total, partial, squares, states = mixer_forward(
            gathered, w_in[layer], w_out[layer], px_all[layer], ps_all[layer], ph_all[layer]
        )
        saved.append((residual, gathered, projected, total, states))
        squares = squares[:, 0, :].reshape(tensor_count, 1, own_tokens)
        squares = jnp.broadcast_to(squares, (tensor_count, 8, own_tokens))
        if layer < LAYERS - 1:
            residual, branch, scale, gathered = forward_pass(partial, squares, residual, in_gains[layer + 1])
            branches[layer] = (branch, scale)
    summed, square_sum, d_rows, rd = scatter_tokens(partial, squares, resid_grad.astype(bf16))
    residual = residual + summed * lax.rsqrt(square_sum[0] / INNER + epsilon)[:, None]

    grad_resid = resid_grad
    in_new = [None] * LAYERS
    out_new = [None] * LAYERS
    slots = [None] * LAYERS
    shared_shards = [None] * LAYERS
    small_grads = [None] * LAYERS
    for layer in reversed(range(LAYERS)):
        layer_in, gathered, projected, total, states = saved[layer]
        rd = jnp.transpose(rd[:, :2], (0, 2, 1)).reshape(length, 2)
        d_all, scaled_low, partial, grad_x, grad_s, grad_h = mixer_backward(
            d_rows, w_in[layer], w_out[layer], projected, total, states, rd, px_all[layer], ps_all[layer], ph_all[layer]
        )
        following = None
        if layer > 0:
            following = (layer_in, grad_resid, in_gains[layer], *branches[layer - 1])
        results = exchange(
            partial, gathered, d_all, d_rows, scaled_low, in_momentum_planes[layer], out_momentum[layer], following
        )
        d_normed, in_new[layer], out_new[layer], slots[layer], shared_shards[layer] = results[:5]
        if layer > 0:
            grad_resid, d_in_gain, d_rows, rd = results[5:]
        else:
            grad_resid, d_in_gain = input_step(d_normed, layer_in, grad_resid, in_gains[layer])
        small_grads[layer] = jnp.concatenate([grad_x, grad_s, grad_h, d_in_gain.reshape(8, D // 8)], 1)

    in_momentum_new = jnp.transpose(jnp.stack(in_new), (0, 2, 1, 3))
    out_momentum_new = jnp.stack(out_new)
    block_count = 3 * LAYERS
    dp_count = lax.axis_size("dp")
    shared_total, vectors, turned = finish_blocks(
        jnp.concatenate(shared_shards, 0), jnp.concatenate(small_grads, 1), jnp.concatenate(slots, 0)
    )
    turned = turned.reshape(dp_count, shard_rows, local_cols)
    returned = lax.all_to_all(turned, "dp", split_axis=0, concat_axis=0, tiled=True)[:block_count]
    scale = muon_rate * (D / local_cols) ** 0.5
    updates = returned.astype(f32).reshape(LAYERS, 3, shard_rows, local_cols) * scale
    in_weight_new = in_weight.astype(f32) - jnp.transpose(updates[:, :2], (0, 2, 1, 3))
    out_weight_new = out_weight.astype(f32) - updates[:, 2]

    share = SHARED_COLS // dp_count
    shared_total = shared_total.reshape(dp_count, LAYERS, share, D)
    shared_total = jnp.transpose(shared_total, (1, 0, 2, 3)).reshape(LAYERS, SHARED_COLS, D)[:, :SSM_COLS]
    turned_momentum = muon_decay * jnp.transpose(shared_momentum, (0, 2, 1)) + shared_total.astype(f32)
    shared_momentum_new = jnp.transpose(turned_momentum, (0, 2, 1))
    shared_weight_new = jnp.transpose(
        shared_step(turned_momentum, jnp.transpose(shared_weight, (0, 2, 1))), (0, 2, 1)
    )
    small_rows = []
    for layer in range(LAYERS):
        width = local_cols + 2 * STATE + LANES + D // 8
        mine = vectors[:, :, layer * width : (layer + 1) * width]
        channel_grads = jnp.transpose(mine[:, :7, :local_cols], (1, 0, 2)).reshape(7, INNER)
        head_grads = jnp.transpose(mine[:, :2, local_cols + 2 * STATE :][:, :, :local_heads], (1, 0, 2))
        common = jnp.sum(mine, 0)
        state_grads = common[: KERNEL + 1, local_cols : local_cols + 2 * STATE]
        small_rows.append(
            jnp.concatenate(
                [
                    channel_grads[: KERNEL + 2].reshape(-1),
                    state_grads.reshape(-1),
                    head_grads.reshape(-1),
                    channel_grads[6].reshape(HEADS, WIDTH).sum(1),
                    common[:, local_cols + 2 * STATE + LANES :].reshape(-1),
                ]
            )
        )
    small_grad = jnp.stack(small_rows)
    first_new = beta_first * small_first + (1.0 - beta_first) * small_grad
    small_second_new = beta_second * small_second + (1.0 - beta_second) * small_grad * small_grad
    small_new = small_params - adam_rate * (first_new / (1.0 - beta_first**STEP)) / (
        jnp.sqrt(small_second_new / (1.0 - beta_second**STEP)) + 1e-08
    )
    return (
        residual,
        grad_resid,
        small_grad,
        small_second_new,
        small_new,
        in_momentum_new,
        in_weight_new,
        out_momentum_new,
        out_weight_new,
        shared_momentum_new,
        shared_weight_new,
    )


def solution(mesh):
    placed = (
        P(("dp", "tensor"), None),
        P(None, "dp", None, "tensor"),
        P(None, "dp", "tensor"),
        P(),
        P(),
        P(None, "dp", None, "tensor"),
        P(None, "dp", "tensor"),
        P(),
        P(),
        P(),
        P(("dp", "tensor"), None),
    )
    return jax.shard_map(
        body,
        mesh=mesh,
        in_specs=placed,
        out_specs=(
            P(("dp", "tensor"), None),
            P(("dp", "tensor"), None),
            P(),
            P(),
            P(),
            P(None, "dp", None, "tensor"),
            P(None, "dp", None, "tensor"),
            P(None, "dp", "tensor"),
            P(None, "dp", "tensor"),
            P(),
            P(),
        ),
        check_vma=False,
    )
```

time: 2390 us -> 720 us (0.30)
  waiting for transfers between devices: 915 us -> 0.72 us
  Pallas kernels: 0 us -> 625 us
  matrix products: 580 us -> 0 us
  local copies, waits for them, and re-layouts: 568 us -> 39.3 us
  other arithmetic: 242 us -> 27.3 us
  blocking collectives: 39.6 us -> 0 us
    pallas_call x0 -> x11, Pallas kernels: none -> 625 us  [the longest x2 176 us: exchange(): pl.pallas_call(functools.partial(exchange_kernel, follows=following is no...]
    dot_general x167 -> x0, matrix products: 573 us -> none  [the longest x15 123 us: orthogonal(): current = coef_first * current + jnp.dot(poly, current, precision=highest)]
    reduce_scatter x6 -> x0, waiting for transfers between devices: 505 us -> none  [the longest x2 217 us: body(): lax.psum_scatter(lax.dot_general(scaled_low, w_out, (((1,), (1,)), ((), (...]
    dynamic_update_slice x74 -> x0, local copies, waits for them, and re-layouts: 325 us -> none  [the longest x64 323 us: mixer_core(): last_state, outputs = lax.scan(jax.checkpoint(span_step), initial, pieces)]
    all_gather x8 -> x2, waiting for transfers between devices: 250 us -> 0.01 us  [the longest x1 0.01 us: body(): lax.all_gather(held[LAYERS - 1 + later], 'dp', axis=0, tiled=True)]
    psum x1 -> x0, waiting for transfers between devices: 145 us -> none  [body(): lax.psum((jnp.stack(shared_grads), jnp.stack(small_grads)), ('dp', 'tenso...]
    reduce_sum x32 -> x4, other arithmetic: 80 us -> 3.34 us  [the longest x1 1.99 us: input_step(): d_in_gain = jnp.sum(d_normed * scaled_in, 0)]
    another operation x88 -> x1, other arithmetic: 60.6 us -> 1.09 us  [body(): out_momentum_new = jnp.stack(out_new)]
  transfers between devices with their start and end apart: 17 -> 3, of which waited for: 13 -> 0; matrix products, arithmetic and copies ran while one was open for 22% -> 3% of each run, Pallas kernels for 0% -> 21%
where the time goes in v1:
time: 720 us; the launch traced here: 712 us
  Pallas kernels  625 us (87%)
  local copies, waits for them, and re-layouts  39.3 us (5%)
  other arithmetic  27.3 us (4%)
  between operations  14.9 us (2%)
    pallas_call x2, Pallas kernels, exchange(): pl.pallas_call(functools.partial(exchange_kernel, follows=following is no...  176 us
    pallas_call x1, Pallas kernels, forward_pass(): pl.pallas_call(forward_pass_kernel, out_shape=(jax.ShapeDtypeStruct((coun...  97 us
    pallas_call x2, Pallas kernels, mixer_backward(): pl.pallas_call(backward_kernel, grid=(spans,), in_specs=[pl.BlockSpec((SP...  78.3 us
    pallas_call x1, Pallas kernels, scatter_tokens(): pl.pallas_call(scatter_kernel, out_shape=(jax.ShapeDtypeStruct((count, co...  73.3 us
    pallas_call x1, Pallas kernels, gather_first(): pl.pallas_call(first_kernel, out_shape=(larger(rows, 4), larger(w_rows, 8...  61.7 us
    pallas_call x1, Pallas kernels, finish_blocks(): pl.pallas_call(tail_kernel, out_shape=(jax.ShapeDtypeStruct((8, *shard.sh...  60.4 us
    pallas_call x2, Pallas kernels, mixer_forward(): pl.pallas_call(forward_kernel, grid=(spans,), in_specs=[pl.BlockSpec((SPA...  54.2 us
    pallas_call x1, Pallas kernels, shared_step(): pl.pallas_call(shared_step_kernel, out_shape=jax.ShapeDtypeStruct(momentu...  23.6 us
  transfers between devices with their start and end apart: 3, of which 0 were waited for; matrix products, arithmetic and copies ran while one was open for 3% of the time, Pallas kernels for 21%

profile of v1, /device:TPU:0, one launch (start us, length us, event | category | flops | bytes accessed | tf_op | source)
XLA Modules:
  0.0 712.1 jit_solution(13677797068383873916)
XLA Ops:
  9.7 1.7 fusion.12
  17.0 61.7 %shard_map.194 = (bf16[1024,1536]{1,0:T(8,128)(2,1)}, bf16[1536,1920]{1,0:T(8,128)(2,1)}, bf16[1536,768]{1,0:T(8,128)(2,1)}) custom-call(bf16[256,1536]{1,0:T(8,128)(2,1)} %multiply_convert_fusion.x_ref, bf16[192,1920]{1,0:T(8,128)(2,1)} %fusion.4.w_ref, bf16[192,768]{1,0:T(8,128)(2,1)} %get-tuple-element.157.v_ref), custom_call_target="tpu_custom_call" | custom-call | bytes 157286400 | tf_op jit(solution)/shard_map/pallas_call | solution.py:646
  83.0 27.3 %shard_map.195 = (f32[1024,1920]{1,0:T(8,128)}, f32[1024,768]{1,0:T(8,128)}, bf16[1024,1536]{1,0:T(8,128)(2,1)}, f32[4,8,256]{2,1,0:T(8,128)}, bf16[4,128,768]{2,1,0:T(8,128)(2,1)}) custom-call(bf16[1024,1536]{1,0:T(8,128)(2,1)} %get-tuple-element.64.g_ref.x_any, bf16[1536,1920]{1,0:T(8,128)(2,1)} %get-tuple-element.65.w_ref, ...), custom_call_target="tpu_custom_call" | custom-call | flops 10000000000 | bytes 33554432 | tf_op jit(solution)/shard_map/pallas_call | solution.py:347
  113.9 97.0 %shard_map.196 = (f32[256,1536]{1,0:T(8,128)S(1)}, f32[256,1536]{1,0:T(8,128)S(1)}, f32[8,256]{1,0:T(8,128)S(1)}, bf16[1024,1536]{1,0:T(8,128)(2,1)S(1)}) custom-call(bf16[1024,1536]{1,0:T(8,128)(2,1)S(1)} %copy-done.1, f32[4,8,256]{2,1,0:T(8,128)S(1)} %broadcast_in_dim.40.q_ref, f32[256,1536]{1,0:T(8,128)S(1)} %copy-done, ...), custom_call_target="tpu_custom_call" | custom-call | bytes 262144000 | tf_op jit(solution)/shard_map/pallas_call | solution.py:876
  216.8 26.9 %shard_map.197 = (f32[1024,1920]{1,0:T(8,128)}, f32[1024,768]{1,0:T(8,128)}, bf16[1024,1536]{1,0:T(8,128)(2,1)}, f32[4,8,256]{2,1,0:T(8,128)}, bf16[4,128,768]{2,1,0:T(8,128)(2,1)}) custom-call(bf16[1024,1536]{1,0:T(8,128)(2,1)} %copy-done.7, bf16[1536,1920]{1,0:T(8,128)(2,1)} %all-gather.3.cloned.1.call-done.w_ref, ...), custom_call_target="tpu_custom_call" | custom-call | flops 10000000000 | bytes 33554432 | tf_op jit(solution)/shard_map/pallas_call | solution.py:347
  244.5 1.9 copy-done.2
  246.4 73.3 %shard_map.198 = (f32[256,1536]{1,0:T(8,128)S(1)}, f32[8,256]{1,0:T(8,128)S(1)}, bf16[1024,1536]{1,0:T(8,128)(2,1)S(1)}, f32[4,8,256]{2,1,0:T(8,128)S(1)}) custom-call(bf16[1024,1536]{1,0:T(8,128)(2,1)S(1)} %copy-done.2, f32[4,8,256]{2,1,0:T(8,128)S(1)} %broadcast_in_dim.44.q_ref, bf16[256,1536]{1,0:T(8,128)(2,1)S(1)} %convert_element_type.26.x_ref), custom_call_target="tpu_custom_call" | custom-call | bytes 157286400 | tf_op jit(solution)/shard_map/pallas_call | solution.py:984
  320.8 1.7 copy-done.8
  323.5 38.9 %shard_map.199 = (bf16[1024,1920]{1,0:T(8,128)(2,1)}, bf16[1024,768]{1,0:T(8,128)(2,1)}, bf16[1024,1536]{1,0:T(8,128)(2,1)}, f32[8,768]{1,0:T(8,128)}, f32[8,256]{1,0:T(8,128)}, /*index=5*/f32[8,128]{1,0:T(8,128)}) custom-call(bf16[1024,1536]{1,0:T(8,128)(2,1)} %copy-done.8, bf16[1536,1920]{1,0:T(8,128)(2,1)} %all-gather.3.cloned.1.call-done.w_ref, ...), custom_call_target="tpu_custom_call" | custom-call | flops 16000000000 | bytes 50331648 | tf_op jit(solution)/shard_map/pallas_call | solution.py:391
  362.5 103.1 %shard_map.200 = (f32[256,1536]{1,0:T(8,128)}, f32[2,192,768]{2,1,0:T(8,128)}, f32[192,768]{1,0:T(8,128)}, bf16[3,192,768]{2,1,0:T(8,128)(2,1)}, f32[48,1536]{1,...) custom-call(bf16[1024,1536]{1,0:T(8,128)(2,1)} %get-tuple-element.82.p_, ...), custom_call_target="tpu_custom_call" | custom-call | flops 10000000000 | bytes 157286400 | tf_op jit(solution)/shard_map/pallas_call | solution.py:1311
  467.3 39.3 %shard_map.201 = (bf16[1024,1920]{1,0:T(8,128)(2,1)}, bf16[1024,768]{1,0:T(8,128)(2,1)}, bf16[1024,1536]{1,0:T(8,128)(2,1)}, f32[8,768]{1,0:T(8,128)}, f32[8,256]{1,0:T(8,128)}, /*index=5*/f32[8,128]{1,0:T(8,128)}) custom-call(bf16[1024,1536]{1,0:T(8,128)(2,1)} %get-tuple-element.88.dr_ref.dr_any, bf16[1536,1920]{1,0:T(8,128)(2,1)} %get-tuple-element.65.w_ref, ...), custom_call_target="tpu_custom_call" | custom-call | flops 16000000000 | bytes 50331648 | tf_op jit(solution)/shard_map/pallas_call | solution.py:391
  506.7 73.4 %shard_map.202 = (f32[256,1536]{1,0:T(8,128)}, f32[2,192,768]{2,1,0:T(8,128)}, f32[192,768]{1,0:T(8,128)}, bf16[3,192,768]{2,1,0:T(8,128)(2,1)}, f32[48,1536]{1,0:T(8,128)}) custom-call(bf16[1024,1536]{1,0:T(8,128)(2,1)} %get-tuple-element.93.p_any, bf16[1024,1536]{1,0:T(8,128)(2,1)} %get-tuple-element.64.g_ref.x_any, ...), custom_call_target="tpu_custom_call" | custom-call | flops 10000000000 | bytes 157286400 | tf_op jit(solution)/shard_map/pallas_call | solution.py:1311
  580.1 2.0 multiply_reduce_fusion
  584.0 2.6 pad_maximum_fusion.b_ref
  587.3 60.4 %shard_map.203 = (bf16[8,96,1536]{2,1,0:T(8,128)(2,1)}, f32[4,8,2688]{2,1,0:T(8,128)}, bf16[1536,768]{1,0:T(8,128)(2,1)}) custom-call(f32[96,1536]{1,0:T(8,128)} %pad_maximum_fusion.2.s_ref, f32[8,2688]{1,0:T(8,128)} %concatenate.28.v_ref, bf16[6,192,768]{2,1,0:T(8,128)(2,1)} %pad_maximum_fusion.b_ref), custom_call_target="tpu_custom_call" | custom-call | flops 20000000000 | bytes 104857600 | tf_op jit(solution)/shard_map/pallas_call | solution.py:1516
  651.8 4.8 all-to-all-start
  656.6 3.5 multiply_add_fusion
  660.3 2.3 divide_subtract_fusion
  662.7 2.9 multiply_add_fusion.1
  665.8 3.2 copy.57
  671.7 2.5 bitcast_add_fusion.m_ref
  674.1 23.6 %shard_map.204 = f32[2,304,1536]{2,1,0:T(8,128)} custom-call(f32[2,304,1536]{2,1,0:T(8,128)} %bitcast_add_fusion.m_ref, bf16[2,304,1536]{2,1,0:T(8,128)(2,1)} %bitcast.98), custom_call_target="tpu_custom_call" | custom-call | flops 10192158720 | bytes 7077888 | tf_op jit(solution)/shard_map/pallas_call | solution.py:1611
  697.8 1.9 convert_multiply_fusion
  701.9 3.2 copy.58
  (165 shorter events, 38.0 us)
Async XLA Ops:
  7.2 209.6 %all-gather.5.cloned.1.call-start = ((), (), s32[]{:S(2)}) async-start(), calls=%async_computation.2 | async-start | bytes 2654208 | tf_op jit(solution)/shard_map/all_gather | solution.py:1710
  9.7 2.9 copy-start.11
  79.7 137.1 %all-gather.3.cloned.1.call-start = ((), (), s32[]{:S(2)}) async-start(), calls=%async_computation.1 | async-start | bytes 6635520 | tf_op jit(solution)/shard_map/all_gather | solution.py:1709
  83.0 28.2 %copy-start.18 = (f32[256,1536]{1,0:T(8,128)S(1)}, f32[256,1536]{1,0:T(8,128)}, u32[]{:S(2)}) copy-start(f32[256,1536]{1,0:T(8,128)} %refs_1_.1) | copy-start | bytes 4718596
  113.9 97.0 %copy-start.6 = (f32[8,1536]{1,0:T(8,128)}, f32[8,1536]{1,0:T(8,128)S(1)}, u32[]{:S(2)}) copy-start(f32[8,1536]{1,0:T(8,128)S(1)} %broadcast_in_dim.42.gain_ref.refs_2_) | copy-start | bytes 147460
  113.9 99.8 %copy-start.19 = (f32[2,192,768]{2,1,0:T(8,128)S(1)}, f32[2,192,768]{2,1,0:T(8,128)}, u32[]{:S(2)}) copy-start(f32[2,192,768]{2,1,0:T(8,128)} %param.17) | copy-start | bytes 3538948
  213.7 3.1 copy-start.10
  580.1 3.0 copy-start.27
  580.1 3.0 copy-start.28
  580.1 3.8 copy-start.22
  584.0 2.6 copy-start.29
  584.0 2.6 copy-start.30
  584.0 2.6 copy-start.31
  584.0 2.6 copy-start.32
  584.0 2.6 copy-start.33
  584.0 2.6 copy-start.34
  651.8 46.0 %all-to-all-start = ((bf16[8,192,768]{2,1,0:T(8,128)(2,1)}), bf16[8,192,768]{2,1,0:T(8,128)(2,1)}, u32[]{:S(2)}, u32[]{:S(2)}) async-start(bf16[8,192,768]{2,1,0:T(8,128)(2,1)} %bitcast.96), calls=%async_computation | async-start | bytes 4718592 | tf_op jit(solution)/shard_map/all_to_all | solution.py:1759
  656.6 3.7 copy-start.23
  656.6 6.1 copy-start.4
  662.7 2.9 copy-start.20
  662.7 2.9 copy-start.21
  665.8 3.2 copy-start.15
  665.8 3.4 copy-start.26
  669.1 2.6 copy-start.13
  (17 other events, 27.9 us)
Sparse Core Ops, SparseCore 0:
  79.8 27.2 all-gather.4
  109.6 43.8 all-gather.2

commit v2 on v1

--- a/solution.py
+++ b/solution.py
@@ -70,8 +70,12 @@
     return raw, timestep, decay, log_decay, cumulative, lower
 
 
-def pair_of(table, pair, low_half):
-    return jnp.where(low_half, table[:, 2 * pair : 2 * pair + 1], table[:, 2 * pair + 1 : 2 * pair + 2])
+def spread_heads(table, columns):
+    high = table.astype(bf16)
+    low = (table - high.astype(f32)).astype(bf16)
+    head = lax.rem(lax.broadcasted_iota(jnp.int32, (2 * LANES, columns), 0), LANES)
+    owned = head == lax.broadcasted_iota(jnp.int32, (2 * LANES, columns), 1) // WIDTH
+    return dot(jnp.concatenate([high, low], 1), jnp.where(owned, 1.0, 0.0).astype(bf16))
 
 
 def conv_of(pad, lanes, weights, first):
@@ -124,6 +128,7 @@
     grown = jnp.exp(cumulative)
     tail = jnp.exp(cumulative[SPAN - 1 : SPAN, :] - cumulative)
     scores = dot(c_low, b_low, NT) * lower
+    wide_step, wide_grown, wide_tail = (spread_heads(each, columns) for each in (timestep, grown, tail))
     low_half = lax.broadcasted_iota(jnp.int32, (SPAN, LANES), 1) < WIDTH
     squares = jnp.zeros((SPAN, LANES), f32)
     half = SPAN // 2
@@ -131,24 +136,23 @@
         lanes = slice(pair * LANES, (pair + 1) * LANES)
         pre = conv_of(xpad, lanes, px_ref, first)
         xc = pre * sigmoid(pre)
-        u = xc * pair_of(timestep, pair, low_half)
+        u = xc * wide_step[:, lanes]
         u_low = u.astype(bf16)
         mine = [jnp.where(low_half == (side == 0), u_low, jnp.zeros_like(u_low)) for side in range(2)]
         inside = []
         for rows, count in ((slice(0, half), half), (slice(half, SPAN), SPAN)):
-            both = jnp.zeros((half, LANES), f32)
+            mixing = []
             for side in range(2):
                 head = 2 * pair + side
                 spread = cumulative[rows, head : head + 1] - turned[head : head + 1, :count]
-                mixing = (scores[rows, :count] * jnp.exp(jnp.minimum(spread, 0.0))).astype(bf16)
-                both = both + dot(mixing, mine[side][:count])
-            inside.append(both)
+                mixing.append((scores[rows, :count] * jnp.exp(jnp.minimum(spread, 0.0))).astype(bf16))
+            inside.append(dot(jnp.concatenate(mixing, 1), jnp.concatenate([mine[0][:count], mine[1][:count]], 0)))
         held = state[:, lanes]
         held_low = held.astype(bf16)
         st_ref[0, :, lanes] = held_low
-        grown_pair = pair_of(grown, pair, low_half)
+        grown_pair = wide_grown[:, lanes]
         carried = dot(c_low, held_low) * grown_pair
-        tail_u = (pair_of(tail, pair, low_half) * u).astype(bf16)
+        tail_u = (wide_tail[:, lanes] * u).astype(bf16)
         state[:, lanes] = grown_pair[SPAN - 1 : SPAN, :] * held + dot(b_low, tail_u, TN)
         total = jnp.concatenate(inside, 0) + carried + px_ref[6:7, lanes] * xc
         yt_ref[:, lanes] = total
@@ -224,6 +228,7 @@
     tail = jnp.exp(cumulative[SPAN - 1 : SPAN, :] - cumulative)
     upper = lower.T
     scores = dot(b_low, c_low, NT) * upper
+    wide_step, wide_grown, wide_tail = (spread_heads(each, columns) for each in (timestep, grown, tail))
     low_half = lax.broadcasted_iota(jnp.int32, (SPAN, LANES), 1) < WIDTH
     inverse = rd_ref[:, 0:1]
     dots = rd_ref[:, 1:2] * (1.0 / INNER)
@@ -243,7 +248,7 @@
         pre = conv_of(xpad, lanes, px_ref, first)
         sig = sigmoid(pre)
         xc = pre * sig
-        step_pair = pair_of(timestep, pair, low_half)
+        step_pair = wide_step[:, lanes]
         u = xc * step_pair
         u_low = u.astype(bf16)
         gate = gate_ref[:, lanes]
@@ -267,23 +272,22 @@
         du = []
         for block, start in ((0, 0), (1, half)):
             rows = slice(start, start + half)
-            both = jnp.zeros((half, LANES), f32)
+            mixing = []
             for side in range(2):
                 head = 2 * pair + side
                 spread = turned[head : head + 1, start:] - cumulative[rows, head : head + 1]
                 mask = jnp.exp(jnp.minimum(spread, 0.0))
-                mixing = (scores[rows, start:] * mask).astype(bf16)
-                both = both + dot(mixing, mine[side][start:])
+                mixing.append((scores[rows, start:] * mask).astype(bf16))
                 d_scores[block] = d_scores[block] + dot(u_low[rows], mine[side][start:], NT) * mask
-            du.append(both)
+            du.append(dot(jnp.concatenate(mixing, 1), jnp.concatenate([mine[0][start:], mine[1][start:]], 0)))
         held_low = st_ref[0, :, lanes]
-        grown_pair = pair_of(grown, pair, low_half)
+        grown_pair = wide_grown[:, lanes]
         last_pair = grown_pair[SPAN - 1 : SPAN, :]
         d_after = dstate[:, lanes]
         d_after_low = d_after.astype(bf16)
         grown_dy = (grown_pair * dy).astype(bf16)
         d_c = d_c + dot(grown_dy, held_low, NT)
-        tail_pair = pair_of(tail, pair, low_half)
+        tail_pair = wide_tail[:, lanes]
         du_tail = tail_pair * dot(b_low, d_after_low)
         d_b = d_b + dot((tail_pair * u).astype(bf16), d_after_low, NT)
         dstate[:, lanes] = last_pair * d_after + dot(c_low, grown_dy, TN)
@@ -864,8 +868,7 @@
 def forward_pass(partial, squares, residual, in_gain):
     count, columns = residual.shape
     if not kernels_fit():
-        summed, side = scatter_tokens(partial, squares)
-        scale = lax.rsqrt(side / INNER + epsilon)
+        summed, scale = plain_scatter(partial, squares)
         branch = summed * scale[0][:, None]
         fresh = residual + branch
         inverse = lax.rsqrt(jnp.mean(fresh * fresh, -1, keepdims=True) + epsilon)
@@ -904,10 +907,12 @@
     p_ref,
     q_ref,
     x_ref,
+    r_ref,
+    or_ref,
+    ox_ref,
+    rd_ref,
     o_ref,
     oq_ref,
-    ox_ref,
-    rd_ref,
     came,
     came_q,
     send_sem,
@@ -954,6 +959,7 @@
     copies.append(pltpu.make_async_copy(scalars, rd_ref.at[me], rd_local))
     for copy in copies:
         copy.start()
+    or_ref[...] = r_ref[...] + o_ref[...] * column_of(inverse[0:1, :], rows)
     for stream in streams:
         stream.finish()
     for copy in small:
@@ -962,19 +968,20 @@
         copy.wait()
 
 
-def scatter_tokens(partial, extra, rows=None):
+def plain_scatter(partial, extra):
+    total = lax.psum_scatter(partial, "tensor", scatter_dimension=0, tiled=True).astype(f32)
+    flat = jnp.transpose(extra, (0, 2, 1)).reshape(partial.shape[0], 8)
+    side = lax.psum_scatter(flat, "tensor", scatter_dimension=0, tiled=True).T
+    return total, lax.rsqrt(side / INNER + epsilon)
+
+
+def last_scatter(partial, extra, rows, residual):
     if not kernels_fit():
-        total = lax.psum_scatter(partial, "tensor", scatter_dimension=0, tiled=True).astype(f32)
-        flat = jnp.transpose(extra, (0, 2, 1)).reshape(partial.shape[0], 8)
-        side = lax.psum_scatter(flat, "tensor", scatter_dimension=0, tiled=True).T
-        if rows is None:
-            return total, side
-        inverse = lax.rsqrt(side / INNER + epsilon)
+        total, inverse = plain_scatter(partial, extra)
         dots = jnp.sum(rows.astype(f32) * total, -1)[None] * inverse
         scalars = jnp.concatenate([inverse[:1], dots[1:]])
         return (
-            total,
-            side,
+            residual + total * inverse[0][:, None],
             lax.all_gather(rows, "tensor", axis=0, tiled=True),
             lax.all_gather(scalars, "tensor", axis=0),
         )
@@ -985,13 +992,14 @@
         scatter_kernel,
         out_shape=(
             jax.ShapeDtypeStruct((count, columns), f32),
-            jax.ShapeDtypeStruct((8, count), f32),
             jax.ShapeDtypeStruct((4 * rows.shape[0], rows.shape[1]), rows.dtype),
             jax.ShapeDtypeStruct((4, 8, count), f32),
         ),
-        in_specs=[vmem] * 3,
-        out_specs=(vmem, vmem, anywhere, vmem),
+        in_specs=[vmem] * 4,
+        out_specs=(vmem, anywhere, vmem),
         scratch_shapes=[
+            pltpu.VMEM((count, columns), f32),
+            pltpu.VMEM((8, count), f32),
             pltpu.VMEM((6, count, columns), bf16),
             pltpu.VMEM((3, 8, count), f32),
             pltpu.SemaphoreType.DMA((6,)),
@@ -1010,7 +1018,7 @@
             collective_id=5, has_side_effects=True, vmem_limit_bytes=32 * 2**20
         ),
         cost_estimate=pl.CostEstimate(flops=0, bytes_accessed=150 * 2**20, transcendentals=0),
-    )(partial, extra, rows)
+    )(partial, extra, rows, residual)
 
 
 def near_rows(rows):
@@ -1098,14 +1106,18 @@
     sc_any,
     mi_ref,
     mo_ref,
+    l_ref,
+    r_ref,
+    gain_ref,
     *refs,
-    follows,
+    gathers,
 ):
-    if follows:
-        (l_ref, r_ref, gain_ref, b_ref, i_ref), refs = refs[:5], refs[5:]
-    (o_ref, ni_ref, no_ref, slots_ref, os_ref), refs = refs[:5], refs[5:]
-    if follows:
-        (or_ref, og_ref, ox_ref, rd_ref), refs = refs[:4], refs[4:]
+    if gathers:
+        (b_ref, i_ref), refs = refs[:2], refs[2:]
+    (ni_ref, no_ref, slots_ref, os_ref, or_ref, og_ref), refs = refs[:6], refs[6:]
+    if gathers:
+        (ox_ref, rd_ref), refs = refs[:2], refs[2:]
+    o_ref, refs = refs[0], refs[1:]
     (p_ref, x_ref, d_ref, dr_ref, sc_ref, g_ref, h_ref, s_ref, fetch_sem), refs = refs[:9], refs[9:]
     square, refs = refs[:15], refs[15:]
     lines = (Line(0), Line(1))
@@ -1121,22 +1133,26 @@
         fetch.start()
     greet([{"tensor": lax.rem(me + 1, 4)}, {"tensor": lax.rem(me + 3, 4)}, {"dp": sibling}, {"dp": by_x}, {"dp": by_y}])
     sums = [SquareSum(ref, *square[5 * at : 5 * at + 5]) for at, ref in enumerate((g_ref, h_ref, s_ref))]
-    if follows:
+    og_ref[...] = jnp.zeros_like(og_ref)
+    half = o_ref.shape[0] // 2
+
+    def input_part(rows):
+        d_normed = o_ref[rows, :]
+        layer_in = l_ref[rows, :]
+        inverse = lax.rsqrt(jnp.mean(layer_in * layer_in, -1, keepdims=True) + epsilon)
+        scaled = layer_in * inverse
+        og_ref[0:1, :] += jnp.sum(d_normed * scaled, 0, keepdims=True)
+        d_scaled = d_normed * gain_ref[0:1, :]
+        fresh = r_ref[rows, :] + inverse * (d_scaled - scaled * jnp.mean(d_scaled * scaled, -1, keepdims=True))
+        or_ref[rows, :] = fresh
+        return fresh
+
+    if gathers:
         came, low_grad, scalars, rd_local, rd_send, rd_recv, *line_sems = refs
-        half = o_ref.shape[0] // 2
-        og_ref[...] = jnp.zeros_like(og_ref)
 
         def work(part):
             rows = slice(part * half, (part + 1) * half)
-            d_normed = o_ref[rows, :]
-            layer_in = l_ref[rows, :]
-            inverse = lax.rsqrt(jnp.mean(layer_in * layer_in, -1, keepdims=True) + epsilon)
-            scaled = layer_in * inverse
-            og_ref[0:1, :] += jnp.sum(d_normed * scaled, 0, keepdims=True)
-            d_scaled = d_normed * gain_ref[0:1, :]
-            fresh = r_ref[rows, :] + inverse * (d_scaled - scaled * jnp.mean(d_scaled * scaled, -1, keepdims=True))
-            or_ref[rows, :] = fresh
-            low = fresh.astype(bf16)
+            low = input_part(rows).astype(bf16)
             low_grad[rows, :] = low
             products = low.astype(f32) * b_ref[rows, :]
             dots = dot_exact(jnp.ones((8, products.shape[1]), f32), products, NT)
@@ -1149,7 +1165,7 @@
     else:
         total = LineSum(lines, p_ref, o_ref, *refs)
     fetches[0].wait()
-    if follows:
+    if gathers:
         line_pass.start()
     else:
         total.start()
@@ -1173,7 +1189,8 @@
 
     grads(0)
     grads(1)
-    total.step(1)
+    if gathers:
+        total.step(1)
     grads(2)
     grads(3)
     heads = HEADS // 4
@@ -1187,16 +1204,18 @@
         s_ref[: 2 * STATE, cols] = dot(both, x_ref[:, cols], TN).astype(bf16)
         s_ref[2 * STATE :, cols] = dot(moved, dot(steps, x_ref[:, cols], TN).astype(bf16)).astype(bf16)
     sums[2].start()
-    if follows:
+    if gathers:
         total.step(2)
     for each in sums:
         each.cores()
-    if follows:
+    if gathers:
         line_pass.turn(0)
         line_pass.between()
+    else:
+        total.step(1)
     for each in sums:
         each.join()
-    if follows:
+    if gathers:
         line_pass.across()
         line_pass.turn(1)
         small.start()
@@ -1211,7 +1230,7 @@
     no_ref[...] = fresh
     slots_ref[2] = fresh.astype(bf16)
     os_ref[...] = sums[2].finish()
-    if follows:
+    if gathers:
         line_pass.last()
         for time in range(1, 4):
             small.step(time)
@@ -1220,10 +1239,14 @@
     else:
         total.step(3)
         total.own()
+        for part in range(2):
+            input_part(slice(part * half, (part + 1) * half))
         total.finish()
 
 
-def exchange(partial, gathered, d_all, d_rows, scaled_low, in_momentum, out_momentum, following=None):
+def exchange(
+    partial, gathered, d_all, d_rows, scaled_low, in_momentum, out_momentum, layer_in, grad_resid, in_gain, below=None
+):
     rows, width = out_momentum.shape
     if not kernels_fit():
         heads = HEADS // lax.axis_size("tensor")
@@ -1242,24 +1265,23 @@
         in_new = muon_decay * in_momentum + jnp.stack([in_sum[:, :width], in_sum[:, width:]])
         out_new = muon_decay * out_momentum + add(out_grad)
         d_normed = lax.psum_scatter(partial, "tensor", scatter_dimension=0, tiled=True).astype(f32)
+        grad_resid, d_in_gain = input_step(d_normed, layer_in, grad_resid, in_gain)
         results = (
-            d_normed,
             in_new,
             out_new,
             jnp.concatenate([in_new, out_new[None]]).astype(bf16),
             add(shared_grad),
+            grad_resid,
+            d_in_gain,
         )
-        if following is None:
+        if below is None:
             return results
-        layer_in, grad_resid, in_gain, branch, scale = following
-        grad_resid, d_in_gain = input_step(d_normed, layer_in, grad_resid, in_gain)
+        branch, scale = below
         d_branch = grad_resid.astype(bf16)
         dots = jnp.sum(d_branch.astype(f32) * branch, -1)
         scalars = jnp.concatenate([scale[:1], jnp.broadcast_to(dots[None], (7, dots.shape[0]))])
         return (
             *results,
-            grad_resid,
-            d_in_gain,
             lax.all_gather(d_branch, "tensor", axis=0, tiled=True),
             lax.all_gather(scalars, "tensor", axis=0),
         )
@@ -1279,26 +1301,24 @@
         ]
     line = pltpu.SemaphoreType.DMA((6,))
     out_shape = [
-        jax.ShapeDtypeStruct((count, columns), f32),
         jax.ShapeDtypeStruct((2, rows, width), f32),
         jax.ShapeDtypeStruct((rows, width), f32),
         jax.ShapeDtypeStruct((3, rows, width), bf16),
         jax.ShapeDtypeStruct((SHARED_COLS // 8, D), f32),
+        jax.ShapeDtypeStruct((count, columns), f32),
+        jax.ShapeDtypeStruct((8, columns), f32),
     ]
-    out_specs = [vmem] * 5
-    if following is None:
-        more = ()
+    out_specs = [vmem] * 6
+    operands = [*fetched, in_momentum, out_momentum, layer_in, grad_resid, jnp.broadcast_to(in_gain[None], (8, columns))]
+    if below is None:
         scratch = [pltpu.VMEM((6, count, columns), bf16), line, line]
     else:
-        layer_in, grad_resid, in_gain, branch, scale = following
-        more = (layer_in, grad_resid, jnp.broadcast_to(in_gain[None], (8, columns)), branch, scale)
+        operands += below
         out_shape += [
-            jax.ShapeDtypeStruct((count, columns), f32),
-            jax.ShapeDtypeStruct((8, columns), f32),
             jax.ShapeDtypeStruct((4 * count, columns), bf16),
             jax.ShapeDtypeStruct((4, 8, count), f32),
         ]
-        out_specs += [vmem, vmem, anywhere, vmem]
+        out_specs += [anywhere, vmem]
         scratch = [
             pltpu.VMEM((2, 6, count // 2, columns), bf16),
             pltpu.VMEM((count, columns), bf16),
@@ -1309,11 +1329,12 @@
             *pass_sems(),
         ]
     results = pl.pallas_call(
-        functools.partial(exchange_kernel, follows=following is not None),
+        functools.partial(exchange_kernel, gathers=below is not None),
         out_shape=tuple(out_shape),
-        in_specs=[anywhere] * 5 + [vmem] * (2 + len(more)),
+        in_specs=[anywhere] * 5 + [vmem] * (len(operands) - 5),
         out_specs=tuple(out_specs),
         scratch_shapes=[
+            pltpu.VMEM((count, columns), f32),
             *[pltpu.VMEM(each.shape, bf16) for each in fetched],
             *[pltpu.VMEM(shape, bf16) for shape in shapes],
             pltpu.SemaphoreType.DMA((5,)),
@@ -1321,13 +1342,11 @@
             *scratch,
         ],
         compiler_params=pltpu.CompilerParams(
-            collective_id=3 if following is None else 7, has_side_effects=True, vmem_limit_bytes=62 * 2**20
+            collective_id=3 if below is None else 7, has_side_effects=True, vmem_limit_bytes=62 * 2**20
         ),
         cost_estimate=pl.CostEstimate(flops=10**10, bytes_accessed=150 * 2**20, transcendentals=0),
-    )(*fetched, in_momentum, out_momentum, *more)
-    if following is None:
-        return results
-    return (*results[:6], results[6][0], *results[7:])
+    )(*operands)
+    return (*results[:5], results[5][0], *results[6:])
 
 
 def input_step(d_normed, layer_in, grad_resid, in_gain):
@@ -1605,20 +1624,51 @@
         o_ref[layer] = w_ref[layer].astype(f32) - rate * next_low[layer, :SSM_COLS, :].astype(f32)
 
 
+def shared_pair_kernel(m_ref, w_ref, o_ref, low, next_low, shifted, both, send_sem, recv_sem):
+    index, core, sibling, by_x, by_y = neighbours()
+    greet([{"dp": sibling}])
+    momentum = m_ref[core]
+    scale = 1.0 / (jnp.sqrt(jnp.sum(momentum * momentum)) + 1e-07)
+    low[:SSM_COLS, :] = (momentum * scale).astype(bf16)
+    low[SSM_COLS:, :] = jnp.zeros((low.shape[0] - SSM_COLS, D), bf16)
+    iterate([(low, next_low, shifted)])
+    both[core] = next_low[...]
+    copy = remote(both.at[core], both.at[core], send_sem, recv_sem, 0, {"dp": sibling})
+    copy.start()
+    copy.wait()
+    rate = muon_rate * (D / SSM_COLS) ** 0.5
+    for layer in range(2):
+        o_ref[layer] = w_ref[layer].astype(f32) - rate * both[layer, :SSM_COLS, :].astype(f32)
+
+
 def shared_step(momentum, weight):
     vmem = pl.BlockSpec(memory_space=pltpu.VMEM)
     padded = -(-SSM_COLS // LANES) * LANES
+    pair = kernels_fit() and LAYERS == 2
+    if pair:
+        scratch = [
+            pltpu.VMEM((padded, D), bf16),
+            pltpu.VMEM((padded, D), bf16),
+            pltpu.VMEM((padded, padded), bf16),
+            pltpu.VMEM((2, padded, D), bf16),
+            pltpu.SemaphoreType.DMA((1,)),
+            pltpu.SemaphoreType.DMA((1,)),
+        ]
+        params = pltpu.CompilerParams(collective_id=0, has_side_effects=True, vmem_limit_bytes=56 * 2**20)
+    else:
+        scratch = [
+            pltpu.VMEM((LAYERS, padded, D), bf16),
+            pltpu.VMEM((LAYERS, padded, D), bf16),
+            pltpu.VMEM((LAYERS, padded, padded), bf16),
+        ]
+        params = pltpu.CompilerParams(vmem_limit_bytes=56 * 2**20)
     return pl.pallas_call(
-        shared_step_kernel,
+        shared_pair_kernel if pair else shared_step_kernel,
         out_shape=jax.ShapeDtypeStruct(momentum.shape, f32),
         in_specs=[vmem, vmem],
         out_specs=vmem,
-        scratch_shapes=[
-            pltpu.VMEM((LAYERS, padded, D), bf16),
-            pltpu.VMEM((LAYERS, padded, D), bf16),
-            pltpu.VMEM((LAYERS, padded, padded), bf16),
-        ],
-        compiler_params=pltpu.CompilerParams(vmem_limit_bytes=56 * 2**20),
+        scratch_shapes=scratch,
+        compiler_params=params,
         cost_estimate=pl.CostEstimate(
             flops=20 * padded * padded * (2 * D + padded), bytes_accessed=12 * D * padded, transcendentals=0
         ),
@@ -1720,8 +1770,7 @@
         if layer < LAYERS - 1:
             residual, branch, scale, gathered = forward_pass(partial, squares, residual, in_gains[layer + 1])
             branches[layer] = (branch, scale)
-    summed, square_sum, d_rows, rd = scatter_tokens(partial, squares, resid_grad.astype(bf16))
-    residual = residual + summed * lax.rsqrt(square_sum[0] / INNER + epsilon)[:, None]
+    residual, d_rows, rd = last_scatter(partial, squares, resid_grad.astype(bf16), residual)
 
     grad_resid = resid_grad
     in_new = [None] * LAYERS
@@ -1735,17 +1784,22 @@
         d_all, scaled_low, partial, grad_x, grad_s, grad_h = mixer_backward(
             d_rows, w_in[layer], w_out[layer], projected, total, states, rd, px_all[layer], ps_all[layer], ph_all[layer]
         )
-        following = None
+        results = exchange(
+            partial,
+            gathered,
+            d_all,
+            d_rows,
+            scaled_low,
+            in_momentum_planes[layer],
+            out_momentum[layer],
+            layer_in,
+            grad_resid,
+            in_gains[layer],
+            branches[layer - 1] if layer > 0 else None,
+        )
+        in_new[layer], out_new[layer], slots[layer], shared_shards[layer], grad_resid, d_in_gain = results[:6]
         if layer > 0:
-            following = (layer_in, grad_resid, in_gains[layer], *branches[layer - 1])
-        results = exchange(
-            partial, gathered, d_all, d_rows, scaled_low, in_momentum_planes[layer], out_momentum[layer], following
-        )
-        d_normed, in_new[layer], out_new[layer], slots[layer], shared_shards[layer] = results[:5]
-        if layer > 0:
-            grad_resid, d_in_gain, d_rows, rd = results[5:]
-        else:
-            grad_resid, d_in_gain = input_step(d_normed, layer_in, grad_resid, in_gains[layer])
+            d_rows, rd = results[6:]
         small_grads[layer] = jnp.concatenate([grad_x, grad_s, grad_h, d_in_gain.reshape(8, D // 8)], 1)
 
     in_momentum_new = jnp.transpose(jnp.stack(in_new), (0, 2, 1, 3))

time: 720 us -> 699 us (0.971)
  Pallas kernels: 625 us -> 604 us
    pallas_call x4, Pallas kernels: 273 us -> 257 us  [the longest x2 165 us: exchange(): pl.pallas_call(functools.partial(exchange_kernel, gathers=below is not No...]
    unnamed x76 -> x79, local copies, waits for them, and re-layouts: 20.1 us -> 24.7 us
  transfers between devices with their start and end apart: 3 -> 3, of which waited for: 0 -> 0; matrix products, arithmetic and copies ran while one was open for 3% -> 2% of each run, Pallas kernels for 21% -> 20%
where the time goes in v2:
time: 699 us; the launch traced here: 692 us
  Pallas kernels  604 us (86%)
  local copies, waits for them, and re-layouts  46.1 us (7%)
  other arithmetic  20.6 us (3%)
  between operations  15.1 us (2%)
    pallas_call x2, Pallas kernels, exchange(): pl.pallas_call(functools.partial(exchange_kernel, gathers=below is not No...  165 us
    pallas_call x1, Pallas kernels, forward_pass(): pl.pallas_call(forward_pass_kernel, out_shape=(jax.ShapeDtypeStruct((coun...  97 us
    pallas_call x2, Pallas kernels, mixer_backward(): pl.pallas_call(backward_kernel, grid=(spans,), in_specs=[pl.BlockSpec((SP...  78.6 us
    pallas_call x1, Pallas kernels, last_scatter(): pl.pallas_call(scatter_kernel, out_shape=(jax.ShapeDtypeStruct((count, co...  73.3 us
    pallas_call x1, Pallas kernels, gather_first(): pl.pallas_call(first_kernel, out_shape=(larger(rows, 4), larger(w_rows, 8...  61.7 us
    pallas_call x1, Pallas kernels, finish_blocks(): pl.pallas_call(tail_kernel, out_shape=(jax.ShapeDtypeStruct((8, *shard.sh...  59.8 us
    pallas_call x2, Pallas kernels, mixer_forward(): pl.pallas_call(forward_kernel, grid=(spans,), in_specs=[pl.BlockSpec((SPA...  50.5 us
    unnamed x79, local copies, waits for them, and re-layouts  24.7 us
  transfers between devices with their start and end apart: 3, of which 0 were waited for; matrix products, arithmetic and copies ran while one was open for 2% of the time, Pallas kernels for 20%

profile of v2, /device:TPU:0, one launch (start us, length us, event | category | flops | bytes accessed | tf_op | source)
XLA Modules:
  0.0 691.8 jit_solution(14370642956332988118)
XLA Ops:
  9.7 1.7 fusion.12
  16.2 61.7 %shard_map.194 = (bf16[1024,1536]{1,0:T(8,128)(2,1)}, bf16[1536,1920]{1,0:T(8,128)(2,1)}, bf16[1536,768]{1,0:T(8,128)(2,1)}) custom-call(bf16[256,1536]{1,0:T(8,128)(2,1)} %multiply_convert_fusion.x_ref, bf16[192,1920]{1,0:T(8,128)(2,1)} %fusion.4.w_ref, bf16[192,768]{1,0:T(8,128)(2,1)} %get-tuple-element.155.v_ref), custom_call_target="tpu_custom_call" | custom-call | bytes 157286400 | tf_op jit(solution)/shard_map/pallas_call | solution.py:650
  82.2 25.4 %shard_map.195 = (f32[1024,1920]{1,0:T(8,128)}, f32[1024,768]{1,0:T(8,128)}, bf16[1024,1536]{1,0:T(8,128)(2,1)}, f32[4,8,256]{2,1,0:T(8,128)}, bf16[4,128,768]{2,1,0:T(8,128)(2,1)}) custom-call(bf16[1024,1536]{1,0:T(8,128)(2,1)} %get-tuple-element.64.g_ref.x_any, bf16[1536,1920]{1,0:T(8,128)(2,1)} %get-tuple-element.65.w_ref, ...), custom_call_target="tpu_custom_call" | custom-call | flops 10000000000 | bytes 33554432 | tf_op jit(solution)/shard_map/pallas_call | solution.py:351
  111.2 97.0 %shard_map.196 = (f32[256,1536]{1,0:T(8,128)S(1)}, f32[256,1536]{1,0:T(8,128)S(1)}, f32[8,256]{1,0:T(8,128)S(1)}, bf16[1024,1536]{1,0:T(8,128)(2,1)S(1)}) custom-call(bf16[1024,1536]{1,0:T(8,128)(2,1)S(1)} %copy-done.1, f32[4,8,256]{2,1,0:T(8,128)S(1)} %broadcast_in_dim.42.q_ref, f32[256,1536]{1,0:T(8,128)S(1)} %copy-done, ...), custom_call_target="tpu_custom_call" | custom-call | bytes 262144000 | tf_op jit(solution)/shard_map/pallas_call | solution.py:879
  209.4 1.7 copy-done.6
  214.1 25.1 %shard_map.197 = (f32[1024,1920]{1,0:T(8,128)}, f32[1024,768]{1,0:T(8,128)}, bf16[1024,1536]{1,0:T(8,128)(2,1)}, f32[4,8,256]{2,1,0:T(8,128)}, bf16[4,128,768]{2,1,0:T(8,128)(2,1)}) custom-call(bf16[1024,1536]{1,0:T(8,128)(2,1)} %copy-done.6, bf16[1536,1920]{1,0:T(8,128)(2,1)} %all-gather.3.cloned.1.call-done.w_ref, ...), custom_call_target="tpu_custom_call" | custom-call | flops 10000000000 | bytes 33554432 | tf_op jit(solution)/shard_map/pallas_call | solution.py:351
  240.0 1.9 copy-done.2
  241.9 73.3 %shard_map.198 = (f32[256,1536]{1,0:T(8,128)S(1)}, bf16[1024,1536]{1,0:T(8,128)(2,1)S(1)}, f32[4,8,256]{2,1,0:T(8,128)S(1)}) custom-call(bf16[1024,1536]{1,0:T(8,128)(2,1)S(1)} %copy-done.2, f32[4,8,256]{2,1,0:T(8,128)S(1)} %broadcast_in_dim.46.q_ref, bf16[256,1536]{1,0:T(8,128)(2,1)S(1)} %convert_element_type.26.x_ref, f32[256,1536]{1,0:T(8,128)S(1)} %copy-done.4), custom_call_target="tpu_custom_call" | custom-call | bytes 157286400 | tf_op jit(solution)/shard_map/pallas_call | solution.py:991
  315.3 1.7 copy-done.7
  318.0 39.1 %shard_map.199 = (bf16[1024,1920]{1,0:T(8,128)(2,1)}, bf16[1024,768]{1,0:T(8,128)(2,1)}, bf16[1024,1536]{1,0:T(8,128)(2,1)}, f32[8,768]{1,0:T(8,128)}, f32[8,256]{1,0:T(8,128)}, /*index=5*/f32[8,128]{1,0:T(8,128)}) custom-call(bf16[1024,1536]{1,0:T(8,128)(2,1)} %copy-done.7, bf16[1536,1920]{1,0:T(8,128)(2,1)} %all-gather.3.cloned.1.call-done.w_ref, ...), custom_call_target="tpu_custom_call" | custom-call | flops 16000000000 | bytes 50331648 | tf_op jit(solution)/shard_map/pallas_call | solution.py:395
  357.1 102.7 %shard_map.200 = (f32[2,192,768]{2,1,0:T(8,128)}, f32[192,768]{1,0:T(8,128)}, bf16[3,192,768]{2,1,0:T(8,128)(2,1)}, f32[48,1536]{1,0:T(8,128)}, f32[256,1536]{1,...) custom-call(bf16[1024,1536]{1,0:T(8,128)(2,1)} %get-tuple-element.81.p_any, ...), custom_call_target="tpu_custom_call" | custom-call | flops 10000000000 | bytes 157286400 | tf_op jit(solution)/shard_map/pallas_call | solution.py:1331
  461.6 39.5 %shard_map.201 = (bf16[1024,1920]{1,0:T(8,128)(2,1)}, bf16[1024,768]{1,0:T(8,128)(2,1)}, bf16[1024,1536]{1,0:T(8,128)(2,1)}, f32[8,768]{1,0:T(8,128)}, f32[8,256]{1,0:T(8,128)}, /*index=5*/f32[8,128]{1,0:T(8,128)}) custom-call(bf16[1024,1536]{1,0:T(8,128)(2,1)} %get-tuple-element.86.dr_ref.dr_any, bf16[1536,1920]{1,0:T(8,128)(2,1)} %get-tuple-element.65.w_ref, ...), custom_call_target="tpu_custom_call" | custom-call | flops 16000000000 | bytes 50331648 | tf_op jit(solution)/shard_map/pallas_call | solution.py:395
  501.7 62.3 %shard_map.202 = (f32[2,192,768]{2,1,0:T(8,128)}, f32[192,768]{1,0:T(8,128)}, bf16[3,192,768]{2,1,0:T(8,128)(2,1)}, f32[48,1536]{1,0:T(8,128)}, f32[256,1536]{1,0:T(8,128)}, /*index=5*/f32[8,1536]{1,0:T(8,128)}) custom-call(bf16[1024,1536]{1,0:T(8,128)(2,1)} %get-tuple-element.91.p_any, bf16[1024,1536]{1,0:T(8,128)(2,1)} %get-tuple-element.64.g_ref.x_any, ...), custom_call_target="tpu_custom_call" | custom-call | flops 10000000000 | bytes 157286400 | tf_op jit(solution)/shard_map/pallas_call | solution.py:1331
  565.9 1.8 pad_maximum_fusion.2.s_ref
  567.7 2.6 pad_maximum_fusion.b_ref
  571.0 59.8 %shard_map.203 = (bf16[8,96,1536]{2,1,0:T(8,128)(2,1)}, f32[4,8,2688]{2,1,0:T(8,128)}, bf16[1536,768]{1,0:T(8,128)(2,1)}) custom-call(f32[96,1536]{1,0:T(8,128)} %pad_maximum_fusion.2.s_ref, f32[8,2688]{1,0:T(8,128)} %concatenate.28.v_ref, bf16[6,192,768]{2,1,0:T(8,128)(2,1)} %pad_maximum_fusion.b_ref), custom_call_target="tpu_custom_call" | custom-call | flops 20000000000 | bytes 104857600 | tf_op jit(solution)/shard_map/pallas_call | solution.py:1535
  635.9 4.8 all-to-all-start
  644.4 3.2 copy.57
  647.9 1.9 copy-done.12
  649.7 2.5 bitcast_add_fusion.m_ref
  652.2 18.5 %shard_map.204 = f32[2,304,1536]{2,1,0:T(8,128)} custom-call(f32[2,304,1536]{2,1,0:T(8,128)} %bitcast_add_fusion.m_ref, bf16[2,304,1536]{2,1,0:T(8,128)(2,1)} %bitcast.98), custom_call_target="tpu_custom_call" | custom-call | flops 10192158720 | bytes 7077888 | tf_op jit(solution)/shard_map/pallas_call | solution.py:1665
  671.9 1.9 convert_multiply_fusion
  676.0 3.2 copy.58
  682.7 1.9 copy.73
  (165 shorter events, 41.6 us)
Async XLA Ops:
  7.2 206.9 %all-gather.5.cloned.1.call-start = ((), (), s32[]{:S(2)}) async-start(), calls=%async_computation.2 | async-start | bytes 2654208 | tf_op jit(solution)/shard_map/all_gather | solution.py:1760
  78.9 135.2 %all-gather.3.cloned.1.call-start = ((), (), s32[]{:S(2)}) async-start(), calls=%async_computation.1 | async-start | bytes 6635520 | tf_op jit(solution)/shard_map/all_gather | solution.py:1759
  82.2 26.3 %copy-start.18 = (f32[256,1536]{1,0:T(8,128)S(1)}, f32[256,1536]{1,0:T(8,128)}, u32[]{:S(2)}) copy-start(f32[256,1536]{1,0:T(8,128)} %r_ref.3) | copy-start | bytes 4718596
  111.2 97.0 %copy-start.5 = (f32[8,1536]{1,0:T(8,128)}, f32[8,1536]{1,0:T(8,128)S(1)}, u32[]{:S(2)}) copy-start(f32[8,1536]{1,0:T(8,128)S(1)} %broadcast_in_dim.44.gain_ref) | copy-start | bytes 147460
  111.2 99.8 %copy-start.20 = (f32[2,192,768]{2,1,0:T(8,128)S(1)}, f32[2,192,768]{2,1,0:T(8,128)}, u32[]{:S(2)}) copy-start(f32[2,192,768]{2,1,0:T(8,128)} %param.17) | copy-start | bytes 3538948
  211.0 3.1 copy-start.9
  214.1 25.9 %copy-start.4 = (f32[256,1536]{1,0:T(8,128)S(1)}, f32[256,1536]{1,0:T(8,128)}, u32[]{:S(2)}) copy-start(f32[256,1536]{1,0:T(8,128)} %copy-done.3) | copy-start | bytes 4718596
  501.7 64.2 %copy-start.26 = (f32[48,1536]{1,0:T(8,128)S(1)}, f32[48,1536]{1,0:T(8,128)}, u32[]{:S(2)}) copy-start(f32[48,1536]{1,0:T(8,128)} %get-tuple-element.97) | copy-start | bytes 884740
  564.0 3.7 copy-start.22
  567.7 2.6 copy-start.29
  567.7 2.6 copy-start.30
  567.7 2.6 copy-start.31
  567.7 2.6 copy-start.32
  567.7 2.6 copy-start.33
  567.7 2.6 copy-start.34
  635.9 5.7 copy-start.23
  635.9 5.7 copy-start.27
  635.9 5.7 copy-start.28
  635.9 36.0 %all-to-all-start = ((bf16[8,192,768]{2,1,0:T(8,128)(2,1)}), bf16[8,192,768]{2,1,0:T(8,128)(2,1)}, u32[]{:S(2)}, u32[]{:S(2)}) async-start(bf16[8,192,768]{2,1,0:T(8,128)(2,1)} %bitcast.96), calls=%async_computation | async-start | bytes 4718592 | tf_op jit(solution)/shard_map/all_to_all | solution.py:1813
  640.7 2.3 copy-start.21
  644.4 3.2 copy-start.15
  652.2 18.5 %copy-start.24 = (f32[192,768]{1,0:T(8,128)S(1)}, f32[192,768]{1,0:T(8,128)}, u32[]{:S(2)}) copy-start(f32[192,768]{1,0:T(8,128)} %get-tuple-element.113) | copy-start | bytes 1769476
  652.2 18.6 %copy-start.25 = (f32[192,768]{1,0:T(8,128)S(1)}, f32[192,768]{1,0:T(8,128)}, u32[]{:S(2)}) copy-start(f32[192,768]{1,0:T(8,128)} %get-tuple-element.112) | copy-start | bytes 1769476
  679.2 3.5 copy-start.13
  (17 other events, 29.9 us)
Sparse Core Ops, SparseCore 0:
  79.1 27.2 all-gather.4
  108.8 43.8 all-gather.2

commit v3 on v2

--- a/solution.py
+++ b/solution.py
@@ -91,8 +91,8 @@
     return dot(jnp.concatenate([high, low], 1), owner)
 
 
-def matmul_into(target, left, right, dims, width, piece):
-    for at in range(0, width, piece):
+def matmul_into(target, left, right, dims, width, piece, first=0):
+    for at in range(first, width, piece):
         cols = slice(at, min(at + piece, width))
         mine = right[:, cols] if dims == NN else right[cols, :]
         target[:, cols] = dot(left, mine, dims).astype(target.dtype)
@@ -102,20 +102,38 @@
     g_ref, w_ref, wo_ref, px_ref, ps_ref, ph_ref, proj_ref, yt_ref, p_ref, sq_ref, st_ref, state, xpad, spad, gained
 ):
     step = pl.program_id(0)
+    spans = pl.num_programs(0) - 1
     columns = yt_ref.shape[1]
-    pairs = columns // LANES
+    here, there = lax.rem(step, 2), lax.rem(step + 1, 2)
 
     @pl.when(step == 0)
     def _():
         state[...] = jnp.zeros_like(state)
         xpad[0:HALO, :] = jnp.zeros((HALO, columns), f32)
         spad[0:HALO, :] = jnp.zeros((HALO, 2 * STATE), f32)
+        gained[there] = jnp.zeros((SPAN, columns), bf16)
 
     @pl.when(step > 0)
     def _():
         xpad[0:HALO, :] = xpad[SPAN : SPAN + HALO, :]
         spad[0:HALO, :] = spad[SPAN : SPAN + HALO, :]
 
+    @pl.when(step < spans)
+    def _():
+        forward_span(
+            g_ref, w_ref, wo_ref, px_ref, ps_ref, ph_ref, proj_ref, yt_ref, p_ref, sq_ref, st_ref, state, xpad, spad, gained, here, there
+        )
+
+    @pl.when(step == spans)
+    def _():
+        matmul_into(p_ref, gained[there], wo_ref, NT, D, 2 * LANES)
+
+
+def forward_span(
+    g_ref, w_ref, wo_ref, px_ref, ps_ref, ph_ref, proj_ref, yt_ref, p_ref, sq_ref, st_ref, state, xpad, spad, gained, here, there
+):
+    columns = yt_ref.shape[1]
+    pairs = columns // LANES
     matmul_into(proj_ref, g_ref[...], w_ref, NN, 2 * columns + SHARED_COLS, 2 * LANES)
     xpad[HALO:, :] = proj_ref[:, columns : 2 * columns]
     spad[HALO:, :] = proj_ref[:, 2 * columns : 2 * columns + 2 * STATE]
@@ -133,6 +151,7 @@
     squares = jnp.zeros((SPAN, LANES), f32)
     half = SPAN // 2
     for pair in range(pairs):
+        matmul_into(p_ref, gained[there], wo_ref, NT, (pair + 1) * D // pairs, 2 * LANES, pair * D // pairs)
         lanes = slice(pair * LANES, (pair + 1) * LANES)
         pre = conv_of(xpad, lanes, px_ref, first)
         xc = pre * sigmoid(pre)
@@ -158,10 +177,9 @@
         yt_ref[:, lanes] = total
         gate = proj_ref[:, lanes]
         mixed = total * gate * sigmoid(gate)
-        gained[:, lanes] = (mixed * px_ref[5:6, lanes]).astype(bf16)
+        gained[here, :, lanes] = (mixed * px_ref[5:6, lanes]).astype(bf16)
         squares = squares + mixed * mixed
     sq_ref[0] = dot_exact(jnp.ones((8, LANES), f32), squares, NT)
-    matmul_into(p_ref, gained[...], wo_ref, NT, D, 2 * LANES)
 
 
 def backward_kernel(
@@ -191,11 +209,12 @@
     dxpad,
     dspad,
     dsc,
+    held_all,
 ):
     step = pl.program_id(0)
-    steps = pl.num_programs(0)
+    steps = pl.num_programs(0) - 1
     columns = x_ref.shape[1]
-    pairs = columns // LANES
+    here, there = lax.rem(step, 2), lax.rem(step + 1, 2)
 
     @pl.when(step == 0)
     def _():
@@ -205,12 +224,89 @@
         gx_ref[...] = jnp.zeros_like(gx_ref)
         gs_ref[...] = jnp.zeros_like(gs_ref)
         gh_ref[...] = jnp.zeros_like(gh_ref)
+        held_all[there] = jnp.zeros(dall_ref.shape, bf16)
 
     @pl.when(step > 0)
     def _():
         dxpad[SPAN:, :] = dxpad[0:HALO, :]
         dspad[SPAN:, :] = dspad[0:HALO, :]
 
+    @pl.when(step < steps)
+    def _():
+        backward_span(
+            dr_ref,
+            w_ref,
+            wo_ref,
+            gate_ref,
+            x_ref,
+            xh_ref,
+            sh_ref,
+            shh_ref,
+            yt_ref,
+            st_ref,
+            rd_ref,
+            px_ref,
+            ps_ref,
+            ph_ref,
+            dall_ref,
+            scaled_ref,
+            p_ref,
+            gx_ref,
+            gs_ref,
+            gh_ref,
+            dstate,
+            xpad,
+            spad,
+            dxpad,
+            dspad,
+            dsc,
+            held_all,
+            step,
+            steps,
+            here,
+            there,
+        )
+
+    @pl.when(step == steps)
+    def _():
+        matmul_into(p_ref, held_all[there], w_ref, NT, D, 2 * LANES)
+
+
+def backward_span(
+    dr_ref,
+    w_ref,
+    wo_ref,
+    gate_ref,
+    x_ref,
+    xh_ref,
+    sh_ref,
+    shh_ref,
+    yt_ref,
+    st_ref,
+    rd_ref,
+    px_ref,
+    ps_ref,
+    ph_ref,
+    dall_ref,
+    scaled_ref,
+    p_ref,
+    gx_ref,
+    gs_ref,
+    gh_ref,
+    dstate,
+    xpad,
+    spad,
+    dxpad,
+    dspad,
+    dsc,
+    held_all,
+    step,
+    steps,
+    here,
+    there,
+):
+    columns = x_ref.shape[1]
+    pairs = columns // LANES
     matmul_into(dsc, dr_ref[...], wo_ref, NN, columns, 2 * LANES)
     before = jnp.where(step < steps - 1, 1.0, 0.0).astype(f32)
     xpad[0:HALO, :] = xh_ref[...] * before
@@ -243,6 +339,7 @@
     d_step = jnp.zeros((SPAN, LANES), f32)
     d_last = jnp.zeros((8, LANES), f32)
     for pair in range(pairs):
+        matmul_into(p_ref, held_all[there], w_ref, NT, (pair + 1) * D // pairs, 2 * LANES, pair * D // pairs)
         lanes = slice(pair * LANES, (pair + 1) * LANES)
         owner = jnp.where(head_row + 2 * pair == head_col, 1.0, 0.0).astype(bf16)
         pre = conv_of(xpad, lanes, px_ref, first)
@@ -261,7 +358,7 @@
         d_scaled = dsc[:, lanes]
         gx_ref[5:6, lanes] += jnp.sum(d_scaled * sn, 0, keepdims=True)
         d_mixed = inverse * (d_scaled * gain - sn * dots)
-        dall_ref[:, lanes] = (
+        held_all[here, :, lanes] = (
             d_mixed * total * (sig_gate * (1.0 + gate * (1.0 - sig_gate)))
         ).astype(bf16)
         dy = d_mixed * silu
@@ -311,7 +408,7 @@
             if tap < KERNEL - 1:
                 ahead = KERNEL - 1 - tap
                 d_x = d_x + px_ref[tap : tap + 1, lanes] * dxpad[ahead : ahead + SPAN, lanes]
-        dall_ref[:, columns + pair * LANES : columns + (pair + 1) * LANES] = d_x.astype(bf16)
+        held_all[here, :, columns + pair * LANES : columns + (pair + 1) * LANES] = d_x.astype(bf16)
     d_log = dot_exact(upper, d_cum) + d_last[0:1, :]
     d_raw = (d_step + d_log * decay) * sigmoid(raw)
     gh_ref[0:1, :] += jnp.sum(d_log * log_decay, 0, keepdims=True)
@@ -334,9 +431,9 @@
         if tap < KERNEL - 1:
             ahead = KERNEL - 1 - tap
             d_s = d_s + ps_ref[tap : tap + 1, :] * dspad[ahead : ahead + SPAN, :]
-    dall_ref[:, 2 * columns : 2 * columns + 2 * STATE] = d_s.astype(bf16)
-    dall_ref[:, 2 * columns + 2 * STATE :] = d_raw.astype(bf16)
-    matmul_into(p_ref, dall_ref[...], w_ref, NT, D, 2 * LANES)
+    held_all[here, :, 2 * columns : 2 * columns + 2 * STATE] = d_s.astype(bf16)
+    held_all[here, :, 2 * columns + 2 * STATE :] = d_raw.astype(bf16)
+    dall_ref[...] = held_all[here]
 
 
 def resident(shape):
@@ -347,10 +444,11 @@
     length, columns = gathered.shape[0], px.shape[1]
     spans = length // SPAN
     width = 2 * columns + SHARED_COLS
-    here = lambda i: (i, 0)
+    at = lambda i: jnp.minimum(i, spans - 1)
+    here = lambda i: (at(i), 0)
     return pl.pallas_call(
         forward_kernel,
-        grid=(spans,),
+        grid=(spans + 1,),
         in_specs=[
             pl.BlockSpec((SPAN, D), here),
             resident((D, width)),
@@ -362,9 +460,9 @@
         out_specs=[
             pl.BlockSpec((SPAN, width), here),
             pl.BlockSpec((SPAN, columns), here),
-            pl.BlockSpec((SPAN, D), here),
-            pl.BlockSpec((1, 8, SPAN), lambda i: (i, 0, 0)),
-            pl.BlockSpec((1, STATE, columns), lambda i: (i, 0, 0)),
+            pl.BlockSpec((SPAN, D), lambda i: (jnp.maximum(i - 1, 0), 0)),
+            pl.BlockSpec((1, 8, SPAN), lambda i: (at(i), 0, 0)),
+            pl.BlockSpec((1, STATE, columns), lambda i: (at(i), 0, 0)),
         ],
         out_shape=[
             jax.ShapeDtypeStruct((length, width), f32),
@@ -377,7 +475,7 @@
             pltpu.VMEM((STATE, columns), f32),
             pltpu.VMEM((SPAN + HALO, columns), f32),
             pltpu.VMEM((SPAN + HALO, 2 * STATE), f32),
-            pltpu.VMEM((SPAN, columns), bf16),
+            pltpu.VMEM((2, SPAN, columns), bf16),
         ],
         compiler_params=pltpu.CompilerParams(vmem_limit_bytes=56 * 2**20),
         cost_estimate=pl.CostEstimate(flops=10 * 10**9, bytes_accessed=32 * 2**20, transcendentals=0),
@@ -388,24 +486,25 @@
     length, columns = total.shape
     spans = length // SPAN
     width = 2 * columns + SHARED_COLS
-    here = lambda i: (spans - 1 - i, 0)
+    at = lambda i: jnp.maximum(spans - 1 - i, 0)
+    here = lambda i: (at(i), 0)
     blocks = SPAN // HALO
-    halo = lambda i: jnp.maximum((spans - 1 - i) * blocks - 1, 0)
+    halo = lambda i: jnp.maximum(at(i) * blocks - 1, 0)
     tail_block = 2 * columns // SHARED_COLS
     return pl.pallas_call(
         backward_kernel,
-        grid=(spans,),
+        grid=(spans + 1,),
         in_specs=[
             pl.BlockSpec((SPAN, D), here),
             resident((D, width)),
             resident((D, columns)),
             pl.BlockSpec((SPAN, columns), here),
-            pl.BlockSpec((SPAN, columns), lambda i: (spans - 1 - i, 1)),
+            pl.BlockSpec((SPAN, columns), lambda i: (at(i), 1)),
             pl.BlockSpec((HALO, columns), lambda i: (halo(i), 1)),
-            pl.BlockSpec((SPAN, SHARED_COLS), lambda i: (spans - 1 - i, tail_block)),
+            pl.BlockSpec((SPAN, SHARED_COLS), lambda i: (at(i), tail_block)),
             pl.BlockSpec((HALO, SHARED_COLS), lambda i: (halo(i), tail_block)),
             pl.BlockSpec((SPAN, columns), here),
-            pl.BlockSpec((1, STATE, columns), lambda i: (spans - 1 - i, 0, 0)),
+            pl.BlockSpec((1, STATE, columns), lambda i: (at(i), 0, 0)),
             pl.BlockSpec((SPAN, 2), here),
             resident((8, columns)),
             resident((8, 2 * STATE)),
@@ -414,7 +513,7 @@
         out_specs=[
             pl.BlockSpec((SPAN, width), here),
             pl.BlockSpec((SPAN, columns), here),
-            pl.BlockSpec((SPAN, D), here),
+            pl.BlockSpec((SPAN, D), lambda i: (jnp.minimum(spans - i, spans - 1), 0)),
             pl.BlockSpec((8, columns), lambda i: (0, 0)),
             pl.BlockSpec((8, 2 * STATE), lambda i: (0, 0)),
             pl.BlockSpec((8, LANES), lambda i: (0, 0)),
@@ -434,6 +533,7 @@
             pltpu.VMEM((SPAN + HALO, columns), f32),
             pltpu.VMEM((SPAN + HALO, 2 * STATE), f32),
             pltpu.VMEM((SPAN, columns), f32),
+            pltpu.VMEM((2, SPAN, width), bf16),
         ],
         compiler_params=pltpu.CompilerParams(vmem_limit_bytes=56 * 2**20),
         cost_estimate=pl.CostEstimate(flops=16 * 10**9, bytes_accessed=48 * 2**20, transcendentals=0),
@@ -1025,6 +1125,62 @@
     return -(-rows // 32) * 16
 
 
+class Blocks:
+    def __init__(self, source, result, owners, send_sem, recv_sem, local_sem):
+        self.source, self.result, self.owners = source, result, owners
+        self.send_sem, self.recv_sem, self.local_sem = send_sem, recv_sem, local_sem
+        self.index = lax.axis_index("dp")
+
+    def copy(self, slot):
+        return pltpu.make_async_remote_copy(
+            src_ref=self.source.at[slot],
+            dst_ref=self.result.at[self.index],
+            send_sem=self.send_sem.at[slot],
+            recv_sem=self.recv_sem.at[self.index],
+            device_id={"dp": self.owners[slot]},
+            device_id_type=MESH,
+        )
+
+    def own(self, slot):
+        return pltpu.make_async_copy(self.source.at[slot], self.result.at[self.owners[slot]], self.local_sem)
+
+    def start(self):
+        for slot, owner in enumerate(self.owners):
+
+            @pl.when(self.index != owner)
+            def _(slot=slot):
+                self.copy(slot).start()
+
+            @pl.when(self.index == owner)
+            def _(slot=slot):
+                self.own(slot).start()
+
+    def arrive(self):
+        for slot, owner in enumerate(self.owners):
+
+            @pl.when(self.index == owner)
+            def _(slot=slot, owner=owner):
+                self.own(slot).wait()
+                for sender in range(8):
+                    if sender != owner:
+                        place = self.result.at[sender]
+                        where = {"dp": lax.rem(self.index + 1, 8)}
+                        remote(place, place, self.recv_sem, self.recv_sem, sender, where).wait_recv()
+
+    def finish(self):
+        for slot, owner in enumerate(self.owners):
+
+            @pl.when(self.index != owner)
+            def _(slot=slot):
+                self.copy(slot).wait_send()
+
+
+def owners_of(layer):
+    if not kernels_fit():
+        return tuple(range(3 * layer, 3 * layer + 3))
+    return ((1, 3, 6), (0, 2, 4))[layer]
+
+
 class SquareSum:
     def __init__(self, g_ref, sib, relay, came, send_sem, recv_sem):
         self.g_ref, self.sib, self.relay, self.came = g_ref, sib, relay, came
@@ -1116,7 +1272,7 @@
         (b_ref, i_ref), refs = refs[:2], refs[2:]
     (ni_ref, no_ref, slots_ref, os_ref, or_ref, og_ref), refs = refs[:6], refs[6:]
     if gathers:
-        (ox_ref, rd_ref), refs = refs[:2], refs[2:]
+        (ox_ref, rd_ref, early_ref), refs = refs[:3], refs[3:]
     o_ref, refs = refs[0], refs[1:]
     (p_ref, x_ref, d_ref, dr_ref, sc_ref, g_ref, h_ref, s_ref, fetch_sem), refs = refs[:9], refs[9:]
     square, refs = refs[:15], refs[15:]
@@ -1131,7 +1287,11 @@
     ]
     for fetch in fetches:
         fetch.start()
-    greet([{"tensor": lax.rem(me + 1, 4)}, {"tensor": lax.rem(me + 3, 4)}, {"dp": sibling}, {"dp": by_x}, {"dp": by_y}])
+    near_tensor = [{"tensor": lax.rem(me + 1, 4)}, {"tensor": lax.rem(me + 3, 4)}]
+    if gathers:
+        greet([*near_tensor, *[{"dp": lax.rem(index + ahead, 8)} for ahead in range(1, 8)]])
+    else:
+        greet([*near_tensor, {"dp": sibling}, {"dp": by_x}, {"dp": by_y}])
     sums = [SquareSum(ref, *square[5 * at : 5 * at + 5]) for at, ref in enumerate((g_ref, h_ref, s_ref))]
     og_ref[...] = jnp.zeros_like(og_ref)
     half = o_ref.shape[0] // 2
@@ -1148,7 +1308,9 @@
         return fresh
 
     if gathers:
-        came, low_grad, scalars, rd_local, rd_send, rd_recv, *line_sems = refs
+        came, low_grad, scalars, rd_local, rd_send, rd_recv, *refs = refs
+        blocks = Blocks(slots_ref, early_ref, owners_of(1), *refs[:3])
+        line_sems = refs[3:]
 
         def work(part):
             rows = slice(part * half, (part + 1) * half)
@@ -1229,6 +1391,8 @@
     fresh = muon_decay * mo_ref[...] + sums[1].finish()
     no_ref[...] = fresh
     slots_ref[2] = fresh.astype(bf16)
+    if gathers:
+        blocks.start()
     os_ref[...] = sums[2].finish()
     if gathers:
         line_pass.last()
@@ -1236,6 +1400,8 @@
             small.step(time)
         line_pass.finish()
         small.finish()
+        blocks.arrive()
+        blocks.finish()
     else:
         total.step(3)
         total.own()
@@ -1284,6 +1450,7 @@
             *results,
             lax.all_gather(d_branch, "tensor", axis=0, tiled=True),
             lax.all_gather(scalars, "tensor", axis=0),
+            None,
         )
     count, columns = partial.shape[0] // 4, partial.shape[1]
     vmem = pl.BlockSpec(memory_space=pltpu.VMEM)
@@ -1317,8 +1484,9 @@
         out_shape += [
             jax.ShapeDtypeStruct((4 * count, columns), bf16),
             jax.ShapeDtypeStruct((4, 8, count), f32),
+            jax.ShapeDtypeStruct((8, rows, width), bf16),
         ]
-        out_specs += [anywhere, vmem]
+        out_specs += [anywhere, vmem, anywhere]
         scratch = [
             pltpu.VMEM((2, 6, count // 2, columns), bf16),
             pltpu.VMEM((count, columns), bf16),
@@ -1326,6 +1494,9 @@
             pltpu.SemaphoreType.DMA,
             line,
             line,
+            pltpu.SemaphoreType.DMA((3,)),
+            pltpu.SemaphoreType.DMA((8,)),
+            pltpu.SemaphoreType.DMA,
             *pass_sems(),
         ]
     results = pl.pallas_call(
@@ -1361,9 +1532,12 @@
 
 
 def tail_kernel(
-    s_ref,
-    v_ref,
+    s0_ref,
+    s1_ref,
+    v0_ref,
+    v1_ref,
     b_ref,
+    early_ref,
     os_ref,
     ov_ref,
     t_ref,
@@ -1389,34 +1563,33 @@
     beyond = lax.rem(me + 2, 4)
     others_dp = [lax.rem(index + ahead, 8) for ahead in range(1, 8)]
     greet([{"tensor": beside}, {"tensor": beyond}, *[{"dp": other} for other in others_dp]])
-    blocks, rows = b_ref.shape[0], b_ref.shape[1]
-
-    def block_to(owner):
-        return pltpu.make_async_remote_copy(
-            src_ref=b_ref.at[owner],
-            dst_ref=whole.at[index],
-            send_sem=block_send.at[owner],
-            recv_sem=block_recv.at[index],
-            device_id={"dp": owner},
-            device_id_type=MESH,
-        )
-
-    for owner in range(blocks):
-
-        @pl.when(index != owner)
-        def _(owner=owner):
-            block_to(owner).start()
+    rows = b_ref.shape[1]
+    blocks = Blocks(b_ref, whole, owners_of(0), block_send, block_recv, block_local.at[0])
+    blocks.start()
+    idle = index >= 0
+    for owner in (*owners_of(0), *owners_of(1)):
+        idle = jnp.logical_and(idle, index != owner)
+
+    def stored():
+        return pltpu.make_async_copy(early_ref, whole, block_local.at[0])
+
+    def filler(place):
+        return pltpu.make_async_copy(b_ref.at[place % 3], whole.at[place], block_local.at[place])
+
+    for owner in owners_of(1):
 
         @pl.when(index == owner)
-        def _(owner=owner):
-            pltpu.make_async_copy(b_ref.at[owner], whole.at[owner], block_local.at[0]).start()
-
-    @pl.when(index >= blocks)
+        def _():
+            stored().start()
+
+    @pl.when(idle)
     def _():
         for place in range(8):
-            pltpu.make_async_copy(b_ref.at[place % blocks], whole.at[place], block_local.at[place]).start()
-
-    mine[0] = s_ref[...].astype(bf16)
+            filler(place).start()
+
+    share = s0_ref.shape[0]
+    mine[0, :share, :] = s0_ref[...].astype(bf16)
+    mine[0, share:, :] = s1_ref[...].astype(bf16)
     first = remote(mine.at[0], came.at[0], send_sem, recv_sem, 0, {"tensor": beside})
     first.start()
     first.wait()
@@ -1426,25 +1599,19 @@
     second.wait()
     os_ref[index] = (mine[1].astype(f32) + came[1].astype(f32)).astype(bf16)
 
-    for owner in range(blocks):
+    blocks.arrive()
+    for owner in owners_of(1):
 
         @pl.when(index == owner)
-        def _(owner=owner):
-            pltpu.make_async_copy(b_ref.at[owner], whole.at[owner], block_local.at[0]).wait()
-
-    for sender in range(8):
-
-        @pl.when(jnp.logical_and(index < blocks, index != sender))
-        def _(sender=sender):
-            place = whole.at[sender]
-            remote(place, place, block_send, block_recv, sender, {"dp": sibling}).wait_recv()
-
-    @pl.when(index >= blocks)
+        def _():
+            stored().wait()
+
+    @pl.when(idle)
     def _():
         for place in range(8):
-            pltpu.make_async_copy(b_ref.at[place % blocks], whole.at[place], block_local.at[place]).wait()
-
-    half = s_ref.shape[0] // 2
+            filler(place).wait()
+
+    half = share
     near, far, everything = pl.ds(0, half), pl.ds(half, half), pl.ds(0, 2 * half)
 
     def send(owner, part, slot, where):
@@ -1458,7 +1625,9 @@
         copy.start()
         return copy
 
-    vsum[0] = v_ref[...]
+    width = v0_ref.shape[1]
+    vsum[0, :, :width] = v0_ref[...]
+    vsum[0, :, width:] = v1_ref[...]
     pending = small(vsum.at[0], vcame.at[0], 0, {"dp": sibling})
     copies = [
         send(index, near, 2, by_x),
@@ -1511,50 +1680,49 @@
         copies[at].wait_recv()
     for copy in copies:
         copy.wait_send()
-    for owner in range(blocks):
-
-        @pl.when(index != owner)
-        def _(owner=owner):
-            block_to(owner).wait_send()
-
-
-def finish_blocks(shard, vector, blocks):
-    rows, width = blocks.shape[1:]
+    blocks.finish()
+
+
+def finish_blocks(shards, vectors, slots, early):
+    rows, width = slots[0].shape[1:]
     if not kernels_fit():
         count = lax.axis_size("dp")
-        total = lax.psum(shard, "tensor").astype(bf16)
+        total = lax.psum(jnp.concatenate(shards, 0), "tensor").astype(bf16)
+        blocks = jnp.concatenate(slots, 0)
         padded = jnp.pad(blocks, ((0, count - blocks.shape[0]), (0, 0), (0, 0)))
         whole = lax.all_to_all(padded, "dp", split_axis=0, concat_axis=0, tiled=True)
         return (
             lax.all_gather(total, "dp", axis=0),
-            lax.all_gather(lax.psum(vector, "dp"), "tensor", axis=0),
+            lax.all_gather(lax.psum(jnp.concatenate(vectors, 1), "dp"), "tensor", axis=0),
             orthogonal(whole.reshape(D, width), bf16),
         )
     vmem = pl.BlockSpec(memory_space=pltpu.VMEM)
     anywhere = pl.BlockSpec(memory_space=pl.ANY)
+    shard = (LAYERS * shards[0].shape[0], shards[0].shape[1])
+    vector = (vectors[0].shape[0], LAYERS * vectors[0].shape[1])
     return pl.pallas_call(
         tail_kernel,
         out_shape=(
-            jax.ShapeDtypeStruct((8, *shard.shape), bf16),
-            jax.ShapeDtypeStruct((4, *vector.shape), f32),
+            jax.ShapeDtypeStruct((8, *shard), bf16),
+            jax.ShapeDtypeStruct((4, *vector), f32),
             jax.ShapeDtypeStruct((D, width), bf16),
         ),
-        in_specs=[vmem, vmem, anywhere],
+        in_specs=[vmem] * 4 + [anywhere] * 2,
         out_specs=(vmem, vmem, vmem),
         scratch_shapes=[
             pltpu.VMEM((8, rows, width), bf16),
             pltpu.VMEM((width, D), bf16),
             pltpu.VMEM((width, D), bf16),
             pltpu.VMEM((width, width), bf16),
-            pltpu.VMEM((2, *shard.shape), bf16),
-            pltpu.VMEM((2, *shard.shape), bf16),
-            pltpu.VMEM((3, *vector.shape), f32),
-            pltpu.VMEM((3, *vector.shape), f32),
+            pltpu.VMEM((2, *shard), bf16),
+            pltpu.VMEM((2, *shard), bf16),
+            pltpu.VMEM((3, *vector), f32),
+            pltpu.VMEM((3, *vector), f32),
             pltpu.SemaphoreType.DMA((12,)),
             pltpu.SemaphoreType.DMA((12,)),
             pltpu.SemaphoreType.DMA((5,)),
             pltpu.SemaphoreType.DMA((5,)),
-            pltpu.SemaphoreType.DMA((8,)),
+            pltpu.SemaphoreType.DMA((3,)),
             pltpu.SemaphoreType.DMA((8,)),
             pltpu.SemaphoreType.DMA((8,)),
         ],
@@ -1562,7 +1730,7 @@
             collective_id=4, has_side_effects=True, vmem_limit_bytes=56 * 2**20
         ),
         cost_estimate=pl.CostEstimate(flops=2 * 10**10, bytes_accessed=100 * 2**20, transcendentals=0),
-    )(shard, vector, blocks)
+    )(*shards, *vectors, slots[0], early)
 
 
 def advance(chains, flip):
@@ -1799,22 +1967,22 @@
         )
         in_new[layer], out_new[layer], slots[layer], shared_shards[layer], grad_resid, d_in_gain = results[:6]
         if layer > 0:
-            d_rows, rd = results[6:]
+            d_rows, rd, early = results[6:]
         small_grads[layer] = jnp.concatenate([grad_x, grad_s, grad_h, d_in_gain.reshape(8, D // 8)], 1)
 
     in_momentum_new = jnp.transpose(jnp.stack(in_new), (0, 2, 1, 3))
     out_momentum_new = jnp.stack(out_new)
-    block_count = 3 * LAYERS
     dp_count = lax.axis_size("dp")
-    shared_total, vectors, turned = finish_blocks(
-        jnp.concatenate(shared_shards, 0), jnp.concatenate(small_grads, 1), jnp.concatenate(slots, 0)
-    )
+    shared_total, vectors, turned = finish_blocks(shared_shards, small_grads, slots, early)
     turned = turned.reshape(dp_count, shard_rows, local_cols)
-    returned = lax.all_to_all(turned, "dp", split_axis=0, concat_axis=0, tiled=True)[:block_count]
+    returned = lax.all_to_all(turned, "dp", split_axis=0, concat_axis=0, tiled=True)
     scale = muon_rate * (D / local_cols) ** 0.5
-    updates = returned.astype(f32).reshape(LAYERS, 3, shard_rows, local_cols) * scale
-    in_weight_new = in_weight.astype(f32) - jnp.transpose(updates[:, :2], (0, 2, 1, 3))
-    out_weight_new = out_weight.astype(f32) - updates[:, 2]
+    in_weight_new, out_weight_new = [], []
+    for layer in range(LAYERS):
+        gate, x, out = (returned[owner].astype(f32) * scale for owner in owners_of(layer))
+        in_weight_new.append(in_weight[layer].astype(f32) - jnp.stack([gate, x], 1))
+        out_weight_new.append(out_weight[layer].astype(f32) - out)
+    in_weight_new, out_weight_new = jnp.stack(in_weight_new), jnp.stack(out_weight_new)
 
     share = SHARED_COLS // dp_count
     shared_total = shared_total.reshape(dp_count, LAYERS, share, D)

time: 699 us -> 706 us (1.010)
    unnamed x79 -> x86, local copies, waits for them, and re-layouts: 24.7 us -> 23.7 us
  transfers between devices with their start and end apart: 3 -> 3, of which waited for: 0 -> 0; matrix products, arithmetic and copies ran while one was open for 2% -> 3% of each run, Pallas kernels for 20% -> 20%
where the time goes in v3:
time: 706 us; the launch traced here: 697 us
  Pallas kernels  610 us (86%)
  local copies, waits for them, and re-layouts  48.8 us (7%)
  other arithmetic  17.5 us (2%)
  between operations  15.1 us (2%)
    pallas_call x2, Pallas kernels, exchange(): pl.pallas_call(functools.partial(exchange_kernel, gathers=below is not No...  168 us
    pallas_call x1, Pallas kernels, forward_pass(): pl.pallas_call(forward_pass_kernel, out_shape=(jax.ShapeDtypeStruct((coun...  97 us
    pallas_call x2, Pallas kernels, mixer_backward(): pl.pallas_call(backward_kernel, grid=(spans + 1,), in_specs=[pl.BlockSpec...  82.8 us
    pallas_call x1, Pallas kernels, last_scatter(): pl.pallas_call(scatter_kernel, out_shape=(jax.ShapeDtypeStruct((count, co...  73.7 us
    pallas_call x1, Pallas kernels, gather_first(): pl.pallas_call(first_kernel, out_shape=(larger(rows, 4), larger(w_rows, 8...  61.7 us
    pallas_call x1, Pallas kernels, finish_blocks(): pl.pallas_call(tail_kernel, out_shape=(jax.ShapeDtypeStruct((8, *shard),...  56.1 us
    pallas_call x2, Pallas kernels, mixer_forward(): pl.pallas_call(forward_kernel, grid=(spans + 1,), in_specs=[pl.BlockSpec(...  52.3 us
    unnamed x86, local copies, waits for them, and re-layouts  23.7 us
  transfers between devices with their start and end apart: 3, of which 0 were waited for; matrix products, arithmetic and copies ran while one was open for 3% of the time, Pallas kernels for 20%

profile of v3, /device:TPU:0, one launch (start us, length us, event | category | flops | bytes accessed | tf_op | source)
XLA Modules:
  0.0 697.1 jit_solution(15830793893129541125)
XLA Ops:
  9.7 1.7 fusion.10
  12.0 2.8 fusion.12
  19.0 61.7 %shard_map.194 = (bf16[1024,1536]{1,0:T(8,128)(2,1)}, bf16[1536,1920]{1,0:T(8,128)(2,1)}, bf16[1536,768]{1,0:T(8,128)(2,1)}) custom-call(bf16[256,1536]{1,0:T(8,128)(2,1)} %multiply_convert_fusion.x_ref, bf16[192,1920]{1,0:T(8,128)(2,1)} %fusion.2.w_ref, bf16[192,768]{1,0:T(8,128)(2,1)} %get-tuple-element.163.v_ref), custom_call_target="tpu_custom_call" | custom-call | bytes 157286400 | tf_op jit(solution)/shard_map/pallas_call | solution.py:750
  85.1 26.3 %shard_map.195 = (f32[1024,1920]{1,0:T(8,128)}, f32[1024,768]{1,0:T(8,128)}, bf16[1024,1536]{1,0:T(8,128)(2,1)}, f32[4,8,256]{2,1,0:T(8,128)}, bf16[4,128,768]{2,1,0:T(8,128)(2,1)}) custom-call(bf16[1024,1536]{1,0:T(8,128)(2,1)} %get-tuple-element.64.g_ref.x_any, bf16[1536,1920]{1,0:T(8,128)(2,1)} %get-tuple-element.65.w_ref, ...), custom_call_target="tpu_custom_call" | custom-call | flops 10000000000 | bytes 33554432 | tf_op jit(solution)/shard_map/pallas_call | solution.py:449
  113.3 1.6 copy-done.1
  114.9 97.0 %shard_map.196 = (f32[256,1536]{1,0:T(8,128)S(1)}, f32[256,1536]{1,0:T(8,128)S(1)}, f32[8,256]{1,0:T(8,128)S(1)}, bf16[1024,1536]{1,0:T(8,128)(2,1)S(1)}) custom-call(bf16[1024,1536]{1,0:T(8,128)(2,1)S(1)} %copy-done.1, f32[4,8,256]{2,1,0:T(8,128)S(1)} %broadcast_in_dim.42.q_ref, f32[256,1536]{1,0:T(8,128)S(1)} %copy-done, ...), custom_call_target="tpu_custom_call" | custom-call | bytes 262144000 | tf_op jit(solution)/shard_map/pallas_call | solution.py:979
  213.7 1.8 fusion.11
  218.4 26.0 %shard_map.197 = (f32[1024,1920]{1,0:T(8,128)}, f32[1024,768]{1,0:T(8,128)}, bf16[1024,1536]{1,0:T(8,128)(2,1)}, f32[4,8,256]{2,1,0:T(8,128)}, bf16[4,128,768]{2,1,0:T(8,128)(2,1)}) custom-call(bf16[1024,1536]{1,0:T(8,128)(2,1)} %copy-done.6, bf16[1536,1920]{1,0:T(8,128)(2,1)} %all-gather.3.cloned.1.call-done.w_ref, ...), custom_call_target="tpu_custom_call" | custom-call | flops 10000000000 | bytes 33554432 | tf_op jit(solution)/shard_map/pallas_call | solution.py:449
  245.2 1.9 copy-done.2
  247.1 73.7 %shard_map.198 = (f32[256,1536]{1,0:T(8,128)S(1)}, bf16[1024,1536]{1,0:T(8,128)(2,1)S(1)}, f32[4,8,256]{2,1,0:T(8,128)S(1)}) custom-call(bf16[1024,1536]{1,0:T(8,128)(2,1)S(1)} %copy-done.2, f32[4,8,256]{2,1,0:T(8,128)S(1)} %broadcast_in_dim.46.q_ref, bf16[256,1536]{1,0:T(8,128)(2,1)S(1)} %convert_element_type.89.x_ref, f32[256,1536]{1,0:T(8,128)S(1)} %copy-done.4), custom_call_target="tpu_custom_call" | custom-call | bytes 157286400 | tf_op jit(solution)/shard_map/pallas_call | solution.py:1091
  320.8 1.7 copy-done.7
  323.6 41.3 %shard_map.199 = (bf16[1024,1920]{1,0:T(8,128)(2,1)}, bf16[1024,768]{1,0:T(8,128)(2,1)}, bf16[1024,1536]{1,0:T(8,128)(2,1)}, f32[8,768]{1,0:T(8,128)}, f32[8,256]{1,0:T(8,128)}, /*index=5*/f32[8,128]{1,0:T(8,128)}) custom-call(bf16[1024,1536]{1,0:T(8,128)(2,1)} %copy-done.7, bf16[1536,1920]{1,0:T(8,128)(2,1)} %all-gather.3.cloned.1.call-done.w_ref, ...), custom_call_target="tpu_custom_call" | custom-call | flops 16000000000 | bytes 50331648 | tf_op jit(solution)/shard_map/pallas_call | solution.py:494
  364.9 106.6 %shard_map.200 = (f32[2,192,768]{2,1,0:T(8,128)}, f32[192,768]{1,0:T(8,128)}, bf16[3,192,768]{2,1,0:T(8,128)(2,1)}, f32[48,1536]{1,0:T(8,128)}, f32[256,1536]{1,...) custom-call(bf16[1024,1536]{1,0:T(8,128)(2,1)} %get-tuple-element.81, ...), custom_call_target="tpu_custom_call" | custom-call | flops 10000000000 | bytes 157286400 | tf_op jit(solution)/shard_map/pallas_call | solution.py:1502
  473.3 41.5 %shard_map.201 = (bf16[1024,1920]{1,0:T(8,128)(2,1)}, bf16[1024,768]{1,0:T(8,128)(2,1)}, bf16[1024,1536]{1,0:T(8,128)(2,1)}, f32[8,768]{1,0:T(8,128)}, f32[8,256]{1,0:T(8,128)}, /*index=5*/f32[8,128]{1,0:T(8,128)}) custom-call(bf16[1024,1536]{1,0:T(8,128)(2,1)} %get-tuple-element.86.dr_ref.dr_any, bf16[1536,1920]{1,0:T(8,128)(2,1)} %get-tuple-element.65.w_ref, ...), custom_call_target="tpu_custom_call" | custom-call | flops 16000000000 | bytes 50331648 | tf_op jit(solution)/shard_map/pallas_call | solution.py:494
  515.5 61.1 %shard_map.202 = (f32[2,192,768]{2,1,0:T(8,128)}, f32[192,768]{1,0:T(8,128)}, bf16[3,192,768]{2,1,0:T(8,128)(2,1)}, f32[48,1536]{1,0:T(8,128)}, f32[256,1536]{1,0:T(8,128)}, /*index=5*/f32[8,1536]{1,0:T(8,128)}) custom-call(bf16[1024,1536]{1,0:T(8,128)(2,1)} %get-tuple-element.91.p_any, bf16[1024,1536]{1,0:T(8,128)(2,1)} %get-tuple-element.64.g_ref.x_any, ...), custom_call_target="tpu_custom_call" | custom-call | flops 10000000000 | bytes 157286400 | tf_op jit(solution)/shard_map/pallas_call | solution.py:1502
  579.6 56.1 %shard_map.203 = (bf16[8,96,1536]{2,1,0:T(8,128)(2,1)}, f32[4,8,2688]{2,1,0:T(8,128)}, bf16[1536,768]{1,0:T(8,128)(2,1)}) custom-call(f32[48,1536]{1,0:T(8,128)} %get-tuple-element.96.s0_ref, f32[48,1536]{1,0:T(8,128)} %get-tuple-element.97.s1_ref, f32[8,1344]{1,0:T(8,128)} %pad_maximum_fusion.4.v0_ref, f32[8,1344]{1,0:T(8,128)} %pad_maximum_fusion.5.v1_ref, ...), custom_call_target="tpu_custom_call" | custom-call | flops 20000000000 | bytes 104857600 | tf_op jit(solution)/shard_map/pallas_call | solution.py:1703
  640.8 4.8 all-to-all-start
  649.3 3.2 copy.59
  652.7 1.9 copy-done.12
  654.6 2.5 bitcast_add_fusion.m_ref
  657.1 18.8 %shard_map.204 = f32[2,304,1536]{2,1,0:T(8,128)} custom-call(f32[2,304,1536]{2,1,0:T(8,128)} %bitcast_add_fusion.m_ref, bf16[2,304,1536]{2,1,0:T(8,128)(2,1)} %bitcast.95), custom_call_target="tpu_custom_call" | custom-call | flops 10192158720 | bytes 7077888 | tf_op jit(solution)/shard_map/pallas_call | solution.py:1833
  677.1 1.8 multiply_subtract_fusion.1
  680.3 3.2 copy.60
  687.9 1.9 copy.86
  (176 shorter events, 41.1 us)
Async XLA Ops:
  7.2 211.3 %all-gather.5.cloned.1.call-start = ((), (), s32[]{:S(2)}) async-start(), calls=%async_computation.2 | async-start | bytes 2654208 | tf_op jit(solution)/shard_map/all_gather | solution.py:1928
  12.0 2.8 copy-start.18
  81.8 136.7 %all-gather.3.cloned.1.call-start = ((), (), s32[]{:S(2)}) async-start(), calls=%async_computation.1 | async-start | bytes 6635520 | tf_op jit(solution)/shard_map/all_gather | solution.py:1927
  85.1 27.2 %copy-start.24 = (f32[256,1536]{1,0:T(8,128)S(1)}, f32[256,1536]{1,0:T(8,128)}, u32[]{:S(2)}) copy-start(f32[256,1536]{1,0:T(8,128)} %r_ref.3) | copy-start | bytes 4718596
  114.9 97.0 %copy-start.5 = (f32[8,1536]{1,0:T(8,128)}, f32[8,1536]{1,0:T(8,128)S(1)}, u32[]{:S(2)}) copy-start(f32[8,1536]{1,0:T(8,128)S(1)} %broadcast_in_dim.44.gain_ref) | copy-start | bytes 147460
  114.9 98.7 %copy-start.11 = (bf16[2,192,2,768]{3,2,1,0:T(2,128)(2,1)S(1)}, bf16[2,192,2,768]{3,2,1,0:T(2,128)(2,1)}, u32[]{:S(2)}) copy-start(bf16[2,192,2,768]{3,2,1,0:T(2,128)(2,1)} %param.12) | copy-start | bytes 3538948
  213.7 3.2 copy-start.3
  213.7 3.2 copy-start.6
  218.4 26.8 %copy-start.4 = (f32[256,1536]{1,0:T(8,128)S(1)}, f32[256,1536]{1,0:T(8,128)}, u32[]{:S(2)}) copy-start(f32[256,1536]{1,0:T(8,128)} %copy-done.3) | copy-start | bytes 4718596
  515.4 62.9 %copy-start.34 = (f32[8,768]{1,0:T(8,128)S(1)}, f32[8,768]{1,0:T(8,128)}, u32[]{:S(2)}) copy-start(f32[8,768]{1,0:T(8,128)} %get-tuple-element.98) | copy-start | bytes 73732
  515.4 62.9 %copy-start.36 = (f32[8,256]{1,0:T(8,128)S(1)}, f32[8,256]{1,0:T(8,128)}, u32[]{:S(2)}) copy-start(f32[8,256]{1,0:T(8,128)} %get-tuple-element.99) | copy-start | bytes 24580
  515.4 62.9 %copy-start.38 = (f32[8,128]{1,0:T(8,128)S(1)}, f32[8,128]{1,0:T(8,128)}, u32[]{:S(2)}) copy-start(f32[8,128]{1,0:T(8,128)} %get-tuple-element.100) | copy-start | bytes 12292
  515.4 63.5 %copy-start.33 = (f32[8,768]{1,0:T(8,128)S(1)}, f32[8,768]{1,0:T(8,128)}, u32[]{:S(2)}) copy-start(f32[8,768]{1,0:T(8,128)} %get-tuple-element.102) | copy-start | bytes 73732
  515.4 63.5 %copy-start.35 = (f32[8,256]{1,0:T(8,128)S(1)}, f32[8,256]{1,0:T(8,128)}, u32[]{:S(2)}) copy-start(f32[8,256]{1,0:T(8,128)} %get-tuple-element.103) | copy-start | bytes 24580
  515.4 63.5 %copy-start.37 = (f32[8,128]{1,0:T(8,128)S(1)}, f32[8,128]{1,0:T(8,128)}, u32[]{:S(2)}) copy-start(f32[8,128]{1,0:T(8,128)} %get-tuple-element.104) | copy-start | bytes 12292
  640.8 5.7 copy-start.28
  640.8 5.7 copy-start.31
  640.8 5.7 copy-start.32
  640.8 36.2 %all-to-all-start = ((bf16[8,192,768]{2,1,0:T(8,128)(2,1)}), bf16[8,192,768]{2,1,0:T(8,128)(2,1)}, u32[]{:S(2)}, u32[]{:S(2)}) async-start(bf16[8,192,768]{2,1,0:T(8,128)(2,1)} %bitcast.93), calls=%async_computation | async-start | bytes 4718592 | tf_op jit(solution)/shard_map/all_to_all | solution.py:1978
  645.6 2.3 copy-start.27
  649.3 3.2 copy-start.21
  657.1 18.8 %copy-start.29 = (f32[192,768]{1,0:T(8,128)S(1)}, f32[192,768]{1,0:T(8,128)}, u32[]{:S(2)}) copy-start(f32[192,768]{1,0:T(8,128)} %get-tuple-element.113) | copy-start | bytes 1769476
  657.1 18.9 %copy-start.30 = (f32[192,768]{1,0:T(8,128)S(1)}, f32[192,768]{1,0:T(8,128)}, u32[]{:S(2)}) copy-start(f32[192,768]{1,0:T(8,128)} %get-tuple-element.112) | copy-start | bytes 1769476
  684.6 3.3 copy-start.13
  (21 other events, 35.8 us)
Sparse Core Ops, SparseCore 0:
  81.9 27.2 all-gather.4
  111.6 43.8 all-gather.2
